TPU v7x, 32 devices: a whole 2x2x4 slice. The times are simulated.
32 devices in a mesh: role: 2 (over core), group: 4 (over z), tp: 4 (over y, x).
Axes of the slice: x: 2, y: 2, z: 4, core: 2. Of those that a mesh axis runs over, the one named last changes fastest.
Arguments:
- kv_pages: bfloat16 [2, 4, 4, 64, 128, 512], P('role', 'group', 'tp'), may hold values from -24 to 24, as said below
- send_list: int32 [4, 12, 3], replicated, may hold values from 0 to 63, as said below
- wanted: int32 [4, 6], replicated, may hold values from 0 to 31, as said below
- lengths: int32 [4, 8], P('group'), may hold values from 1 to 1024, as said below
- tables: int32 [4, 8, 8], P('group'), may hold values from 0 to 69, as said below
- queries: bfloat16 [4, 8, 8192], P('group', None, 'tp'), may hold values from -160 to 160
- new_kv: bfloat16 [4, 8, 2048], P('group', None, 'tp'), may hold values from -24 to 24, as said below
- out_weight: bfloat16 [8192, 8192], P('tp', 'role'), may hold values from -3 to 3
Outputs:
- mixed: bfloat16 [4, 8, 8192], P('group', None, ('role', 'tp'))
Inputs may be any that keep to these rules, and one draw needn't show every extreme that they name: `send_list`: column 0 holds 12 distinct store pages of a prefill group, from 8 on; column 1 the destination decode group; column 2 the destination slot. The pairs (destination group, slot) are distinct over all groups. At most 4 pages go from one prefill group to one decode group, and one decode group receives exactly 4 from every prefill group. `wanted`: row g lists 6 distinct pages; page o * 8 + p is store slot p of prefill group o. Each row names pages of exactly 3 owner groups, 2 of each. `lengths`: in every group some row has exactly 1024 tokens. `tables`: entry j of a row serves its tokens j * 128 to (j + 1) * 128 - 1 below its length. An entry below 64 names a slot of the decode device's cache; an entry s from 64 on names the (s - 64)-th wanted page of the group. The entries a row reads are distinct, no cache slot is read by two rows of a group, and entries past a row's last page are 0. `new_kv`: indices of tp that hold the same key-value head hold equal new keys and values. `kv_pages`: indices of tp that hold the same key-value head hold equal pages.
All inputs are finite; a program needn't handle non-finite values.
Results may differ from a plain program's by a relative error of at most 0.006.
Values may be sent and summed in bfloat16 or wider, within the bound.
No kernel may reach another device: no remote copies, remote signals or barrier semaphores. Data moves between devices by JAX's collectives and lax.ppermute only.
A program may use at most 128 MiB of HBM per device.

v0:
```python
import math

import jax
import jax.numpy as jnp
from jax import lax
from jax.sharding import PartitionSpec as P

KVH = 8
HD = 128
CAP = 4
PRE_DEV = 8


def from_behind(value, axis, by):
    size = lax.axis_size(axis)
    pairs = [(i, i + by) for i in range(size) if 0 <= i + by < size]
    return lax.ppermute(value, axis, pairs)


def per_device(kv_pages, send_list, wanted, lengths, tables, queries, new_kv, out_weight):
    stored = kv_pages[0, 0, 0]
    slot_count = stored.shape[0]
    page_shape = stored.shape[1:]
    groups = lax.axis_size("group")
    my_group = lax.axis_index("group")
    is_prefill = lax.axis_index("role") == 0
    held_count = max(1, KVH // lax.axis_size("tp"))
    store_pages = send_list[:, :, 0]
    target_group = send_list[:, :, 1]
    target_slot = send_list[:, :, 2]
    matches = (target_group[:, :, None] == jnp.arange(groups)[None, None, :]).astype(jnp.int32)
    order_rank = jnp.sum((jnp.cumsum(matches, 1) - matches) * matches, 2)
    source = jnp.arange(groups)[:, None]
    landing = jnp.where(target_group == my_group, source * CAP + order_rank, groups * CAP)
    slot_map = (
        jnp.full((groups * CAP,), slot_count, jnp.int32)
        .at[landing.reshape(-1)]
        .set(target_slot.reshape(-1), mode="drop")
    )
    slot_map = jnp.where(is_prefill, slot_count, slot_map)
    outgoing = stored[lax.dynamic_index_in_dim(store_pages, my_group, 0, False)]
    my_target = lax.dynamic_index_in_dim(target_group, my_group, 0, False)
    my_rank = lax.dynamic_index_in_dim(order_rank, my_group, 0, False)
    own_prefix = stored[:PRE_DEV]
    wanted_row = lax.dynamic_index_in_dim(wanted, my_group, 0, False)
    block_width = CAP
    blocks = 2 * groups
    position = jnp.where(
        is_prefill, (groups + my_target) * block_width + my_rank, blocks * block_width
    )
    parcel = (
        jnp.zeros((blocks * block_width,) + page_shape, stored.dtype)
        .at[position]
        .set(outgoing, mode="drop")
    )
    received = lax.all_to_all(parcel, ("role", "group"), split_axis=0, concat_axis=0, tiled=True)[
        : groups * block_width
    ]
    received = received.reshape((groups, block_width) + page_shape)
    arrived = received.reshape((groups * CAP,) + page_shape)
    cache_pages = stored.at[slot_map].set(arrived, mode="drop")
    every_page = lax.all_gather(own_prefix, ("role", "group"), axis=0, tiled=True)
    shared = every_page[wanted_row]
    page_pool = jnp.concatenate([cache_pages, shared], 0)
    row_count = queries.shape[1]
    gathered = page_pool[tables[0]].reshape(row_count, -1, held_count, 2 * HD)
    cache_keys = gathered[..., :HD]
    cache_values = gathered[..., HD:]
    query_heads = queries[0].reshape(row_count, held_count, -1, HD)
    fresh_kv = new_kv[0].reshape(row_count, held_count, 2, HD)
    scale = 1.0 / math.sqrt(HD)
    scores = (
        jnp.einsum("rjhd,rkjd->rjhk", query_heads, cache_keys, preferred_element_type=jnp.float32)
        * scale
    )
    own_score = (
        jnp.einsum(
            "rjhd,rjd->rjh", query_heads, fresh_kv[:, :, 0], preferred_element_type=jnp.float32
        )
        * scale
    )
    is_valid = (jnp.arange(gathered.shape[1])[None, :] < lengths[0][:, None])[:, None, None, :]
    row_top = jnp.maximum(jnp.max(jnp.where(is_valid, scores, -jnp.inf), -1), own_score)
    lifted = jnp.where(is_valid, jnp.exp(scores - row_top[..., None]), 0.0)
    own_lift = jnp.exp(own_score - row_top)
    row_total = jnp.sum(lifted, -1) + own_lift
    weights = (lifted / row_total[..., None]).astype(jnp.bfloat16)
    own_weight = (own_lift / row_total).astype(jnp.bfloat16)
    attended = jnp.einsum(
        "rjhk,rkjd->rjhd", weights, cache_values, preferred_element_type=jnp.float32
    )
    attended = attended + own_weight.astype(jnp.float32)[..., None] * fresh_kv[
        :, :, None, 1
    ].astype(jnp.float32)
    attended = attended.astype(jnp.bfloat16).reshape(row_count, -1)
    partner = from_behind(attended, "role", -1)
    heads_here = jnp.where(is_prefill, partner, attended)
    partial_value = jnp.dot(heads_here, out_weight, preferred_element_type=jnp.float32)
    column_share = lax.psum_scatter(partial_value, "tp", scatter_dimension=1, tiled=True)
    return column_share.astype(jnp.bfloat16)[None]


def solution(mesh):
    return jax.shard_map(
        per_device,
        mesh=mesh,
        in_specs=(
            P("role", "group", "tp", None, None, None),
            P(),
            P(),
            P("group", None),
            P("group", None, None),
            P("group", None, "tp"),
            P("group", None, "tp"),
            P("tp", "role"),
        ),
        out_specs=P("group", None, ("role", "tp")),
        check_vma=False,
    )
```

profile of v0, /device:TPU:0, one launch (start us, length us, event | category | flops | bytes accessed | tf_op | source)
XLA Modules:
  0.0 275.7 jit_solution(10625733502875957740)
XLA Ops:
  6.5 7.6 %copy.70 = bf16[1,1,1,64,128,512]{5,4,3,2,1,0:T(8,128)(2,1)} copy(bf16[1,1,1,64,128,512]{5,4,3,2,1,0:T(8,128)(2,1)} %param.8) | data formatting | bytes 16777216
  14.2 2.3 slice.47
  16.5 0.7 reduce_window_sum.11
  17.3 4.0 %gather_fusion = bf16[12,128,512]{2,1,0:T(8,128)(2,1)S(1)} fusion(bf16[64,128,512]{2,1,0:T(8,128)(2,1)} %bitcast.77, s32[1024]{0:T(1024)S(1)} %pad_clamp_fusion.2), kind=kCustom, calls=%fused_computation | custom fusion | bytes 3145776 | tf_op jit(solution)/shard_map/gather | solution.py:41
  21.3 2.5 broadcast_in_dim.55
  23.8 5.2 %scatter_fusion = bf16[32,128,512]{2,1,0:T(8,128)(2,1)} fusion(bf16[32,128,512]{2,1,0:T(8,128)(2,1)} %broadcast_in_dim.55, s32[12]{0:T(128)S(1)} %get-tuple-element.18, bf16[12,128,512]{2,1,0:T(8,128)(2,1)S(1)} %gather_fusion), kind=kCustom, calls=%fused_computation.4 | custom fusion | bytes 4718640 | tf_op jit(solution)/shard_map/scatter | solution.py:54
  29.0 6.8 %all-to-all-start = ((bf16[32,128,512]{2,1,0:T(8,128)(2,1)}), bf16[32,128,512]{2,1,0:T(8,128)(2,1)}, u32[]{:S(2)}, u32[]{:S(2)}) async-start(bf16[32,128,512]{2,1,0:T(8,128)(2,1)} %scatter_fusion), calls=%async_computation | async-start | bytes 8388608 | tf_op jit(solution)/shard_map/all_to_all | solution.py:56
  36.3 0.7 scatter_custom_fusion
  37.0 0.7 fusion.40
  38.0 151.2 %all-to-all-done = bf16[32,128,512]{2,1,0:T(8,128)(2,1)} async-done(((bf16[32,128,512]{2,1,0:T(8,128)(2,1)}), bf16[32,128,512]{2,1,0:T(8,128)(2,1)}, u32[]{:S(2)}, u32[]{:S(2)}) %all-to-all-start) | async-done | bytes 4194336 | tf_op jit(solution)/shard_map/all_to_all | solution.py:56
  189.3 1.8 slice.46
  191.1 4.4 %scatter_fusion.1 = bf16[64,128,512]{2,1,0:T(8,128)(2,1)} fusion(bf16[64,128,512]{2,1,0:T(8,128)(2,1)} %bitcast.78, s32[16]{0:T(128)S(1)} %compare_select_fusion.4, bf16[16,128,512]{2,1,0:T(8,128)(2,1)S(1)} %slice.46), kind=kCustom, calls=%fused_computation.5 | custom fusion | bytes 6291520 | tf_op jit(solution)/shard_map/scatter | solution.py:61
  195.5 4.0 %gather_fusion.1 = bf16[6,128,512]{2,1,0:T(8,128)(2,1)S(1)} fusion(bf16[64,128,512]{2,1,0:T(8,128)(2,1)} %bitcast.81, s32[1024]{0:T(1024)S(1)} %pad_clamp_fusion.1), kind=kCustom, calls=%fused_computation.1 | custom fusion | bytes 1572888 | tf_op jit(solution)/shard_map/gather | solution.py:63
  199.5 7.4 %pad_maximum_fusion = bf16[70,128,512]{2,1,0:T(8,128)(2,1)} fusion(bf16[6,128,512]{2,1,0:T(8,128)(2,1)S(1)} %gather_fusion.1, bf16[64,128,512]{2,1,0:T(8,128)(2,1)} %scatter_fusion.1), kind=kLoop, calls=%fused_computation.6 | loop fusion | flops 4587520 | bytes 18350080 | tf_op jit(solution)/shard_map/concatenate | solution.py:64
  206.8 9.1 %gather_fusion.2 = bf16[64,128,512]{2,1,0:T(8,128)(2,1)} fusion(bf16[70,128,512]{2,1,0:T(8,128)(2,1)} %pad_maximum_fusion, s32[1024]{0:T(1024)S(1)} %pad_clamp_fusion), kind=kCustom, calls=%fused_computation.2 | custom fusion | bytes 16777472 | tf_op jit(solution)/shard_map/gather | solution.py:66
  215.9 12.5 %reshape.265 = bf16[8,1024,2,256]{3,2,1,0:T(2,128)(2,1)} reshape(bf16[64,128,512]{2,1,0:T(8,128)(2,1)} %gather_fusion.2) | data formatting | bytes 16777216 | tf_op jit(solution)/shard_map/reshape | solution.py:66
  228.5 8.3 %fusion.46 = (bf16[8,1024,2,128]{3,2,1,0:T(2,128)(2,1)S(1)}, bf16[8,1024,2,128]{3,2,1,0:T(2,128)(2,1)S(1)}) fusion(bf16[8,1024,2,256]{3,2,1,0:T(2,128)(2,1)} %reshape.265), kind=kLoop, calls=%fused_computation.77 | loop fusion | bytes 16777216 | tf_op jit(solution)/shard_map/slice | solution.py:67
  236.8 1.3 select_reduce_fusion
  238.4 0.9 fusion.13
  239.3 1.3 collective-permute-start
  240.6 1.8 collective-permute-done
  242.4 2.9 %fusion.22 = f32[8,4096]{1,0:T(8,128)} fusion(bf16[2048,4096]{1,0:T(8,128)(2,1)S(1)} %bitcast.80, bf16[8,2048]{1,0:T(8,128)(2,1)S(1)} %collective-permute-done, pred[]{:T(512)S(6)} %eq.35, bf16[1,8,16,128]{3,2,1,0:T(8,128)(2,1)S(1)} %fusion.13), kind=kOutput, calls=%fused_computation.25 | convolution fusion | flops 134234112 | bytes 16973824 | tf_op jit(solution)/shard_map/dot_general | solution.py:98
  245.4 22.1 %reduce-scatter.2.cloned.1.call-done = f32[8,1024]{1,0:T(8,128)} async-done(((f32[8,4096]{1,0:T(8,128)}), f32[8,1024]{1,0:T(8,128)}) %reduce-scatter.2.cloned.1.call-update) | async-done | bytes 32784 | tf_op jit(solution)/shard_map/reduce_scatter | solution.py:99
  267.5 1.4 convert_bitcast_fusion
  (49 shorter events, 1.2 us)
Async XLA Ops:
  6.5 9.9 %copy-start = (s32[4,12,3]{1,0,2:T(4,128)S(1)}, s32[4,12,3]{1,0,2:T(4,128)}, u32[]{:S(2)}) copy-start(s32[4,12,3]{1,0,2:T(4,128)} %param.9) | copy-start | bytes 1732
  6.5 188.9 %all-gather.3.cloned.1.call-start = ((), (), s32[]{:S(2)}) async-start(), calls=%async_computation.3 | async-start | bytes 9437184 | tf_op jit(solution)/shard_map/all_gather | solution.py:62
  29.0 7.2 %copy-start.2 = (s32[1,8,8]{2,1,0:T(8,128)S(1)}, s32[1,8,8]{2,1,0:T(8,128)}, u32[]{:S(2)}) copy-start(s32[1,8,8]{2,1,0:T(8,128)} %param.12) | copy-start | bytes 772
  29.0 8.8 %copy-start.3 = (s32[1,8]{1,0:T(1,128)S(1)}, s32[1,8]{1,0:T(1,128)}, u32[]{:S(2)}) copy-start(s32[1,8]{1,0:T(1,128)} %param.11) | copy-start | bytes 100
  29.0 8.9 %copy-start.1 = (bf16[1,8,512]{2,1,0:T(8,128)(2,1)S(1)}, bf16[1,8,512]{2,1,0:T(8,128)(2,1)}, u32[]{:S(2)}) copy-start(bf16[1,8,512]{2,1,0:T(8,128)(2,1)} %param.14) | copy-start | bytes 24580
  29.0 8.9 %copy-start.4 = (bf16[1,8,2048]{2,1,0:T(8,128)(2,1)S(1)}, bf16[1,8,2048]{2,1,0:T(8,128)(2,1)}, u32[]{:S(2)}) copy-start(bf16[1,8,2048]{2,1,0:T(8,128)(2,1)} %param.13) | copy-start | bytes 98308
  29.0 160.3 %all-to-all-start = ((bf16[32,128,512]{2,1,0:T(8,128)(2,1)}), bf16[32,128,512]{2,1,0:T(8,128)(2,1)}, u32[]{:S(2)}, u32[]{:S(2)}) async-start(bf16[32,128,512]{2,1,0:T(8,128)(2,1)} %scatter_fusion), calls=%async_computation | async-start | bytes 8388608 | tf_op jit(solution)/shard_map/all_to_all | solution.py:56
  35.8 231.7 %reduce-scatter.2.cloned.1.call-start = ((), (), s32[]{:S(2)}) async-start(), calls=%async_computation.2 | async-start | bytes 163840 | tf_op jit(solution)/shard_map/reduce_scatter | solution.py:99
  228.5 13.9 %slice-start = ((s8[16777216]{0:T(1024)(128)(4,1)}), s8[4194304]{0:T(1024)(128)(4,1)S(1)}, s32[]{:S(2)}) async-start(s8[16777216]{0:T(1024)(128)(4,1)} %bitcast.79), calls=%async_computation.4 | async-start | bytes 8388608
  228.5 13.9 %slice-start.1 = ((s8[16777216]{0:T(1024)(128)(4,1)}), s8[4194304]{0:T(1024)(128)(4,1)S(1)}, s32[]{:S(2)}) async-start(s8[16777216]{0:T(1024)(128)(4,1)} %bitcast.79), calls=%async_computation.5 | async-start | bytes 8388608
  228.5 13.9 %slice-start.2 = ((s8[16777216]{0:T(1024)(128)(4,1)}), s8[4194304]{0:T(1024)(128)(4,1)S(1)}, s32[]{:S(2)}) async-start(s8[16777216]{0:T(1024)(128)(4,1)} %bitcast.79), calls=%async_computation.6 | async-start | bytes 8388608
  236.8 5.6 %slice-start.3 = ((s8[16777216]{0:T(1024)(128)(4,1)}), s8[4194304]{0:T(1024)(128)(4,1)S(1)}, s32[]{:S(2)}) async-start(s8[16777216]{0:T(1024)(128)(4,1)} %bitcast.79), calls=%async_computation.7 | async-start | bytes 8388608
  239.3 3.1 %collective-permute-start = (bf16[8,2048]{1,0:T(8,128)(2,1)S(1)}, bf16[8,2048]{1,0:T(8,128)(2,1)S(1)}, u32[]{:S(2)}, u32[]{:S(2)}) collective-permute-start(bf16[8,2048]{1,0:T(8,128)(2,1)S(1)} %bitcast.84), channel_id=1, source_target_pairs={{16,0},{17,1},{18,2},{19,3},{20,4},{21,5},{22,6},{23,7},{24,8},{25... | collective-permute-start | bytes 98312 | tf_op jit(solution)/shard_map/ppermute | solution.py:17
Sparse Core Ops, SparseCore 0:
  16.6 159.9 all-gather.2
  245.5 21.9 reduce-scatter.1
where the time goes:
time: 277 us; the launch traced here: 276 us
  waiting for transfers between devices  175 us (63%)
  local copies, waits for them, and re-layouts  62.8 us (23%)
  between operations  13.6 us (5%)
  other arithmetic  10.7 us (4%)
  starting transfers between devices  8.15 us (3%)
  matrix products  5.25 us (2%)
    all_to_all x1, waiting for transfers between devices, per_device(): lax.all_to_all(parcel, ('role', 'group'), split_axis=0, concat_axis=0, ti...  151 us
    reduce_scatter x1, waiting for transfers between devices, per_device(): lax.psum_scatter(partial_value, 'tp', scatter_dimension=1, tiled=True)  22.1 us
    reshape x1, local copies, waits for them, and re-layouts, per_device(): gathered = page_pool[tables[0]].reshape(row_count, -1, held_count, 2 * HD)  12.5 us
    gather x1, local copies, waits for them, and re-layouts, per_device(): gathered = page_pool[tables[0]].reshape(row_count, -1, held_count, 2 * HD)  9.1 us
    slice x1, local copies, waits for them, and re-layouts, per_device(): cache_keys = gathered[..., :HD]  8.3 us
    unnamed x20, local copies, waits for them, and re-layouts  7.68 us
    concatenate x1, other arithmetic, per_device(): page_pool = jnp.concatenate([cache_pages, shared], 0)  7.35 us
    all_to_all x1, starting transfers between devices, per_device(): lax.all_to_all(parcel, ('role', 'group'), split_axis=0, concat_axis=0, ti...  6.82 us
  transfers between devices with their start and end apart: 4, of which 3 were waited for; matrix products, arithmetic and copies ran while one was open for 8% of the time, Pallas kernels for 0%

commit v1 on v0

v1 whole, which is shorter than its diff:
```python
import functools
import math

import jax
import jax.numpy as jnp
from jax import lax
from jax.experimental import pallas as pl
from jax.experimental.pallas import tpu as pltpu
from jax.sharding import PartitionSpec as P

KVH = 8
HD = 128
CAP = 4
CAPP = 2
PRE_DEV = 8
LANES = 128
NEG = -1e30
SCALE = 1.0 / math.sqrt(HD)
PARTS = CAP + CAPP


def head_rows(q, first, count):
    return jnp.concatenate([q[:, (first + i) * HD : (first + i + 1) * HD] for i in range(count)], 0)


def stats_block(columns):
    rows = columns[0].shape[0]
    lane = lax.broadcasted_iota(jnp.int32, (rows, LANES), 1)
    out = jnp.zeros((rows, LANES), jnp.float32)
    for h, column in enumerate(columns):
        out = jnp.where(lane == h, column, out)
    return out


def list_pages(send, wanted, owner, target, slots, page_list, slot_list, base):
    for c in range(PARTS):
        page_list[base + c] = 0
        slot_list[base + c] = -1
    sends = send.shape[1] // 3

    def sent(j, count):
        hit = send[owner, 3 * j + 1] == target

        @pl.when(hit)
        def _():
            page_list[base + count] = send[owner, 3 * j]
            slot_list[base + count] = send[owner, 3 * j + 2]

        return count + hit.astype(jnp.int32)

    lax.fori_loop(0, sends, sent, 0, unroll=True)

    def prefix(j, count):
        page = wanted[target, j]
        hit = page // PRE_DEV == owner

        @pl.when(hit)
        def _():
            page_list[base + CAP + count] = page % PRE_DEV
            slot_list[base + CAP + count] = slots + j

        return count + hit.astype(jnp.int32)

    lax.fori_loop(0, wanted.shape[1], prefix, 0, unroll=True)


def owner_part(qa, pages, slot_list, base, out, held, per_held, maxp):
    rows = qa.shape[0]
    wide = held * per_held * HD
    q = qa[:, :wide].astype(jnp.float32)
    tab = qa[:, wide : wide + LANES].astype(jnp.float32)
    cnt = qa[:, wide + LANES : wide + 2 * LANES].astype(jnp.float32)
    lane = lax.broadcasted_iota(jnp.int32, (rows, LANES), 1)
    masks = []
    for c in range(PARTS):
        entry = slot_list[base + c].astype(jnp.float32)
        valid = jnp.sum(jnp.where(tab == entry, cnt, 0.0), 1, keepdims=True)
        masks.append(lane.astype(jnp.float32) < valid)
    mask = jnp.concatenate(masks, 1)[None]
    tops, sums = [], []
    for j in range(held):
        qj = head_rows(q, j * per_held, per_held).astype(jnp.bfloat16)
        keys = jnp.concatenate([pages[c, :, 2 * j * HD : (2 * j + 1) * HD] for c in range(PARTS)], 0)
        values = jnp.concatenate([pages[c, :, (2 * j + 1) * HD : (2 * j + 2) * HD] for c in range(PARTS)], 0)
        s = lax.dot_general(qj, keys, (((1,), (1,)), ((), ())), preferred_element_type=jnp.float32)
        s = s.reshape(per_held, rows, s.shape[1]) * SCALE
        s = jnp.where(mask, s, NEG)
        top = jnp.max(s, 2, keepdims=True)
        p = jnp.where(mask, jnp.exp(s - top), 0.0)
        total = jnp.sum(p, 2, keepdims=True)
        p = p.reshape(per_held * rows, p.shape[2]).astype(jnp.bfloat16)
        acc = jnp.dot(p, values, preferred_element_type=jnp.float32)
        out[j * per_held * rows : (j + 1) * per_held * rows, :] = acc
        tops += [top[i] for i in range(per_held)]
        sums += [total[i] for i in range(per_held)]
    end = held * per_held * rows
    out[end : end + rows, :] = stats_block(tops)
    out[end + rows : end + 2 * rows, :] = stats_block(sums)


def resident_part(qa, new_kv, send, tables, lengths, group, kv, pages, flags, sems, out, held, per_held):
    rows = qa.shape[0]
    maxp = tables.shape[1]
    slots = flags.shape[0]
    copies = []
    for r in range(rows):
        for e in range(maxp):
            slot = tables[r, e]
            slot = jnp.where(slot < slots, slot, 0)
            copy = pltpu.make_async_copy(kv.at[slot], pages.at[r, e], sems.at[r, e])
            copy.start()
            copies.append(copy)

    def clear(i, _):
        flags[i] = 0
        return 0

    lax.fori_loop(0, slots, clear, 0, unroll=8)
    sends = send.shape[1] // 3

    def mark(o, _):
        for j in range(sends):

            @pl.when(send[o, 3 * j + 1] == group)
            def _():
                flags[send[o, 3 * j + 2]] = 1

        return 0

    lax.fori_loop(0, send.shape[0], mark, 0)
    wide = held * per_held * HD
    q = qa[:, :wide].astype(jnp.float32)
    fresh = new_kv[...].astype(jnp.float32)
    lane = lax.broadcasted_iota(jnp.int32, (rows, LANES), 1)
    row = lax.broadcasted_iota(jnp.int32, (rows, LANES), 0)
    qs, owns, accs, tops, sums = [], [], [], [], []
    for j in range(held):
        qf = head_rows(q, j * per_held, per_held)
        qs.append(qf.astype(jnp.bfloat16))
        key = fresh[:, 2 * j * HD : (2 * j + 1) * HD]
        own = jnp.sum(qf.reshape(per_held, rows, HD) * key[None], 2, keepdims=True) * SCALE
        owns.append(own)
        tops.append(own)
        sums.append(jnp.zeros_like(own))
        accs.append(jnp.zeros((per_held * rows, HD), jnp.float32))
    for r in range(rows):
        masks = []
        for e in range(maxp):
            slot = tables[r, e]
            here = jnp.logical_and(slot < slots, flags[jnp.minimum(slot, slots - 1)] == 0)
            valid = jnp.where(here, lengths[0, r] - e * LANES, 0)
            masks.append(jnp.logical_and(lane < valid, row == r))
        mask = jnp.concatenate(masks, 1)[None]
        for e in range(maxp):
            copies[r * maxp + e].wait()
        for j in range(held):
            keys = jnp.concatenate([pages[r, e, :, 2 * j * HD : (2 * j + 1) * HD] for e in range(maxp)], 0)
            values = jnp.concatenate([pages[r, e, :, (2 * j + 1) * HD : (2 * j + 2) * HD] for e in range(maxp)], 0)
            s = lax.dot_general(qs[j], keys, (((1,), (1,)), ((), ())), preferred_element_type=jnp.float32)
            s = s.reshape(per_held, rows, s.shape[1]) * SCALE
            s = jnp.where(mask, s, NEG)
            top = jnp.maximum(jnp.max(s, 2, keepdims=True), owns[j])
            p = jnp.where(mask, jnp.exp(s - top), 0.0)
            sums[j] += jnp.sum(p, 2, keepdims=True)
            tops[j] = jnp.maximum(tops[j], top)
            p = p.reshape(per_held * rows, p.shape[2]).astype(jnp.bfloat16)
            accs[j] += jnp.dot(p, values, preferred_element_type=jnp.float32)
    all_tops, all_sums = [], []
    for j in range(held):
        value = fresh[:, (2 * j + 1) * HD : (2 * j + 2) * HD]
        lift = jnp.exp(owns[j] - tops[j])
        weight = lift.astype(jnp.bfloat16).astype(jnp.float32)
        acc = accs[j].reshape(per_held, rows, HD) + weight * value[None]
        out[j * per_held * rows : (j + 1) * per_held * rows, :] = acc.reshape(per_held * rows, HD)
        total = sums[j] + lift
        all_tops += [tops[j][i] for i in range(per_held)]
        all_sums += [total[i] for i in range(per_held)]
    end = held * per_held * rows
    out[end : end + rows, :] = stats_block(all_tops)
    out[end + rows : end + 2 * rows, :] = stats_block(all_sums)


def first_kernel(held, per_held, send, wanted, tables, lengths, qa, new_kv, kv, out, pages, flags, page_list, slot_list, sems):
    group = lax.axis_index("group")
    prefill = lax.axis_index("role") == 0

    @pl.when(prefill)
    def _():
        list_pages(send, wanted, group, group, kv.shape[0], page_list, slot_list, 0)
        copies = [pltpu.make_async_copy(kv.at[page_list[c]], pages.at[0, c], sems.at[0, c]) for c in range(PARTS)]
        for copy in copies:
            copy.start()
        for copy in copies:
            copy.wait()
        owner_part(qa, pages.at[0], slot_list, 0, out, held, per_held, tables.shape[1])

    @pl.when(jnp.logical_not(prefill))
    def _():
        resident_part(qa, new_kv, send, tables, lengths, group, kv, pages, flags, sems, out, held, per_held)


def second_kernel(held, per_held, maxp, count, send, wanted, *refs):
    qas, kv, outs = refs[:count], refs[count], refs[count + 1 : 2 * count + 1]
    pages, page_list, slot_list, sems = refs[2 * count + 1 :]
    group = lax.axis_index("group")
    groups = count + 1

    @pl.when(lax.axis_index("role") == 0)
    def _():
        copies = []
        for k in range(count):
            target = lax.rem(group - (k + 1) + groups, groups)
            list_pages(send, wanted, group, target, kv.shape[0], page_list, slot_list, k * PARTS)
            for c in range(PARTS):
                copy = pltpu.make_async_copy(kv.at[page_list[k * PARTS + c]], pages.at[k, c], sems.at[k, c])
                copy.start()
                copies.append(copy)
        for k in range(count):
            for c in range(PARTS):
                copies[k * PARTS + c].wait()
            owner_part(qas[k], pages.at[k], slot_list, k * PARTS, outs[k], held, per_held, maxp)


def merge_kernel(heads, rows, *refs):
    parts, out = refs[:-1], refs[-1]
    end = heads * rows
    tops = [part[end : end + rows, :] for part in parts]
    top = functools.reduce(jnp.maximum, tops)
    factors = [jnp.exp(t - top) for t in tops]
    total = functools.reduce(jnp.add, [f * part[end + rows : end + 2 * rows, :] for f, part in zip(factors, parts)])
    lane = lax.broadcasted_iota(jnp.int32, total.shape, 1)
    total = jnp.where(lane < heads, total, 1.0)
    factors = [f / total for f in factors]
    columns = []
    for h in range(heads):
        terms = [f[:, h : h + 1] * part[h * rows : (h + 1) * rows, :] for f, part in zip(factors, parts)]
        columns.append(functools.reduce(jnp.add, terms))
    out[...] = jnp.concatenate(columns, 1).astype(out.dtype)


def per_device(kv_pages, send_list, wanted, lengths, tables, queries, new_kv, out_weight):
    stored = kv_pages[0, 0, 0]
    slots, page = stored.shape[0], stored.shape[1]
    groups, tps = lax.axis_size("group"), lax.axis_size("tp")
    held = max(1, KVH // tps)
    rows, wide = queries.shape[1], queries.shape[2]
    heads = wide // HD
    per_held = heads // held
    maxp = tables.shape[2]
    send = send_list.reshape(groups, -1)
    counts = jnp.clip(lengths[0][:, None] - jnp.arange(maxp, dtype=jnp.int32)[None, :] * page, 0, page)
    pad = jnp.zeros((rows, LANES - maxp), jnp.bfloat16)
    qa = jnp.concatenate(
        [queries[0], tables[0].astype(jnp.bfloat16), pad, counts.astype(jnp.bfloat16), pad], 1
    )
    asked = [
        lax.ppermute(qa, ("role", "group"), [(i, (i + k) % groups) for i in range(groups)]) for k in range(1, groups)
    ]
    part_shape = jax.ShapeDtypeStruct(((heads + 2) * rows, HD), jnp.float32)
    smem = pl.BlockSpec(memory_space=pltpu.SMEM)
    vmem = pl.BlockSpec(memory_space=pltpu.VMEM)
    hbm = pl.BlockSpec(memory_space=pl.ANY)
    page_shape = stored.shape[1:]
    mine = pl.pallas_call(
        functools.partial(first_kernel, held, per_held),
        out_shape=part_shape,
        in_specs=[smem] * 4 + [vmem, vmem, hbm],
        out_specs=vmem,
        scratch_shapes=[
            pltpu.VMEM((rows, maxp) + page_shape, jnp.bfloat16),
            pltpu.SMEM((slots,), jnp.int32),
            pltpu.SMEM((PARTS,), jnp.int32),
            pltpu.SMEM((PARTS,), jnp.int32),
            pltpu.SemaphoreType.DMA((rows, maxp)),
        ],
        compiler_params=pltpu.CompilerParams(vmem_limit_bytes=20 * 2**20),
        name="resident",
    )(send, wanted, tables[0], lengths, qa, new_kv[0], stored)
    count = groups - 1
    theirs = pl.pallas_call(
        functools.partial(second_kernel, held, per_held, maxp, count),
        out_shape=[part_shape] * count,
        in_specs=[smem] * 2 + [vmem] * count + [hbm],
        out_specs=[vmem] * count,
        scratch_shapes=[
            pltpu.VMEM((count, PARTS) + page_shape, jnp.bfloat16),
            pltpu.SMEM((count * PARTS,), jnp.int32),
            pltpu.SMEM((count * PARTS,), jnp.int32),
            pltpu.SemaphoreType.DMA((count, PARTS)),
        ],
        compiler_params=pltpu.CompilerParams(vmem_limit_bytes=20 * 2**20),
        name="owned",
    )(send, wanted, *asked, stored)
    parts = [mine, lax.ppermute(mine, "role", [(0, 1)])]
    for k in range(1, groups):
        parts.append(
            lax.ppermute(theirs[k - 1], ("role", "group"), [(i, groups + (i - k) % groups) for i in range(groups)])
        )
    attended = pl.pallas_call(
        functools.partial(merge_kernel, heads, rows),
        out_shape=jax.ShapeDtypeStruct((rows, wide), jnp.bfloat16),
        in_specs=[vmem] * len(parts),
        out_specs=vmem,
        name="merge",
    )(*parts)
    partner = lax.ppermute(attended, "role", [(1, 0)])
    heads_here = jnp.where(lax.axis_index("role") == 0, partner, attended)
    partial_value = jnp.dot(heads_here, out_weight, preferred_element_type=jnp.float32)
    me = lax.axis_index("tp")
    share = partial_value.shape[1] // tps

    def chunk(index):
        return lax.dynamic_slice_in_dim(partial_value, lax.rem(index, tps) * share, share, 1)

    total = chunk(me)
    for d in range(1, tps):
        total = total + lax.ppermute(chunk(me + d), "tp", [(i, (i + d) % tps) for i in range(tps)])
    return total.astype(jnp.bfloat16)[None]


def solution(mesh):
    return jax.shard_map(
        per_device,
        mesh=mesh,
        in_specs=(
            P("role", "group", "tp", None, None, None),
            P(),
            P(),
            P("group", None),
            P("group", None, None),
            P("group", None, "tp"),
            P("group", None, "tp"),
            P("tp", "role"),
        ),
        out_specs=P("group", None, ("role", "tp")),
        check_vma=False,
    )
```

time: 277 us -> 74.5 us (0.27)
  waiting for transfers between devices: 175 us -> 11.1 us
  local copies, waits for them, and re-layouts: 62.8 us -> 11.8 us
  starting transfers between devices: 8.15 us -> 29 us
  between operations: 13.6 us -> 0.22 us
  Pallas kernels: 0 us -> 11.5 us
  other arithmetic: 10.7 us -> 2.04 us
  matrix products: 5.25 us -> 8.04 us
    all_to_all x1 -> x0, waiting for transfers between devices: 151 us -> none  [per_device(): lax.all_to_all(parcel, ('role', 'group'), split_axis=0, concat_axis=0, ti...]
    ppermute x1 -> x11, starting transfers between devices: 1.29 us -> 29 us  [the longest x3 12.7 us: per_device(): lax.ppermute(qa, ('role', 'group'), [(i, (i + k) % groups) for i in range...]
    reduce_scatter x1 -> x0, waiting for transfers between devices: 22.1 us -> none  [per_device(): lax.psum_scatter(partial_value, 'tp', scatter_dimension=1, tiled=True)]
    gather x3 -> x0, local copies, waits for them, and re-layouts: 17.1 us -> none  [the longest x1 9.1 us: per_device(): gathered = page_pool[tables[0]].reshape(row_count, -1, held_count, 2 * HD)]
    reshape x1, local copies, waits for them, and re-layouts: 12.5 us -> 0.09 us  [per_device(): send = send_list.reshape(groups, -1)]
    slice x5 -> x0, local copies, waits for them, and re-layouts: 12.4 us -> none  [the longest x1 8.3 us: per_device(): cache_keys = gathered[..., :HD]]
    pallas_call x0 -> x3, Pallas kernels: none -> 11.5 us  [the longest x1 6.52 us: per_device(): pl.pallas_call(functools.partial(second_kernel, held, per_held, maxp, cou...]
    scatter x3 -> x0, local copies, waits for them, and re-layouts: 10.3 us -> none  [the longest x1 5.2 us: per_device(): parcel = jnp.zeros((blocks * block_width,) + page_shape, stored.dtype).at...]
  transfers between devices with their start and end apart: 4 -> 11, of which waited for: 3 -> 5; matrix products, arithmetic and copies ran while one was open for 8% -> 1% of each run, Pallas kernels for 0% -> 13%
where the time goes in v1:
time: 74.5 us; the launch traced here: 73.8 us
  starting transfers between devices  29 us (39%)
  local copies, waits for them, and re-layouts  11.8 us (16%)
  Pallas kernels  11.5 us (15%)
  waiting for transfers between devices  11.1 us (15%)
  matrix products  8.04 us (11%)
  other arithmetic  2.04 us (3%)
    ppermute x3, starting transfers between devices, per_device(): lax.ppermute(qa, ('role', 'group'), [(i, (i + k) % groups) for i in range...  12.7 us
    unnamed x23, local copies, waits for them, and re-layouts  10.9 us
    dot_general x1, matrix products, per_device(): jnp.dot(heads_here, out_weight, preferred_element_type=jnp.float32)  8.04 us
    ppermute x1, starting transfers between devices, per_device(): parts = [mine, lax.ppermute(mine, 'role', [(0, 1)])]  7.57 us
    pallas_call x1, Pallas kernels, per_device(): pl.pallas_call(functools.partial(second_kernel, held, per_held, maxp, cou...  6.52 us
    ppermute x1, waiting for transfers between devices, per_device(): partner = lax.ppermute(attended, 'role', [(1, 0)])  5.46 us
    ppermute x3, starting transfers between devices, per_device(): lax.ppermute(theirs[k - 1], ('role', 'group'), [(i, groups + (i - k) % gr...  3.88 us
    ppermute x3, waiting for transfers between devices, per_device(): lax.ppermute(chunk(me + d), 'tp', [(i, (i + d) % tps) for i in range(tps)])  3.71 us
  transfers between devices with their start and end apart: 11, of which 5 were waited for; matrix products, arithmetic and copies ran while one was open for 1% of the time, Pallas kernels for 13%

profile of v1, /device:TPU:0, one launch (start us, length us, event | category | flops | bytes accessed | tf_op | source)
XLA Modules:
  0.0 73.8 jit_solution(13668243412372422449)
XLA Ops:
  0.0 0.7 bitcast_convert_fusion
  0.7 0.7 clamp_convert_fusion
  1.4 0.8 %concatenate.3.qa = bf16[8,2304]{1,0:T(8,128)(2,1)S(1)} concatenate(bf16[8,2048]{1,0:T(8,128)(2,1)} %bitcast.14, bf16[8,8]{1,0:T(8,128)(2,1)S(1)} %bitcast_convert_fusion, bf16[8,120]{1,0:T(8,128)(2,1)S(1)} %broadcast_in_dim.7, bf16[8,8]{1,0:T(8,128)(2,1)S(1)} %clamp_convert_fusion, bf16[8,120]{1,0:T(8,128)(2,1)S(1)} %broadcast_in_dim.7), dimensions={1} | concatenate | bytes 73728 | tf_op jit(solution)/shard_map/concatenate | solution.py:253
  2.3 4.9 %collective-permute-start.1 = (bf16[8,2304]{1,0:T(8,128)(2,1)S(1)}, bf16[8,2304]{1,0:T(8,128)(2,1)S(1)}, u32[]{:S(2)}, u32[]{:S(2)}) collective-permute-start(bf16[8,2304]{1,0:T(8,128)(2,1)S(1)} %concatenate.3.qa), channel_id=1, source_target_pairs={{0,4},{4,8},{8,12},{12,0},{1,5},{5,9},{9,13},{13,1},{2,6},{6,10},{... | collective-permute-start | bytes 110600 | tf_op jit(solution)/shard_map/ppermute | solution.py:257
  7.2 4.5 %collective-permute-start.2 = (bf16[8,2304]{1,0:T(8,128)(2,1)S(1)}, bf16[8,2304]{1,0:T(8,128)(2,1)S(1)}, u32[]{:S(2)}, u32[]{:S(2)}) collective-permute-start(bf16[8,2304]{1,0:T(8,128)(2,1)S(1)} %concatenate.3.qa), channel_id=1, source_target_pairs={{0,8},{4,12},{8,0},{12,4},{1,9},{5,13},{9,1},{13,5},{2,10},{6,14},... | collective-permute-start | bytes 110600 | tf_op jit(solution)/shard_map/ppermute | solution.py:257
  11.7 3.3 %collective-permute-start.3 = (bf16[8,2304]{1,0:T(8,128)(2,1)S(1)}, bf16[8,2304]{1,0:T(8,128)(2,1)S(1)}, u32[]{:S(2)}, u32[]{:S(2)}) collective-permute-start(bf16[8,2304]{1,0:T(8,128)(2,1)S(1)} %concatenate.3.qa), channel_id=1, source_target_pairs={{0,12},{4,0},{8,4},{12,8},{1,13},{5,1},{9,5},{13,9},{2,14},{6,2},{... | collective-permute-start | bytes 110600 | tf_op jit(solution)/shard_map/ppermute | solution.py:257
  15.0 0.8 %copy.10 = s32[4,12,3]{2,1,0:T(8,128)S(1)} copy(s32[4,12,3]{1,0,2:T(4,128)} %param.9) | data formatting | bytes 1152 | tf_op args[1]
  15.9 3.4 %copy-done = bf16[1,1,1,64,128,512]{5,4,3,2,1,0:T(8,128)(2,1)S(1)} copy-done((bf16[1,1,1,64,128,512]{5,4,3,2,1,0:T(8,128)(2,1)S(1)}, bf16[1,1,1,64,128,512]{5,4,3,2,1,0:T(8,128)(2,1)}, u32[]{:S(2)}) %copy-start) | copy-done | bytes 8388632
  19.9 0.7 copy-done.4
  22.0 3.1 %resident.1.refs_0_ = f32[144,128]{1,0:T(8,128)S(1)} custom-call(s32[4,36]{1,0:T(4,128)S(1)} %reshape.9.send, s32[4,6]{1,0:T(4,128)S(1)} %copy-done.5, s32[8,8]{1,0:T(8,128)S(1)} %bitcast.11, s32[1,8]{1,0:T(1,128)S(1)} %copy-done.6, bf16[8,2304]{1,0:T(8,128)(2,1)S(1)} %concatenate.3.qa, bf16[8,512]{1,0:T(8,128)(2,1)S(1)} %bitcast.12, ...), custom_call_target="tpu_custom_call" | custom-call | tf_op jit(solution)/shard_map/resident/pallas_call | solution.py:264
  25.1 7.6 %collective-permute-start = (f32[144,128]{1,0:T(8,128)S(1)}, f32[144,128]{1,0:T(8,128)S(1)}, u32[]{:S(2)}, u32[]{:S(2)}) collective-permute-start(f32[144,128]{1,0:T(8,128)S(1)} %resident.1.refs_0_), channel_id=1, source_target_pairs={{0,16},{1,17},{2,18},{3,19},{4,20},{5,21},{6,22},{7,23},{8,24},{9,... | collective-permute-start | bytes 221192 | tf_op jit(solution)/shard_map/ppermute | solution.py:294
  32.7 3.4 %copy-done.1 = bf16[1,1,1,64,128,512]{5,4,3,2,1,0:T(8,128)(2,1)S(1)} copy-done((bf16[1,1,1,64,128,512]{5,4,3,2,1,0:T(8,128)(2,1)S(1)}, bf16[1,1,1,64,128,512]{5,4,3,2,1,0:T(8,128)(2,1)}, u32[]{:S(2)}) %copy-start.1) | copy-done | bytes 8388632
  36.1 6.5 %owned.1 = (f32[144,128]{1,0:T(8,128)S(1)}, f32[144,128]{1,0:T(8,128)S(1)}, f32[144,128]{1,0:T(8,128)S(1)}) custom-call(s32[4,36]{1,0:T(4,128)S(1)} %reshape.9.send, s32[4,6]{1,0:T(4,128)S(1)} %copy-done.5, bf16[8,2304]{1,0:T(8,128)(2,1)S(1)} %collective-permute-done.1.refs_0_, bf16[8,2304]{1,0:T(8,128)(2,1)S(1)} %collective-permute-done.2.refs_1_, ...), custom_call_target="tpu_custom_call" | custom-call | tf_op jit(solution)/shard_map/owned/pallas_call | solution.py:280
  42.7 1.3 %collective-permute-start.4 = (f32[144,128]{1,0:T(8,128)S(1)}, f32[144,128]{1,0:T(8,128)S(1)}, u32[]{:S(2)}, u32[]{:S(2)}) collective-permute-start(f32[144,128]{1,0:T(8,128)S(1)} %get-tuple-element.8), channel_id=1, source_target_pairs={{0,28},{4,16},{8,20},{12,24},{1,29},{5,17},{9,21},{13,25},{2,30},{... | collective-permute-start | bytes 221192 | tf_op jit(solution)/shard_map/ppermute | solution.py:297
  44.0 1.3 %collective-permute-start.5 = (f32[144,128]{1,0:T(8,128)S(1)}, f32[144,128]{1,0:T(8,128)S(1)}, u32[]{:S(2)}, u32[]{:S(2)}) collective-permute-start(f32[144,128]{1,0:T(8,128)S(1)} %get-tuple-element.9), channel_id=1, source_target_pairs={{0,24},{4,28},{8,16},{12,20},{1,25},{5,29},{9,17},{13,21},{2,26},{... | collective-permute-start | bytes 221192 | tf_op jit(solution)/shard_map/ppermute | solution.py:297
  45.3 1.3 %collective-permute-start.6 = (f32[144,128]{1,0:T(8,128)S(1)}, f32[144,128]{1,0:T(8,128)S(1)}, u32[]{:S(2)}, u32[]{:S(2)}) collective-permute-start(f32[144,128]{1,0:T(8,128)S(1)} %get-tuple-element.10), channel_id=1, source_target_pairs={{0,20},{4,24},{8,28},{12,16},{1,21},{5,25},{9,29},{13,17},{2,22},{... | collective-permute-start | bytes 221192 | tf_op jit(solution)/shard_map/ppermute | solution.py:297
  47.2 1.3 %collective-permute-done.6.refs_4_ = f32[144,128]{1,0:T(8,128)S(1)} collective-permute-done((f32[144,128]{1,0:T(8,128)S(1)}, f32[144,128]{1,0:T(8,128)S(1)}, u32[]{:S(2)}, u32[]{:S(2)}) %collective-permute-start.6) | collective-permute-done | bytes 73760 | tf_op jit(solution)/shard_map/ppermute | solution.py:297
  49.2 1.8 %merge.1 = bf16[8,2048]{1,0:T(8,128)(2,1)} custom-call(f32[144,128]{1,0:T(8,128)} %copy-done.2, f32[144,128]{1,0:T(8,128)} %copy-done.7, f32[144,128]{1,0:T(8,128)} %copy-done.8, f32[144,128]{1,0:T(8,128)} %copy-done.9, f32[144,128]{1,0:T(8,128)} %copy-done.10), custom_call_target="tpu_custom_call" | custom-call | tf_op jit(solution)/shard_map/merge/pallas_call | solution.py:299
  51.0 1.3 %collective-permute-start.7 = (bf16[8,2048]{1,0:T(8,128)(2,1)}, bf16[8,2048]{1,0:T(8,128)(2,1)S(1)}, u32[]{:S(2)}, u32[]{:S(2)}) collective-permute-start(bf16[8,2048]{1,0:T(8,128)(2,1)} %merge.1), channel_id=1, source_target_pairs={{16,0},{17,1},{18,2},{19,3},{20,4},{21,5},{22,6},{23,7},{24,8},{25... | collective-permute-start | bytes 98312 | tf_op jit(solution)/shard_map/ppermute | solution.py:306
  52.3 5.5 %collective-permute-done.7 = bf16[8,2048]{1,0:T(8,128)(2,1)S(1)} collective-permute-done((bf16[8,2048]{1,0:T(8,128)(2,1)}, bf16[8,2048]{1,0:T(8,128)(2,1)S(1)}, u32[]{:S(2)}, u32[]{:S(2)}) %collective-permute-start.7) | collective-permute-done | bytes 32800 | tf_op jit(solution)/shard_map/ppermute | solution.py:306
  57.8 8.0 %fusion = f32[8,4096]{1,0:T(8,128)S(1)} fusion(bf16[2048,4096]{1,0:T(8,128)(2,1)} %param.15, bf16[8,2048]{1,0:T(8,128)(2,1)S(1)} %collective-permute-done.7, bf16[8,2048]{1,0:T(8,128)(2,1)} %merge.1, pred[]{:T(512)S(6)} %eq.3), kind=kOutput, calls=%fused_computation.1 | convolution fusion | flops 134234112 | bytes 16973824 | tf_op jit(solution)/shard_map/dot_general | solution.py:308
  65.8 2.5 %collective-permute-start.10 = (f32[8,1024]{1,0:T(8,128)S(1)}, f32[8,1024]{1,0:T(8,128)S(1)}, u32[]{:S(2)}, u32[]{:S(2)}) collective-permute-start(f32[8,1024]{1,0:T(8,128)S(1)} %get-tuple-element.12), channel_id=1, source_target_pairs={{0,3},{1,0},{2,1},{3,2},{4,7},{5,4},{6,5},{7,6},{8,11},{9,8},{10,9... | collective-permute-start | bytes 98312 | tf_op jit(solution)/shard_map/ppermute | solution.py:317
  68.3 1.1 %collective-permute-start.9 = (f32[8,1024]{1,0:T(8,128)S(1)}, f32[8,1024]{1,0:T(8,128)S(1)}, u32[]{:S(2)}, u32[]{:S(2)}) collective-permute-start(f32[8,1024]{1,0:T(8,128)S(1)} %get-tuple-element.13), channel_id=1, source_target_pairs={{0,2},{1,3},{2,0},{3,1},{4,6},{5,7},{6,4},{7,5},{8,10},{9,11},{10,... | collective-permute-start | bytes 98312 | tf_op jit(solution)/shard_map/ppermute | solution.py:317
  69.9 3.2 %collective-permute-done.8 = f32[8,1024]{1,0:T(8,128)S(1)} collective-permute-done((f32[8,1024]{1,0:T(8,128)S(1)}, f32[8,1024]{1,0:T(8,128)S(1)}, u32[]{:S(2)}, u32[]{:S(2)}) %collective-permute-start.8) | collective-permute-done | bytes 32800 | tf_op jit(solution)/shard_map/ppermute | solution.py:317
  (33 shorter events, 4.5 us)
Async XLA Ops:
  2.3 30.4 %collective-permute-start.1 = (bf16[8,2304]{1,0:T(8,128)(2,1)S(1)}, bf16[8,2304]{1,0:T(8,128)(2,1)S(1)}, u32[]{:S(2)}, u32[]{:S(2)}) collective-permute-start(bf16[8,2304]{1,0:T(8,128)(2,1)S(1)} %concatenate.3.qa), channel_id=1, source_target_pairs={{0,4},{4,8},{8,12},{12,0},{1,5},{5,9},{9,13},{13,1},{2,6},{6,10},{... | collective-permute-start | bytes 110600 | tf_op jit(solution)/shard_map/ppermute | solution.py:257
  7.2 25.5 %collective-permute-start.2 = (bf16[8,2304]{1,0:T(8,128)(2,1)S(1)}, bf16[8,2304]{1,0:T(8,128)(2,1)S(1)}, u32[]{:S(2)}, u32[]{:S(2)}) collective-permute-start(bf16[8,2304]{1,0:T(8,128)(2,1)S(1)} %concatenate.3.qa), channel_id=1, source_target_pairs={{0,8},{4,12},{8,0},{12,4},{1,9},{5,13},{9,1},{13,5},{2,10},{6,14},... | collective-permute-start | bytes 110600 | tf_op jit(solution)/shard_map/ppermute | solution.py:257
  11.7 21.0 %collective-permute-start.3 = (bf16[8,2304]{1,0:T(8,128)(2,1)S(1)}, bf16[8,2304]{1,0:T(8,128)(2,1)S(1)}, u32[]{:S(2)}, u32[]{:S(2)}) collective-permute-start(bf16[8,2304]{1,0:T(8,128)(2,1)S(1)} %concatenate.3.qa), channel_id=1, source_target_pairs={{0,12},{4,0},{8,4},{12,8},{1,13},{5,1},{9,5},{13,9},{2,14},{6,2},{... | collective-permute-start | bytes 110600 | tf_op jit(solution)/shard_map/ppermute | solution.py:257
  15.9 3.4 %copy-start = (bf16[1,1,1,64,128,512]{5,4,3,2,1,0:T(8,128)(2,1)S(1)}, bf16[1,1,1,64,128,512]{5,4,3,2,1,0:T(8,128)(2,1)}, u32[]{:S(2)}) copy-start(bf16[1,1,1,64,128,512]{5,4,3,2,1,0:T(8,128)(2,1)} %param.8) | copy-start | bytes 25165828
  19.2 0.7 copy-start.3
  19.9 0.7 copy-start.4
  20.6 0.7 copy-start.5
  21.3 0.7 copy-start.6
  25.1 23.4 %copy-start.2 = (f32[144,128]{1,0:T(8,128)}, f32[144,128]{1,0:T(8,128)S(1)}, u32[]{:S(2)}) copy-start(f32[144,128]{1,0:T(8,128)S(1)} %resident.1.refs_0_) | copy-start | bytes 221188
  25.1 21.4 %collective-permute-start = (f32[144,128]{1,0:T(8,128)S(1)}, f32[144,128]{1,0:T(8,128)S(1)}, u32[]{:S(2)}, u32[]{:S(2)}) collective-permute-start(f32[144,128]{1,0:T(8,128)S(1)} %resident.1.refs_0_), channel_id=1, source_target_pairs={{0,16},{1,17},{2,18},{3,19},{4,20},{5,21},{6,22},{7,23},{8,24},{9,... | collective-permute-start | bytes 221192 | tf_op jit(solution)/shard_map/ppermute | solution.py:294
  32.7 3.4 %copy-start.1 = (bf16[1,1,1,64,128,512]{5,4,3,2,1,0:T(8,128)(2,1)S(1)}, bf16[1,1,1,64,128,512]{5,4,3,2,1,0:T(8,128)(2,1)}, u32[]{:S(2)}) copy-start(bf16[1,1,1,64,128,512]{5,4,3,2,1,0:T(8,128)(2,1)} %param.8) | copy-start | bytes 25165828
  42.7 3.9 %collective-permute-start.4 = (f32[144,128]{1,0:T(8,128)S(1)}, f32[144,128]{1,0:T(8,128)S(1)}, u32[]{:S(2)}, u32[]{:S(2)}) collective-permute-start(f32[144,128]{1,0:T(8,128)S(1)} %get-tuple-element.8), channel_id=1, source_target_pairs={{0,28},{4,16},{8,20},{12,24},{1,29},{5,17},{9,21},{13,25},{2,30},{... | collective-permute-start | bytes 221192 | tf_op jit(solution)/shard_map/ppermute | solution.py:297
  44.0 3.3 %collective-permute-start.5 = (f32[144,128]{1,0:T(8,128)S(1)}, f32[144,128]{1,0:T(8,128)S(1)}, u32[]{:S(2)}, u32[]{:S(2)}) collective-permute-start(f32[144,128]{1,0:T(8,128)S(1)} %get-tuple-element.9), channel_id=1, source_target_pairs={{0,24},{4,28},{8,16},{12,20},{1,25},{5,29},{9,17},{13,21},{2,26},{... | collective-permute-start | bytes 221192 | tf_op jit(solution)/shard_map/ppermute | solution.py:297
  45.3 3.3 %collective-permute-start.6 = (f32[144,128]{1,0:T(8,128)S(1)}, f32[144,128]{1,0:T(8,128)S(1)}, u32[]{:S(2)}, u32[]{:S(2)}) collective-permute-start(f32[144,128]{1,0:T(8,128)S(1)} %get-tuple-element.10), channel_id=1, source_target_pairs={{0,20},{4,24},{8,28},{12,16},{1,21},{5,25},{9,29},{13,17},{2,22},{... | collective-permute-start | bytes 221192 | tf_op jit(solution)/shard_map/ppermute | solution.py:297
  46.6 2.0 %copy-start.7 = (f32[144,128]{1,0:T(8,128)}, f32[144,128]{1,0:T(8,128)S(1)}, u32[]{:S(2)}) copy-start(f32[144,128]{1,0:T(8,128)S(1)} %collective-permute-done.refs_1_) | copy-start | bytes 221188
  46.6 1.9 %copy-start.8 = (f32[144,128]{1,0:T(8,128)}, f32[144,128]{1,0:T(8,128)S(1)}, u32[]{:S(2)}) copy-start(f32[144,128]{1,0:T(8,128)S(1)} %collective-permute-done.4.refs_2_) | copy-start | bytes 221188
  47.2 1.3 %copy-start.9 = (f32[144,128]{1,0:T(8,128)}, f32[144,128]{1,0:T(8,128)S(1)}, u32[]{:S(2)}) copy-start(f32[144,128]{1,0:T(8,128)S(1)} %collective-permute-done.5.refs_3_) | copy-start | bytes 221188
  48.5 0.6 copy-start.10
  51.0 6.8 %collective-permute-start.7 = (bf16[8,2048]{1,0:T(8,128)(2,1)}, bf16[8,2048]{1,0:T(8,128)(2,1)S(1)}, u32[]{:S(2)}, u32[]{:S(2)}) collective-permute-start(bf16[8,2048]{1,0:T(8,128)(2,1)} %merge.1), channel_id=1, source_target_pairs={{16,0},{17,1},{18,2},{19,3},{20,4},{21,5},{22,6},{23,7},{24,8},{25... | collective-permute-start | bytes 98312 | tf_op jit(solution)/shard_map/ppermute | solution.py:306
  65.8 4.1 %collective-permute-start.10 = (f32[8,1024]{1,0:T(8,128)S(1)}, f32[8,1024]{1,0:T(8,128)S(1)}, u32[]{:S(2)}, u32[]{:S(2)}) collective-permute-start(f32[8,1024]{1,0:T(8,128)S(1)} %get-tuple-element.12), channel_id=1, source_target_pairs={{0,3},{1,0},{2,1},{3,2},{4,7},{5,4},{6,5},{7,6},{8,11},{9,8},{10,9... | collective-permute-start | bytes 98312 | tf_op jit(solution)/shard_map/ppermute | solution.py:317
  68.3 4.8 %collective-permute-start.8 = (f32[8,1024]{1,0:T(8,128)S(1)}, f32[8,1024]{1,0:T(8,128)S(1)}, u32[]{:S(2)}, u32[]{:S(2)}) collective-permute-start(f32[8,1024]{1,0:T(8,128)S(1)} %get-tuple-element.11), channel_id=1, source_target_pairs={{0,1},{1,2},{2,3},{3,0},{4,5},{5,6},{6,7},{7,4},{8,9},{9,10},{10,1... | collective-permute-start | bytes 98312 | tf_op jit(solution)/shard_map/ppermute | solution.py:317
  68.3 4.8 %collective-permute-start.9 = (f32[8,1024]{1,0:T(8,128)S(1)}, f32[8,1024]{1,0:T(8,128)S(1)}, u32[]{:S(2)}, u32[]{:S(2)}) collective-permute-start(f32[8,1024]{1,0:T(8,128)S(1)} %get-tuple-element.13), channel_id=1, source_target_pairs={{0,2},{1,3},{2,0},{3,1},{4,6},{5,7},{6,4},{7,5},{8,10},{9,11},{10,... | collective-permute-start | bytes 98312 | tf_op jit(solution)/shard_map/ppermute | solution.py:317

commit v2 on v0

v2 whole, which is shorter than its diff:
```python
import functools
import math

import jax
import jax.numpy as jnp
from jax import lax
from jax.experimental import pallas as pl
from jax.experimental.pallas import tpu as pltpu
from jax.sharding import PartitionSpec as P

KVH = 8
HD = 128
CAP = 4
CAPP = 2
PRE_DEV = 8
LANES = 128
NEG = -1e30
SCALE = 1.0 / math.sqrt(HD)
PARTS = CAP + CAPP
MIB = 2**20


def dot(a, b, ca, cb):
    return lax.dot_general(a, b, (((ca,), (cb,)), ((), ())), preferred_element_type=jnp.float32)


def query_block(qa, held, per_held):
    q = qa[:, : held * per_held * HD].astype(jnp.float32)
    rows = q.shape[0]
    bands = []
    for j in range(held):
        heads = [q[:, (j * per_held + i) * HD : (j * per_held + i + 1) * HD] for i in range(per_held)]
        band = jnp.concatenate(heads, 0)
        blank = jnp.zeros_like(band)
        bands.append(jnp.concatenate([band if i == j else blank for i in range(held)], 1))
    return jnp.concatenate(bands, 0).astype(jnp.bfloat16)


def entry_rows(qa, held, per_held, maxp):
    wide = held * per_held * HD
    aux = qa[:, wide : wide + LANES].astype(jnp.float32)
    turned = jnp.concatenate([aux] * (held * per_held), 0).T
    return turned[:maxp], turned[maxp : 2 * maxp]


def lanes_of(page, first, held):
    return jnp.concatenate([page[:, (2 * j + first) * HD : (2 * j + first + 1) * HD] for j in range(held)], 1)


def write_part(out, acc, top, total, held, per_held):
    count = acc.shape[0]
    band = count // held
    for j in range(held):
        out[j * band : (j + 1) * band, :] = acc[j * band : (j + 1) * band, j * HD : (j + 1) * HD]
    out[count : count + 1, :count] = top
    out[count + 1 : count + 2, :count] = total


def owner_part(qa, pages, entries, out, held, per_held, maxp):
    q = query_block(qa, held, per_held)
    tab, cnt = entry_rows(qa, held, per_held, maxp)
    count = q.shape[0]
    token = lax.broadcasted_iota(jnp.int32, (LANES, count), 0).astype(jnp.float32)
    masks = []
    for c in range(PARTS):
        valid = jnp.sum(jnp.where(tab == entries[c : c + 1, :count], cnt, 0.0), 0, keepdims=True)
        masks.append(token < valid)
    mask = jnp.concatenate(masks, 0)
    keys = jnp.concatenate([lanes_of(pages.at[c], 0, held) for c in range(PARTS)], 0)
    values = jnp.concatenate([lanes_of(pages.at[c], 1, held) for c in range(PARTS)], 0)
    s = jnp.where(mask, dot(keys, q, 1, 1) * SCALE, NEG)
    top = jnp.max(s, 0, keepdims=True)
    p = jnp.where(mask, jnp.exp(s - top), 0.0)
    total = jnp.sum(p, 0, keepdims=True)
    acc = dot(p.astype(jnp.bfloat16), values, 0, 0)
    write_part(out, acc, top, total, held, per_held)


def resident_part(qa, new_kv, send, tables, group, kv, pages, sems, out, held, per_held):
    rows = qa.shape[0]
    maxp = tables.shape[1]
    slots = kv.shape[0]
    copies = []
    for r in range(rows):
        for e in range(maxp):
            slot = tables[r, e]
            slot = jnp.where(slot < slots, slot, 0)
            copy = pltpu.make_async_copy(kv.at[slot], pages.at[r, e], sems.at[r, e])
            copy.start()
            copies.append(copy)
    q = query_block(qa, held, per_held)
    tab, cnt = entry_rows(qa, held, per_held, maxp)
    count = q.shape[0]
    gone = tab >= slots
    for o in range(send.shape[1]):
        for i in range(send.shape[2]):
            slot = jnp.where(send[1, o, i] == group, send[2, o, i], -1)
            gone = jnp.logical_or(gone, tab == slot.astype(jnp.float32))
    cnt = jnp.where(gone, 0.0, cnt)
    lane_row = lax.rem(lax.broadcasted_iota(jnp.int32, (1, count), 1), rows)
    token = lax.broadcasted_iota(jnp.int32, (LANES, count), 0).astype(jnp.float32)
    fresh = new_kv[...].astype(jnp.float32)
    fresh = jnp.concatenate([fresh, jnp.zeros_like(fresh)], 0).astype(jnp.bfloat16)
    own_mask = lax.broadcasted_iota(jnp.int32, (2 * rows, count), 0) == lane_row
    own = dot(lanes_of(fresh, 0, held), q, 1, 1) * SCALE
    own_top = jnp.max(jnp.where(own_mask, own, NEG), 0, keepdims=True)
    tops, total, acc = own_top, 0.0, 0.0
    for r in range(rows):
        for e in range(maxp):
            copies[r * maxp + e].wait()
        valid = jnp.where(lane_row == r, cnt, 0.0)
        mask = jnp.concatenate([token < valid[e : e + 1] for e in range(maxp)], 0)
        keys = jnp.concatenate([lanes_of(pages.at[r, e], 0, held) for e in range(maxp)], 0)
        values = jnp.concatenate([lanes_of(pages.at[r, e], 1, held) for e in range(maxp)], 0)
        s = jnp.where(mask, dot(keys, q, 1, 1) * SCALE, NEG)
        top = jnp.maximum(jnp.max(s, 0, keepdims=True), own_top)
        p = jnp.where(mask, jnp.exp(s - top), 0.0)
        total = total + jnp.sum(p, 0, keepdims=True)
        tops = jnp.maximum(tops, top)
        acc = acc + dot(p.astype(jnp.bfloat16), values, 0, 0)
    lift = jnp.where(own_mask, jnp.exp(own - tops), 0.0)
    total = total + jnp.sum(lift, 0, keepdims=True)
    acc = acc + dot(lift.astype(jnp.bfloat16), lanes_of(fresh, 1, held), 0, 0)
    write_part(out, acc, tops, total, held, per_held)


def list_pages(send, wanted, owner, target, slots, page_list, slot_list, base):
    for c in range(PARTS):
        page_list[base + c] = 0
        slot_list[base + c] = -1
    at = jnp.int32(base)
    for i in range(send.shape[2]):
        hit = send[1, owner, i] == target

        @pl.when(hit)
        def _(at=at, i=i):
            page_list[at] = send[0, owner, i]
            slot_list[at] = send[2, owner, i]

        at = at + hit.astype(jnp.int32)
    at = jnp.int32(base + CAP)
    for i in range(wanted.shape[1]):
        page = wanted[target, i]
        first = owner * PRE_DEV
        hit = jnp.logical_and(page >= first, page < first + PRE_DEV)

        @pl.when(hit)
        def _(at=at, i=i, page=page):
            page_list[at] = page - owner * PRE_DEV
            slot_list[at] = slots + i

        at = at + hit.astype(jnp.int32)


def first_kernel(held, per_held, groups, qa, new_kv, send_hbm, wanted_hbm, tables_hbm, kv, *refs):
    out, chosen, entries, pages, send, wanted, tables, page_list, slot_list, int_sems, chosen_sems, sems = refs
    group = lax.axis_index("group")
    prefill = lax.axis_index("role") == 0
    maxp = tables.shape[1]
    ints = [
        pltpu.make_async_copy(a, b, int_sems.at[i])
        for i, (a, b) in enumerate(((send_hbm, send), (wanted_hbm, wanted), (tables_hbm, tables)))
    ]
    for copy in ints:
        copy.start()
    for copy in ints:
        copy.wait()

    @pl.when(prefill)
    def _():
        copies = []
        for k in range(groups):
            target = lax.rem(group - k + groups, groups)
            list_pages(send, wanted, group, target, kv.shape[0], page_list, slot_list, k * PARTS)
            for c in range(PARTS):
                at = k * PARTS + c
                copy = pltpu.make_async_copy(kv.at[page_list[at]], chosen.at[at], chosen_sems.at[at])
                copy.start()
                copies.append(copy)
                entry = slot_list[at].astype(jnp.float32)
                entries[at : at + 1, :] = jnp.full((1, LANES), entry, jnp.float32)
        for copy in copies[:PARTS]:
            copy.wait()
        owner_part(qa, chosen.at[pl.ds(0, PARTS)], entries[:PARTS, :], out, held, per_held, maxp)
        for copy in copies[PARTS:]:
            copy.wait()

    @pl.when(jnp.logical_not(prefill))
    def _():
        resident_part(qa, new_kv, send, tables, group, kv, pages, sems, out, held, per_held)


def second_kernel(held, per_held, maxp, count, chosen, entries, *refs):
    qas, outs = refs[:count], refs[count:]

    @pl.when(lax.axis_index("role") == 0)
    def _():
        for k in range(count):
            at = (k + 1) * PARTS
            owner_part(
                qas[k], chosen.at[pl.ds(at, PARTS)], entries[at : at + PARTS, :], outs[k], held, per_held, maxp
            )


def merge_kernel(heads, rows, *refs):
    parts, out = refs[:-1], refs[-1]
    count = heads * rows
    pad = -len(parts) % 8
    tops = jnp.concatenate([part[count : count + 1, :count] for part in parts], 0)
    totals = jnp.concatenate([part[count + 1 : count + 2, :count] for part in parts], 0)
    factors = jnp.exp(tops - jnp.max(tops, 0, keepdims=True))
    factors = factors / jnp.sum(factors * totals, 0, keepdims=True)
    factors = jnp.concatenate([factors, jnp.zeros((pad, count), jnp.float32)], 0).T
    terms = [factors[:, i : i + 1] * part[:count, :] for i, part in enumerate(parts)]
    merged = functools.reduce(jnp.add, terms)
    out[...] = jnp.concatenate([merged[h * rows : (h + 1) * rows] for h in range(heads)], 1).astype(out.dtype)


def project_kernel(steps, attended, partner, weight, *outs):
    tps = lax.axis_size("tp")
    share = outs[0].shape[1]
    here = jnp.where(lax.axis_index("role") == 0, partner[...].astype(jnp.float32), attended[...].astype(jnp.float32))
    here = here.astype(jnp.bfloat16)
    for d, out in zip(steps, outs):
        first = lax.rem(lax.axis_index("tp") + d, tps) * share
        columns = pl.ds(pl.multiple_of(first, LANES), share)
        out[...] = jnp.dot(here, weight[:, columns], preferred_element_type=jnp.float32)


def per_device(kv_pages, send_list, wanted, lengths, tables, queries, new_kv, out_weight):
    stored = kv_pages[0, 0, 0]
    slots, page = stored.shape[0], stored.shape[1]
    groups, tps = lax.axis_size("group"), lax.axis_size("tp")
    held = max(1, KVH // tps)
    rows, wide = queries.shape[1], queries.shape[2]
    heads = wide // HD
    per_held = heads // held
    maxp = tables.shape[2]
    send = jnp.transpose(send_list, (2, 0, 1))
    counts = jnp.clip(lengths[0][:, None] - jnp.arange(maxp, dtype=jnp.int32)[None, :] * page, 0, page)
    qa = (
        jnp.pad(queries[0], ((0, 0), (0, LANES)))
        + jnp.pad(tables[0].astype(jnp.bfloat16), ((0, 0), (wide, LANES - maxp)))
        + jnp.pad(counts.astype(jnp.bfloat16), ((0, 0), (wide + maxp, LANES - 2 * maxp)))
    )
    asked = [
        lax.ppermute(qa, ("role", "group"), [(groups + i, (i + k) % groups) for i in range(groups)])
        for k in range(1, groups)
    ]
    part_shape = jax.ShapeDtypeStruct((heads * rows + 8, HD), jnp.float32)
    vmem = pl.BlockSpec(memory_space=pltpu.VMEM)
    hbm = pl.BlockSpec(memory_space=pltpu.HBM)
    page_shape = stored.shape[1:]
    chosen_count = groups * PARTS
    mine, chosen, entries = pl.pallas_call(
        functools.partial(first_kernel, held, per_held, groups),
        out_shape=[
            part_shape,
            jax.ShapeDtypeStruct((chosen_count,) + page_shape, jnp.bfloat16),
            jax.ShapeDtypeStruct((chosen_count, LANES), jnp.float32),
        ],
        in_specs=[vmem, vmem, hbm, hbm, hbm, hbm],
        out_specs=[vmem] * 3,
        scratch_shapes=[
            pltpu.VMEM((rows, maxp) + page_shape, jnp.bfloat16),
            pltpu.SMEM(send.shape, jnp.int32),
            pltpu.SMEM(wanted.shape, jnp.int32),
            pltpu.SMEM(tables.shape[1:], jnp.int32),
            pltpu.SMEM((chosen_count,), jnp.int32),
            pltpu.SMEM((chosen_count,), jnp.int32),
            pltpu.SemaphoreType.DMA((3,)),
            pltpu.SemaphoreType.DMA((chosen_count,)),
            pltpu.SemaphoreType.DMA((rows, maxp)),
        ],
        compiler_params=pltpu.CompilerParams(vmem_limit_bytes=24 * MIB),
        cost_estimate=pl.CostEstimate(flops=4 * 10**9, bytes_accessed=12 * MIB, transcendentals=10**6),
        name="resident",
    )(qa, new_kv[0], send, wanted, tables[0], stored)
    count = groups - 1
    theirs = pl.pallas_call(
        functools.partial(second_kernel, held, per_held, maxp, count),
        out_shape=[part_shape] * count,
        in_specs=[vmem] * (2 + count),
        out_specs=[vmem] * count,
        compiler_params=pltpu.CompilerParams(vmem_limit_bytes=16 * MIB),
        cost_estimate=pl.CostEstimate(flops=4 * 10**9, bytes_accessed=8 * MIB, transcendentals=10**6),
        name="owned",
    )(chosen, entries, *asked)
    parts = [mine, lax.ppermute(mine, "role", [(0, 1)])]
    for k in range(1, groups):
        parts.append(
            lax.ppermute(theirs[k - 1], ("role", "group"), [(i, groups + (i - k) % groups) for i in range(groups)])
        )
    attended = pl.pallas_call(
        functools.partial(merge_kernel, heads, rows),
        out_shape=jax.ShapeDtypeStruct((rows, wide), jnp.bfloat16),
        in_specs=[vmem] * len(parts),
        out_specs=vmem,
        compiler_params=pltpu.CompilerParams(vmem_limit_bytes=8 * MIB),
        name="merge",
    )(*parts)
    partner = lax.ppermute(attended, "role", [(1, 0)])
    share = out_weight.shape[1] // tps

    def project(steps, name):
        return pl.pallas_call(
            functools.partial(project_kernel, steps),
            out_shape=[jax.ShapeDtypeStruct((rows, share), jnp.float32)] * len(steps),
            in_specs=[vmem] * 3,
            out_specs=[vmem] * len(steps),
            compiler_params=pltpu.CompilerParams(vmem_limit_bytes=24 * MIB),
            cost_estimate=pl.CostEstimate(
                flops=len(steps) * 32 * wide * share, bytes_accessed=len(steps) * 2 * wide * share, transcendentals=0
            ),
            name=name,
        )(attended, partner, out_weight)

    steps = list(range(1, tps))
    sent = project(steps, "project")
    arrived = [lax.ppermute(part, "tp", [(i, (i + d) % tps) for i in range(tps)]) for d, part in zip(steps, sent)]
    total = functools.reduce(jnp.add, arrived, project([0], "project_own")[0])
    return total.astype(jnp.bfloat16)[None]


def solution(mesh):
    return jax.shard_map(
        per_device,
        mesh=mesh,
        in_specs=(
            P("role", "group", "tp", None, None, None),
            P(),
            P(),
            P("group", None),
            P("group", None, None),
            P("group", None, "tp"),
            P("group", None, "tp"),
            P("tp", "role"),
        ),
        out_specs=P("group", None, ("role", "tp")),
        check_vma=False,
    )
```

time: 277 us -> 60.1 us (0.22)
  waiting for transfers between devices: 175 us -> 6.32 us
  local copies, waits for them, and re-layouts: 62.8 us -> 6.14 us
  starting transfers between devices: 8.15 us -> 33 us
  between operations: 13.6 us -> 0.15 us
  Pallas kernels: 0 us -> 11.1 us
  other arithmetic: 10.7 us -> 2.87 us
  matrix products: 5.25 us -> 0 us
    all_to_all x1 -> x0, waiting for transfers between devices: 151 us -> none  [per_device(): lax.all_to_all(parcel, ('role', 'group'), split_axis=0, concat_axis=0, ti...]
    ppermute x1 -> x11, starting transfers between devices: 1.29 us -> 33 us  [the longest x1 19.5 us: per_device(): parts = [mine, lax.ppermute(mine, 'role', [(0, 1)])]]
    reduce_scatter x1 -> x0, waiting for transfers between devices: 22.1 us -> none  [per_device(): lax.psum_scatter(partial_value, 'tp', scatter_dimension=1, tiled=True)]
    gather x3 -> x0, local copies, waits for them, and re-layouts: 17.1 us -> none  [the longest x1 9.1 us: per_device(): gathered = page_pool[tables[0]].reshape(row_count, -1, held_count, 2 * HD)]
    reshape x1 -> x0, local copies, waits for them, and re-layouts: 12.5 us -> none  [per_device(): gathered = page_pool[tables[0]].reshape(row_count, -1, held_count, 2 * HD)]
    slice x5 -> x0, local copies, waits for them, and re-layouts: 12.4 us -> none  [the longest x1 8.3 us: per_device(): cache_keys = gathered[..., :HD]]
    pallas_call x0 -> x5, Pallas kernels: none -> 11.1 us  [the longest x1 6.76 us: per_device(): pl.pallas_call(functools.partial(first_kernel, held, per_held, groups), o...]
    scatter x3 -> x0, local copies, waits for them, and re-layouts: 10.3 us -> none  [the longest x1 5.2 us: per_device(): parcel = jnp.zeros((blocks * block_width,) + page_shape, stored.dtype).at...]
  transfers between devices with their start and end apart: 4 -> 11, of which waited for: 3 -> 5; matrix products, arithmetic and copies ran while one was open for 8% -> 0% of each run, Pallas kernels for 0% -> 15%
where the time goes in v2:
time: 60.1 us; the launch traced here: 59.6 us
  starting transfers between devices  33 us (55%)
  Pallas kernels  11.1 us (18%)
  waiting for transfers between devices  6.32 us (11%)
  local copies, waits for them, and re-layouts  6.14 us (10%)
  other arithmetic  2.87 us (5%)
    ppermute x1, starting transfers between devices, per_device(): parts = [mine, lax.ppermute(mine, 'role', [(0, 1)])]  19.5 us
    pallas_call x1, Pallas kernels, per_device(): pl.pallas_call(functools.partial(first_kernel, held, per_held, groups), o...  6.76 us
    unnamed x12, local copies, waits for them, and re-layouts  6.14 us
    ppermute x3, starting transfers between devices, per_device(): lax.ppermute(part, 'tp', [(i, (i + d) % tps) for i in range(tps)])  4.46 us
    ppermute x3, starting transfers between devices, per_device(): lax.ppermute(theirs[k - 1], ('role', 'group'), [(i, groups + (i - k) % gr...  3.88 us
    ppermute x3, starting transfers between devices, per_device(): lax.ppermute(qa, ('role', 'group'), [(groups + i, (i + k) % groups) for i...  3.86 us
    ppermute x1, waiting for transfers between devices, per_device(): partner = lax.ppermute(attended, 'role', [(1, 0)])  2.57 us
    pallas_call x2, Pallas kernels, project(): pl.pallas_call(functools.partial(project_kernel, steps), out_shape=[jax.S...  2.37 us
  transfers between devices with their start and end apart: 11, of which 5 were waited for; matrix products, arithmetic and copies ran while one was open for 0% of the time, Pallas kernels for 15%

profile of v2, /device:TPU:0, one launch (start us, length us, event | category | flops | bytes accessed | tf_op | source)
XLA Modules:
  0.0 59.6 jit_solution(11606418466756214437)
XLA Ops:
  0.0 0.7 %bitcast_convert_fusion = bf16[8,8]{1,0:T(8,128)(2,1)S(1)} fusion(s32[1,8,8]{2,1,0:T(8,128)} %param.12), kind=kLoop, calls=%fused_computation.5 | loop fusion | flops 64 | bytes 384 | tf_op jit(solution)/shard_map/convert_element_type | solution.py:243
  0.7 0.7 %clamp_convert_fusion = bf16[8,8]{1,0:T(8,128)(2,1)S(1)} fusion(s32[8]{0:T(128)S(1)} %iota_multiply_fusion, s32[8]{0:T(128)} %bitcast.14), kind=kLoop, calls=%fused_computation.3 | loop fusion | flops 192 | bytes 192 | tf_op jit(solution)/shard_map/convert_element_type | solution.py:244
  1.4 0.8 %pad_add_fusion.qa = bf16[8,2176]{1,0:T(8,128)(2,1)S(1)} fusion(bf16[8,8]{1,0:T(8,128)(2,1)S(1)} %clamp_convert_fusion, bf16[8,8]{1,0:T(8,128)(2,1)S(1)} %bitcast_convert_fusion, bf16[8,2048]{1,0:T(8,128)(2,1)} %bitcast.13), kind=kLoop, calls=%fused_computation | loop fusion | flops 104448 | bytes 67840 | tf_op jit(solution)/shard_map/add | solution.py:242
  2.3 1.3 %collective-permute-start.3 = (bf16[8,2176]{1,0:T(8,128)(2,1)S(1)}, bf16[8,2176]{1,0:T(8,128)(2,1)S(1)}, u32[]{:S(2)}, u32[]{:S(2)}) collective-permute-start(bf16[8,2176]{1,0:T(8,128)(2,1)S(1)} %pad_add_fusion.qa), channel_id=1, source_target_pairs={{16,12},{20,0},{24,4},{28,8},{17,13},{21,1},{25,5},{29,9},{18,14},... | collective-permute-start | bytes 104456 | tf_op jit(solution)/shard_map/ppermute | solution.py:247
  3.5 1.3 %collective-permute-start.2 = (bf16[8,2176]{1,0:T(8,128)(2,1)S(1)}, bf16[8,2176]{1,0:T(8,128)(2,1)S(1)}, u32[]{:S(2)}, u32[]{:S(2)}) collective-permute-start(bf16[8,2176]{1,0:T(8,128)(2,1)S(1)} %pad_add_fusion.qa), channel_id=1, source_target_pairs={{16,8},{20,12},{24,0},{28,4},{17,9},{21,13},{25,1},{29,5},{18,10},... | collective-permute-start | bytes 104456 | tf_op jit(solution)/shard_map/ppermute | solution.py:247
  4.8 1.3 %collective-permute-start.1 = (bf16[8,2176]{1,0:T(8,128)(2,1)S(1)}, bf16[8,2176]{1,0:T(8,128)(2,1)S(1)}, u32[]{:S(2)}, u32[]{:S(2)}) collective-permute-start(bf16[8,2176]{1,0:T(8,128)(2,1)S(1)} %pad_add_fusion.qa), channel_id=1, source_target_pairs={{16,4},{20,8},{24,12},{28,0},{17,5},{21,9},{25,13},{29,1},{18,6},{... | collective-permute-start | bytes 104456 | tf_op jit(solution)/shard_map/ppermute | solution.py:247
  6.8 3.4 %copy-done.2 = bf16[1,1,1,64,128,512]{5,4,3,2,1,0:T(8,128)(2,1)S(1)} copy-done((bf16[1,1,1,64,128,512]{5,4,3,2,1,0:T(8,128)(2,1)S(1)}, bf16[1,1,1,64,128,512]{5,4,3,2,1,0:T(8,128)(2,1)}, u32[]{:S(2)}) %copy-start.2) | copy-done | bytes 8388632
  10.2 0.7 %copy-done.3 = bf16[1,8,512]{2,1,0:T(8,128)(2,1)S(1)} copy-done((bf16[1,8,512]{2,1,0:T(8,128)(2,1)S(1)}, bf16[1,8,512]{2,1,0:T(8,128)(2,1)}, u32[]{:S(2)}) %copy-start.3) | copy-done | bytes 8216
  10.9 0.7 %copy-done.4 = s32[4,12,3]{1,0,2:T(4,128)S(1)} copy-done((s32[4,12,3]{1,0,2:T(4,128)S(1)}, s32[4,12,3]{1,0,2:T(4,128)}, u32[]{:S(2)}) %copy-start.4) | copy-done | bytes 600
  11.6 0.7 %copy-done.5 = s32[4,6]{1,0:T(4,128)S(1)} copy-done((s32[4,6]{1,0:T(4,128)S(1)}, s32[4,6]{1,0:T(4,128)}, u32[]{:S(2)}) %copy-start.5) | copy-done | bytes 120
  12.3 6.8 %resident.1 = (f32[136,128]{1,0:T(8,128)S(1)}, bf16[24,128,512]{2,1,0:T(8,128)(2,1)S(1)}, f32[24,128]{1,0:T(8,128)S(1)}) custom-call(bf16[8,2176]{1,0:T(8,128)(2,1)S(1)} %pad_add_fusion.qa, bf16[8,512]{1,0:T(8,128)(2,1)S(1)} %bitcast.11, s32[3,4,12]{2,1,0:T(4,128)S(1)} %bitcast.12, s32[4,6]{1,0:T(4,128)S(1)} %copy-done.5, s32[8,8]{1,0:T(8,128)S(1)} %bitcast.9, ...), custom_call_target="tpu_custom_call" | custom-call | flops 4000000000 | bytes 12582912 | tf_op jit(solution)/shard_map/resident/pallas_call | solution.py:255
  19.1 19.5 %collective-permute-start = (f32[136,128]{1,0:T(8,128)S(1)}, f32[136,128]{1,0:T(8,128)S(1)}, u32[]{:S(2)}, u32[]{:S(2)}) collective-permute-start(f32[136,128]{1,0:T(8,128)S(1)} %get-tuple-element.14.refs_0_), channel_id=1, source_target_pairs={{0,16},{1,17},{2,18},{3,19},{4,20},{5,21},{6,22},{7,23},{8,24},{9,... | collective-permute-start | bytes 208904 | tf_op jit(solution)/shard_map/ppermute | solution.py:289
  38.6 1.7 %owned.1 = (f32[136,128]{1,0:T(8,128)S(1)}, f32[136,128]{1,0:T(8,128)S(1)}, f32[136,128]{1,0:T(8,128)S(1)}) custom-call(bf16[24,128,512]{2,1,0:T(8,128)(2,1)S(1)} %get-tuple-element.15.chosen, f32[24,128]{1,0:T(8,128)S(1)} %get-tuple-element.16.entries, bf16[8,2176]{1,0:T(8,128)(2,1)S(1)} %collective-permute-done.1.refs_0_, ...), custom_call_target="tpu_custom_call" | custom-call | flops 4000000000 | bytes 8388608 | tf_op jit(solution)/shard_map/owned/pallas_call | solution.py:280
  40.3 1.3 %collective-permute-start.4 = (f32[136,128]{1,0:T(8,128)S(1)}, f32[136,128]{1,0:T(8,128)S(1)}, u32[]{:S(2)}, u32[]{:S(2)}) collective-permute-start(f32[136,128]{1,0:T(8,128)S(1)} %get-tuple-element.17), channel_id=1, source_target_pairs={{0,28},{4,16},{8,20},{12,24},{1,29},{5,17},{9,21},{13,25},{2,30},{... | collective-permute-start | bytes 208904 | tf_op jit(solution)/shard_map/ppermute | solution.py:292
  41.6 1.3 %collective-permute-start.5 = (f32[136,128]{1,0:T(8,128)S(1)}, f32[136,128]{1,0:T(8,128)S(1)}, u32[]{:S(2)}, u32[]{:S(2)}) collective-permute-start(f32[136,128]{1,0:T(8,128)S(1)} %get-tuple-element.18), channel_id=1, source_target_pairs={{0,24},{4,28},{8,16},{12,20},{1,25},{5,29},{9,17},{13,21},{2,26},{... | collective-permute-start | bytes 208904 | tf_op jit(solution)/shard_map/ppermute | solution.py:292
  42.9 1.3 %collective-permute-start.6 = (f32[136,128]{1,0:T(8,128)S(1)}, f32[136,128]{1,0:T(8,128)S(1)}, u32[]{:S(2)}, u32[]{:S(2)}) collective-permute-start(f32[136,128]{1,0:T(8,128)S(1)} %get-tuple-element.19), channel_id=1, source_target_pairs={{0,20},{4,24},{8,28},{12,16},{1,21},{5,25},{9,29},{13,17},{2,22},{... | collective-permute-start | bytes 208904 | tf_op jit(solution)/shard_map/ppermute | solution.py:292
  44.8 1.3 %collective-permute-done.6.refs_4_ = f32[136,128]{1,0:T(8,128)S(1)} collective-permute-done((f32[136,128]{1,0:T(8,128)S(1)}, f32[136,128]{1,0:T(8,128)S(1)}, u32[]{:S(2)}, u32[]{:S(2)}) %collective-permute-start.6) | collective-permute-done | bytes 69664 | tf_op jit(solution)/shard_map/ppermute | solution.py:292
  46.4 1.3 %collective-permute-start.7 = (bf16[8,2048]{1,0:T(8,128)(2,1)S(1)}, bf16[8,2048]{1,0:T(8,128)(2,1)S(1)}, u32[]{:S(2)}, u32[]{:S(2)}) collective-permute-start(bf16[8,2048]{1,0:T(8,128)(2,1)S(1)} %merge.1.attended), channel_id=1, source_target_pairs={{16,0},{17,1},{18,2},{19,3},{20,4},{21,5},{22,6},{23,7},{24,8},{25... | collective-permute-start | bytes 98312 | tf_op jit(solution)/shard_map/ppermute | solution.py:302
  47.7 2.6 %collective-permute-done.7.partner = bf16[8,2048]{1,0:T(8,128)(2,1)S(1)} collective-permute-done((bf16[8,2048]{1,0:T(8,128)(2,1)S(1)}, bf16[8,2048]{1,0:T(8,128)(2,1)S(1)}, u32[]{:S(2)}, u32[]{:S(2)}) %collective-permute-start.7) | collective-permute-done | bytes 32800 | tf_op jit(solution)/shard_map/ppermute | solution.py:302
  50.3 1.7 %project.1 = (f32[8,1024]{1,0:T(8,128)S(1)}, f32[8,1024]{1,0:T(8,128)S(1)}, f32[8,1024]{1,0:T(8,128)S(1)}) custom-call(bf16[8,2048]{1,0:T(8,128)(2,1)S(1)} %merge.1.attended, bf16[8,2048]{1,0:T(8,128)(2,1)S(1)} %collective-permute-done.7.partner, bf16[2048,4096]{1,0:T(8,128)(2,1)S(1)} %copy-done), custom_call_target="tpu_custom_call" | custom-call | flops 201326592 | bytes 12582912 | tf_op jit(solution)/shard_map/project/pallas_call | solution.py:306
  52.0 1.5 %collective-permute-start.8 = (f32[8,1024]{1,0:T(8,128)S(1)}, f32[8,1024]{1,0:T(8,128)S(1)}, u32[]{:S(2)}, u32[]{:S(2)}) collective-permute-start(f32[8,1024]{1,0:T(8,128)S(1)} %get-tuple-element.20), channel_id=1, source_target_pairs={{0,1},{1,2},{2,3},{3,0},{4,5},{5,6},{6,7},{7,4},{8,9},{9,10},{10,1... | collective-permute-start | bytes 98312 | tf_op jit(solution)/shard_map/ppermute | solution.py:320
  53.5 1.5 %collective-permute-start.9 = (f32[8,1024]{1,0:T(8,128)S(1)}, f32[8,1024]{1,0:T(8,128)S(1)}, u32[]{:S(2)}, u32[]{:S(2)}) collective-permute-start(f32[8,1024]{1,0:T(8,128)S(1)} %get-tuple-element.21), channel_id=1, source_target_pairs={{0,2},{1,3},{2,0},{3,1},{4,6},{5,7},{6,4},{7,5},{8,10},{9,11},{10,... | collective-permute-start | bytes 98312 | tf_op jit(solution)/shard_map/ppermute | solution.py:320
  55.0 1.4 %collective-permute-start.10 = (f32[8,1024]{1,0:T(8,128)S(1)}, f32[8,1024]{1,0:T(8,128)S(1)}, u32[]{:S(2)}, u32[]{:S(2)}) collective-permute-start(f32[8,1024]{1,0:T(8,128)S(1)} %get-tuple-element.22), channel_id=1, source_target_pairs={{0,3},{1,0},{2,1},{3,2},{4,7},{5,4},{6,5},{7,6},{8,11},{9,8},{10,9... | collective-permute-start | bytes 98312 | tf_op jit(solution)/shard_map/ppermute | solution.py:320
  57.4 1.5 %collective-permute-done.10 = f32[8,1024]{1,0:T(8,128)S(1)} collective-permute-done((f32[8,1024]{1,0:T(8,128)S(1)}, f32[8,1024]{1,0:T(8,128)S(1)}, u32[]{:S(2)}, u32[]{:S(2)}) %collective-permute-start.10) | collective-permute-done | bytes 32800 | tf_op jit(solution)/shard_map/ppermute | solution.py:320
  (20 shorter events, 3.2 us)
Async XLA Ops:
  2.3 36.3 %collective-permute-start.3 = (bf16[8,2176]{1,0:T(8,128)(2,1)S(1)}, bf16[8,2176]{1,0:T(8,128)(2,1)S(1)}, u32[]{:S(2)}, u32[]{:S(2)}) collective-permute-start(bf16[8,2176]{1,0:T(8,128)(2,1)S(1)} %pad_add_fusion.qa), channel_id=1, source_target_pairs={{16,12},{20,0},{24,4},{28,8},{17,13},{21,1},{25,5},{29,9},{18,14},... | collective-permute-start | bytes 104456 | tf_op jit(solution)/shard_map/ppermute | solution.py:247
  3.5 35.0 %collective-permute-start.2 = (bf16[8,2176]{1,0:T(8,128)(2,1)S(1)}, bf16[8,2176]{1,0:T(8,128)(2,1)S(1)}, u32[]{:S(2)}, u32[]{:S(2)}) collective-permute-start(bf16[8,2176]{1,0:T(8,128)(2,1)S(1)} %pad_add_fusion.qa), channel_id=1, source_target_pairs={{16,8},{20,12},{24,0},{28,4},{17,9},{21,13},{25,1},{29,5},{18,10},... | collective-permute-start | bytes 104456 | tf_op jit(solution)/shard_map/ppermute | solution.py:247
  4.8 33.7 %collective-permute-start.1 = (bf16[8,2176]{1,0:T(8,128)(2,1)S(1)}, bf16[8,2176]{1,0:T(8,128)(2,1)S(1)}, u32[]{:S(2)}, u32[]{:S(2)}) collective-permute-start(bf16[8,2176]{1,0:T(8,128)(2,1)S(1)} %pad_add_fusion.qa), channel_id=1, source_target_pairs={{16,4},{20,8},{24,12},{28,0},{17,5},{21,9},{25,13},{29,1},{18,6},{... | collective-permute-start | bytes 104456 | tf_op jit(solution)/shard_map/ppermute | solution.py:247
  6.1 0.7 %copy-start.1 = (s32[1,8,8]{2,1,0:T(8,128)S(1)}, s32[1,8,8]{2,1,0:T(8,128)}, u32[]{:S(2)}) copy-start(s32[1,8,8]{2,1,0:T(8,128)} %param.12) | copy-start | bytes 772
  6.8 3.4 %copy-start.2 = (bf16[1,1,1,64,128,512]{5,4,3,2,1,0:T(8,128)(2,1)S(1)}, bf16[1,1,1,64,128,512]{5,4,3,2,1,0:T(8,128)(2,1)}, u32[]{:S(2)}) copy-start(bf16[1,1,1,64,128,512]{5,4,3,2,1,0:T(8,128)(2,1)} %param.8) | copy-start | bytes 25165828
  10.2 0.7 %copy-start.3 = (bf16[1,8,512]{2,1,0:T(8,128)(2,1)S(1)}, bf16[1,8,512]{2,1,0:T(8,128)(2,1)}, u32[]{:S(2)}) copy-start(bf16[1,8,512]{2,1,0:T(8,128)(2,1)} %param.14) | copy-start | bytes 24580
  10.9 0.7 %copy-start.4 = (s32[4,12,3]{1,0,2:T(4,128)S(1)}, s32[4,12,3]{1,0,2:T(4,128)}, u32[]{:S(2)}) copy-start(s32[4,12,3]{1,0,2:T(4,128)} %param.9) | copy-start | bytes 1732
  11.6 0.7 %copy-start.5 = (s32[4,6]{1,0:T(4,128)S(1)}, s32[4,6]{1,0:T(4,128)}, u32[]{:S(2)}) copy-start(s32[4,6]{1,0:T(4,128)} %wanted_hbm.1) | copy-start | bytes 292
  12.3 38.0 %copy-start = (bf16[2048,4096]{1,0:T(8,128)(2,1)S(1)}, bf16[2048,4096]{1,0:T(8,128)(2,1)}, u32[]{:S(2)}) copy-start(bf16[2048,4096]{1,0:T(8,128)(2,1)} %weight.3) | copy-start | bytes 50331652
  19.1 25.1 %collective-permute-start = (f32[136,128]{1,0:T(8,128)S(1)}, f32[136,128]{1,0:T(8,128)S(1)}, u32[]{:S(2)}, u32[]{:S(2)}) collective-permute-start(f32[136,128]{1,0:T(8,128)S(1)} %get-tuple-element.14.refs_0_), channel_id=1, source_target_pairs={{0,16},{1,17},{2,18},{3,19},{4,20},{5,21},{6,22},{7,23},{8,24},{9,... | collective-permute-start | bytes 208904 | tf_op jit(solution)/shard_map/ppermute | solution.py:289
  40.3 3.9 %collective-permute-start.4 = (f32[136,128]{1,0:T(8,128)S(1)}, f32[136,128]{1,0:T(8,128)S(1)}, u32[]{:S(2)}, u32[]{:S(2)}) collective-permute-start(f32[136,128]{1,0:T(8,128)S(1)} %get-tuple-element.17), channel_id=1, source_target_pairs={{0,28},{4,16},{8,20},{12,24},{1,29},{5,17},{9,21},{13,25},{2,30},{... | collective-permute-start | bytes 208904 | tf_op jit(solution)/shard_map/ppermute | solution.py:292
  41.6 3.2 %collective-permute-start.5 = (f32[136,128]{1,0:T(8,128)S(1)}, f32[136,128]{1,0:T(8,128)S(1)}, u32[]{:S(2)}, u32[]{:S(2)}) collective-permute-start(f32[136,128]{1,0:T(8,128)S(1)} %get-tuple-element.18), channel_id=1, source_target_pairs={{0,24},{4,28},{8,16},{12,20},{1,25},{5,29},{9,17},{13,21},{2,26},{... | collective-permute-start | bytes 208904 | tf_op jit(solution)/shard_map/ppermute | solution.py:292
  42.9 3.2 %collective-permute-start.6 = (f32[136,128]{1,0:T(8,128)S(1)}, f32[136,128]{1,0:T(8,128)S(1)}, u32[]{:S(2)}, u32[]{:S(2)}) collective-permute-start(f32[136,128]{1,0:T(8,128)S(1)} %get-tuple-element.19), channel_id=1, source_target_pairs={{0,20},{4,24},{8,28},{12,16},{1,21},{5,25},{9,29},{13,17},{2,22},{... | collective-permute-start | bytes 208904 | tf_op jit(solution)/shard_map/ppermute | solution.py:292
  46.4 3.9 %collective-permute-start.7 = (bf16[8,2048]{1,0:T(8,128)(2,1)S(1)}, bf16[8,2048]{1,0:T(8,128)(2,1)S(1)}, u32[]{:S(2)}, u32[]{:S(2)}) collective-permute-start(bf16[8,2048]{1,0:T(8,128)(2,1)S(1)} %merge.1.attended), channel_id=1, source_target_pairs={{16,0},{17,1},{18,2},{19,3},{20,4},{21,5},{22,6},{23,7},{24,8},{25... | collective-permute-start | bytes 98312 | tf_op jit(solution)/shard_map/ppermute | solution.py:302
  52.0 5.1 %collective-permute-start.8 = (f32[8,1024]{1,0:T(8,128)S(1)}, f32[8,1024]{1,0:T(8,128)S(1)}, u32[]{:S(2)}, u32[]{:S(2)}) collective-permute-start(f32[8,1024]{1,0:T(8,128)S(1)} %get-tuple-element.20), channel_id=1, source_target_pairs={{0,1},{1,2},{2,3},{3,0},{4,5},{5,6},{6,7},{7,4},{8,9},{9,10},{10,1... | collective-permute-start | bytes 98312 | tf_op jit(solution)/shard_map/ppermute | solution.py:320
  53.5 3.9 %collective-permute-start.9 = (f32[8,1024]{1,0:T(8,128)S(1)}, f32[8,1024]{1,0:T(8,128)S(1)}, u32[]{:S(2)}, u32[]{:S(2)}) collective-permute-start(f32[8,1024]{1,0:T(8,128)S(1)} %get-tuple-element.21), channel_id=1, source_target_pairs={{0,2},{1,3},{2,0},{3,1},{4,6},{5,7},{6,4},{7,5},{8,10},{9,11},{10,... | collective-permute-start | bytes 98312 | tf_op jit(solution)/shard_map/ppermute | solution.py:320
  55.0 3.9 %collective-permute-start.10 = (f32[8,1024]{1,0:T(8,128)S(1)}, f32[8,1024]{1,0:T(8,128)S(1)}, u32[]{:S(2)}, u32[]{:S(2)}) collective-permute-start(f32[8,1024]{1,0:T(8,128)S(1)} %get-tuple-element.22), channel_id=1, source_target_pairs={{0,3},{1,0},{2,1},{3,2},{4,7},{5,4},{6,5},{7,6},{8,11},{9,8},{10,9... | collective-permute-start | bytes 98312 | tf_op jit(solution)/shard_map/ppermute | solution.py:320

commit v3 on v2

--- a/solution.py
+++ b/solution.py
@@ -14,6 +14,7 @@
 CAPP = 2
 PRE_DEV = 8
 LANES = 128
+PAGE = 128
 NEG = -1e30
 SCALE = 1.0 / math.sqrt(HD)
 PARTS = CAP + CAPP
@@ -37,10 +38,16 @@
 
 
 def entry_rows(qa, held, per_held, maxp):
+    rows = qa.shape[0]
     wide = held * per_held * HD
     aux = qa[:, wide : wide + LANES].astype(jnp.float32)
-    turned = jnp.concatenate([aux] * (held * per_held), 0).T
-    return turned[:maxp], turned[maxp : 2 * maxp]
+    lane = lax.broadcasted_iota(jnp.int32, (rows, LANES), 1) - maxp
+    row = lax.broadcasted_iota(jnp.int32, (rows, LANES), 0)
+    parts = jnp.where(lane == row, 8.0 * aux[:1], jnp.where(lane == row + rows, aux[:1], 0.0))
+    length = jnp.sum(parts, 1, keepdims=True)
+    turned = jnp.concatenate([jnp.where(lane == 0, length, aux)] * (held * per_held), 0).T
+    first = lax.broadcasted_iota(jnp.int32, (maxp, 1), 0).astype(jnp.float32) * PAGE
+    return turned[:maxp], jnp.clip(turned[maxp : maxp + 1] - first, 0.0, PAGE)
 
 
 def lanes_of(page, first, held):
@@ -60,7 +67,7 @@
     q = query_block(qa, held, per_held)
     tab, cnt = entry_rows(qa, held, per_held, maxp)
     count = q.shape[0]
-    token = lax.broadcasted_iota(jnp.int32, (LANES, count), 0).astype(jnp.float32)
+    token = lax.broadcasted_iota(jnp.int32, (PAGE, count), 0).astype(jnp.float32)
     masks = []
     for c in range(PARTS):
         valid = jnp.sum(jnp.where(tab == entries[c : c + 1, :count], cnt, 0.0), 0, keepdims=True)
@@ -76,9 +83,8 @@
     write_part(out, acc, top, total, held, per_held)
 
 
-def resident_part(qa, new_kv, send, tables, group, kv, pages, sems, out, held, per_held):
+def resident_part(qa, fresh_at, send, tables, maxp, group, kv, pages, sems, out, held, per_held):
     rows = qa.shape[0]
-    maxp = tables.shape[1]
     slots = kv.shape[0]
     copies = []
     for r in range(rows):
@@ -98,8 +104,8 @@
             gone = jnp.logical_or(gone, tab == slot.astype(jnp.float32))
     cnt = jnp.where(gone, 0.0, cnt)
     lane_row = lax.rem(lax.broadcasted_iota(jnp.int32, (1, count), 1), rows)
-    token = lax.broadcasted_iota(jnp.int32, (LANES, count), 0).astype(jnp.float32)
-    fresh = new_kv[...].astype(jnp.float32)
+    token = lax.broadcasted_iota(jnp.int32, (PAGE, count), 0).astype(jnp.float32)
+    fresh = qa[:, fresh_at : fresh_at + 2 * held * HD].astype(jnp.float32)
     fresh = jnp.concatenate([fresh, jnp.zeros_like(fresh)], 0).astype(jnp.bfloat16)
     own_mask = lax.broadcasted_iota(jnp.int32, (2 * rows, count), 0) == lane_row
     own = dot(lanes_of(fresh, 0, held), q, 1, 1) * SCALE
@@ -152,18 +158,16 @@
         at = at + hit.astype(jnp.int32)
 
 
-def first_kernel(held, per_held, groups, qa, new_kv, send_hbm, wanted_hbm, tables_hbm, kv, *refs):
-    out, chosen, entries, pages, send, wanted, tables, page_list, slot_list, int_sems, chosen_sems, sems = refs
+def first_kernel(held, per_held, groups, maxp, qa, send_hbm, wanted_hbm, tables_hbm, kv, *refs):
+    out, chosen, entries, pages, send, wanted, tables, page_list, slot_list, list_sems, chosen_sems, sems = refs
     group = lax.axis_index("group")
     prefill = lax.axis_index("role") == 0
-    maxp = tables.shape[1]
-    ints = [
-        pltpu.make_async_copy(a, b, int_sems.at[i])
-        for i, (a, b) in enumerate(((send_hbm, send), (wanted_hbm, wanted), (tables_hbm, tables)))
-    ]
-    for copy in ints:
+    fresh_at = held * per_held * HD + LANES
+    lists = ((send_hbm, send), (wanted_hbm, wanted), (tables_hbm, tables))
+    copies = [pltpu.make_async_copy(a, b, list_sems.at[i]) for i, (a, b) in enumerate(lists)]
+    for copy in copies:
         copy.start()
-    for copy in ints:
+    for copy in copies:
         copy.wait()
 
     @pl.when(prefill)
@@ -187,7 +191,7 @@
 
     @pl.when(jnp.logical_not(prefill))
     def _():
-        resident_part(qa, new_kv, send, tables, group, kv, pages, sems, out, held, per_held)
+        resident_part(qa, fresh_at, send, tables, maxp, group, kv, pages, sems, out, held, per_held)
 
 
 def second_kernel(held, per_held, maxp, count, chosen, entries, *refs):
@@ -229,7 +233,7 @@
 
 def per_device(kv_pages, send_list, wanted, lengths, tables, queries, new_kv, out_weight):
     stored = kv_pages[0, 0, 0]
-    slots, page = stored.shape[0], stored.shape[1]
+    slots = stored.shape[0]
     groups, tps = lax.axis_size("group"), lax.axis_size("tp")
     held = max(1, KVH // tps)
     rows, wide = queries.shape[1], queries.shape[2]
@@ -237,12 +241,16 @@
     per_held = heads // held
     maxp = tables.shape[2]
     send = jnp.transpose(send_list, (2, 0, 1))
-    counts = jnp.clip(lengths[0][:, None] - jnp.arange(maxp, dtype=jnp.int32)[None, :] * page, 0, page)
-    qa = (
-        jnp.pad(queries[0], ((0, 0), (0, LANES)))
-        + jnp.pad(tables[0].astype(jnp.bfloat16), ((0, 0), (wide, LANES - maxp)))
-        + jnp.pad(counts.astype(jnp.bfloat16), ((0, 0), (wide + maxp, LANES - 2 * maxp)))
-    )
+    fresh_at = wide + LANES
+    width = fresh_at + new_kv.shape[2]
+
+    def place(block, at):
+        return jnp.pad(block, ((0, rows - block.shape[0]), (at, width - at - block.shape[1])))
+
+    high = lax.shift_right_logical(place(lengths, wide + maxp), 3)
+    low = jnp.bitwise_and(place(lengths, wide + maxp + rows), 7)
+    integers = place(tables[0], wide) + high + low
+    qa = place(queries[0], 0) + place(new_kv[0], fresh_at) + integers.astype(jnp.bfloat16)
     asked = [
         lax.ppermute(qa, ("role", "group"), [(groups + i, (i + k) % groups) for i in range(groups)])
         for k in range(1, groups)
@@ -253,13 +261,13 @@
     page_shape = stored.shape[1:]
     chosen_count = groups * PARTS
     mine, chosen, entries = pl.pallas_call(
-        functools.partial(first_kernel, held, per_held, groups),
+        functools.partial(first_kernel, held, per_held, groups, maxp),
         out_shape=[
             part_shape,
             jax.ShapeDtypeStruct((chosen_count,) + page_shape, jnp.bfloat16),
             jax.ShapeDtypeStruct((chosen_count, LANES), jnp.float32),
         ],
-        in_specs=[vmem, vmem, hbm, hbm, hbm, hbm],
+        in_specs=[vmem, hbm, hbm, hbm, hbm],
         out_specs=[vmem] * 3,
         scratch_shapes=[
             pltpu.VMEM((rows, maxp) + page_shape, jnp.bfloat16),
@@ -275,7 +283,7 @@
         compiler_params=pltpu.CompilerParams(vmem_limit_bytes=24 * MIB),
         cost_estimate=pl.CostEstimate(flops=4 * 10**9, bytes_accessed=12 * MIB, transcendentals=10**6),
         name="resident",
-    )(qa, new_kv[0], send, wanted, tables[0], stored)
+    )(qa, *[pltpu.with_memory_space_constraint(x, pltpu.HBM) for x in (send, wanted, tables[0], stored)])
     count = groups - 1
     theirs = pl.pallas_call(
         functools.partial(second_kernel, held, per_held, maxp, count),
@@ -286,6 +294,7 @@
         cost_estimate=pl.CostEstimate(flops=4 * 10**9, bytes_accessed=8 * MIB, transcendentals=10**6),
         name="owned",
     )(chosen, entries, *asked)
+    mine, theirs = lax.optimization_barrier((mine, theirs))
     parts = [mine, lax.ppermute(mine, "role", [(0, 1)])]
     for k in range(1, groups):
         parts.append(

time: 60.1 us -> 42.2 us (0.70)
  starting transfers between devices: 33 us -> 21.9 us
  local copies, waits for them, and re-layouts: 6.14 us -> 0.01 us
  waiting for transfers between devices: 6.32 us -> 9.39 us
  Pallas kernels: 11.1 us -> 8.6 us
  other arithmetic: 2.87 us -> 1.52 us
    ppermute x1, starting transfers between devices: 19.5 us -> 1.29 us  [per_device(): parts = [mine, lax.ppermute(mine, 'role', [(0, 1)])]]
    ppermute x3, starting transfers between devices: 3.88 us -> 11 us  [per_device(): lax.ppermute(theirs[k - 1], ('role', 'group'), [(i, groups + (i - k) % gr...]
    unnamed x12 -> x2, local copies, waits for them, and re-layouts: 6.14 us -> 0.01 us
    ppermute x3, waiting for transfers between devices: 0.01 us -> 3.23 us  [per_device(): lax.ppermute(qa, ('role', 'group'), [(groups + i, (i + k) % groups) for i...]
    pallas_call x1, Pallas kernels: 6.76 us -> 4.25 us  [per_device(): pl.pallas_call(functools.partial(first_kernel, held, per_held, groups, ma...]
    convert_element_type x2 -> x0, other arithmetic: 1.42 us -> none  [the longest x1 0.73 us: per_device(): counts.astype(jnp.bfloat16)]
    ppermute x3, waiting for transfers between devices: 1.9 us -> 0.61 us  [per_device(): lax.ppermute(theirs[k - 1], ('role', 'group'), [(i, groups + (i - k) % gr...]
    ppermute x1, waiting for transfers between devices: 2.57 us -> 3.45 us  [per_device(): partner = lax.ppermute(attended, 'role', [(1, 0)])]
  transfers between devices with their start and end apart: 11 -> 11, of which waited for: 5 -> 7; matrix products, arithmetic and copies ran while one was open for 0% -> 0% of each run, Pallas kernels for 15% -> 12%
where the time goes in v3:
time: 42.2 us; the launch traced here: 41.5 us
  starting transfers between devices  21.9 us (52%)
  waiting for transfers between devices  9.39 us (22%)
  Pallas kernels  8.6 us (20%)
  other arithmetic  1.52 us (4%)
    ppermute x3, starting transfers between devices, per_device(): lax.ppermute(theirs[k - 1], ('role', 'group'), [(i, groups + (i - k) % gr...  11 us
    ppermute x3, starting transfers between devices, per_device(): lax.ppermute(part, 'tp', [(i, (i + d) % tps) for i in range(tps)])  4.46 us
    pallas_call x1, Pallas kernels, per_device(): pl.pallas_call(functools.partial(first_kernel, held, per_held, groups, ma...  4.25 us
    ppermute x3, starting transfers between devices, per_device(): lax.ppermute(qa, ('role', 'group'), [(groups + i, (i + k) % groups) for i...  3.87 us
    ppermute x1, waiting for transfers between devices, per_device(): partner = lax.ppermute(attended, 'role', [(1, 0)])  3.45 us
    ppermute x3, waiting for transfers between devices, per_device(): lax.ppermute(qa, ('role', 'group'), [(groups + i, (i + k) % groups) for i...  3.23 us
    pallas_call x2, Pallas kernels, project(): pl.pallas_call(functools.partial(project_kernel, steps), out_shape=[jax.S...  2.37 us
    ppermute x3, waiting for transfers between devices, per_device(): lax.ppermute(part, 'tp', [(i, (i + d) % tps) for i in range(tps)])  1.84 us
  transfers between devices with their start and end apart: 11, of which 7 were waited for; matrix products, arithmetic and copies ran while one was open for 0% of the time, Pallas kernels for 12%

profile of v3, /device:TPU:0, one launch (start us, length us, event | category | flops | bytes accessed | tf_op | source)
XLA Modules:
  0.0 41.5 jit_solution(10186618404333362738)
XLA Ops:
  0.0 0.9 %fusion.qa = bf16[8,2688]{1,0:T(8,128)(2,1)S(1)} fusion(s32[1,8]{1,0:T(1,128)} %param.11, s32[8,8]{1,0:T(8,128)} %bitcast.9, bf16[8,512]{1,0:T(8,128)(2,1)} %bitcast.8, bf16[8,2048]{1,0:T(8,128)(2,1)} %bitcast.7), kind=kLoop, calls=%fused_computation.1 | loop fusion | flops 236544 | bytes 84256 | tf_op jit(solution)/shard_map/add | solution.py:253
  0.9 1.3 %collective-permute-start.2 = (bf16[8,2688]{1,0:T(8,128)(2,1)S(1)}, bf16[8,2688]{1,0:T(8,128)(2,1)S(1)}, u32[]{:S(2)}, u32[]{:S(2)}) collective-permute-start(bf16[8,2688]{1,0:T(8,128)(2,1)S(1)} %fusion.qa), channel_id=1, source_target_pairs={{16,12},{20,0},{24,4},{28,8},{17,13},{21,1},{25,5},{29,9},{18,14},... | collective-permute-start | bytes 129032 | tf_op jit(solution)/shard_map/ppermute | solution.py:255
  2.2 1.3 %collective-permute-start.1 = (bf16[8,2688]{1,0:T(8,128)(2,1)S(1)}, bf16[8,2688]{1,0:T(8,128)(2,1)S(1)}, u32[]{:S(2)}, u32[]{:S(2)}) collective-permute-start(bf16[8,2688]{1,0:T(8,128)(2,1)S(1)} %fusion.qa), channel_id=1, source_target_pairs={{16,8},{20,12},{24,0},{28,4},{17,9},{21,13},{25,1},{29,5},{18,10},... | collective-permute-start | bytes 129032 | tf_op jit(solution)/shard_map/ppermute | solution.py:255
  3.5 1.3 %collective-permute-start = (bf16[8,2688]{1,0:T(8,128)(2,1)S(1)}, bf16[8,2688]{1,0:T(8,128)(2,1)S(1)}, u32[]{:S(2)}, u32[]{:S(2)}) collective-permute-start(bf16[8,2688]{1,0:T(8,128)(2,1)S(1)} %fusion.qa), channel_id=1, source_target_pairs={{16,4},{20,8},{24,12},{28,0},{17,5},{21,9},{25,13},{29,1},{18,6},{... | collective-permute-start | bytes 129032 | tf_op jit(solution)/shard_map/ppermute | solution.py:255
  4.8 4.3 %resident.1 = (f32[136,128]{1,0:T(8,128)S(1)}, bf16[24,128,512]{2,1,0:T(8,128)(2,1)S(1)}, f32[24,128]{1,0:T(8,128)S(1)}) custom-call(bf16[8,2688]{1,0:T(8,128)(2,1)S(1)} %fusion.qa, s32[3,4,12]{2,1,0:T(4,128)} %bitcast.12, s32[4,6]{1,0:T(4,128)} %wanted_hbm.1, s32[8,8]{1,0:T(8,128)} %bitcast.10, bf16[64,128,512]{2,1,0:T(8,128)(2,1)} %bitcast.11), custom_call_target="tpu_custom_call" | custom-call | flops 4000000000 | bytes 12582912 | tf_op jit(solution)/shard_map/resident/pallas_call | solution.py:263
  9.1 0.9 %collective-permute-done.1.refs_1_ = bf16[8,2688]{1,0:T(8,128)(2,1)S(1)} collective-permute-done((bf16[8,2688]{1,0:T(8,128)(2,1)S(1)}, bf16[8,2688]{1,0:T(8,128)(2,1)S(1)}, u32[]{:S(2)}, u32[]{:S(2)}) %collective-permute-start.1) | collective-permute-done | bytes 43040 | tf_op jit(solution)/shard_map/ppermute | solution.py:255
  10.0 2.3 %collective-permute-done.refs_0_ = bf16[8,2688]{1,0:T(8,128)(2,1)S(1)} collective-permute-done((bf16[8,2688]{1,0:T(8,128)(2,1)S(1)}, bf16[8,2688]{1,0:T(8,128)(2,1)S(1)}, u32[]{:S(2)}, u32[]{:S(2)}) %collective-permute-start) | collective-permute-done | bytes 43040 | tf_op jit(solution)/shard_map/ppermute | solution.py:255
  12.3 1.7 %owned.1 = (f32[136,128]{1,0:T(8,128)S(1)}, f32[136,128]{1,0:T(8,128)S(1)}, f32[136,128]{1,0:T(8,128)S(1)}) custom-call(bf16[24,128,512]{2,1,0:T(8,128)(2,1)S(1)} %get-tuple-element.19.chosen, f32[24,128]{1,0:T(8,128)S(1)} %get-tuple-element.20.entries, bf16[8,2688]{1,0:T(8,128)(2,1)S(1)} %collective-permute-done.refs_0_, ...), custom_call_target="tpu_custom_call" | custom-call | flops 4000000000 | bytes 8388608 | tf_op jit(solution)/shard_map/owned/pallas_call | solution.py:288
  14.0 8.3 %collective-permute-start.4 = (f32[136,128]{1,0:T(8,128)S(1)}, f32[136,128]{1,0:T(8,128)S(1)}, u32[]{:S(2)}, u32[]{:S(2)}) collective-permute-start(f32[136,128]{1,0:T(8,128)S(1)} %get-tuple-element.25), channel_id=1, source_target_pairs={{0,28},{4,16},{8,20},{12,24},{1,29},{5,17},{9,21},{13,25},{2,30},{... | collective-permute-start | bytes 208904 | tf_op jit(solution)/shard_map/ppermute | solution.py:301
  22.3 1.4 %collective-permute-start.5 = (f32[136,128]{1,0:T(8,128)S(1)}, f32[136,128]{1,0:T(8,128)S(1)}, u32[]{:S(2)}, u32[]{:S(2)}) collective-permute-start(f32[136,128]{1,0:T(8,128)S(1)} %get-tuple-element.26), channel_id=1, source_target_pairs={{0,24},{4,28},{8,16},{12,20},{1,25},{5,29},{9,17},{13,21},{2,26},{... | collective-permute-start | bytes 208904 | tf_op jit(solution)/shard_map/ppermute | solution.py:301
  23.7 1.3 %collective-permute-start.6 = (f32[136,128]{1,0:T(8,128)S(1)}, f32[136,128]{1,0:T(8,128)S(1)}, u32[]{:S(2)}, u32[]{:S(2)}) collective-permute-start(f32[136,128]{1,0:T(8,128)S(1)} %get-tuple-element.27), channel_id=1, source_target_pairs={{0,20},{4,24},{8,28},{12,16},{1,21},{5,25},{9,29},{13,17},{2,22},{... | collective-permute-start | bytes 208904 | tf_op jit(solution)/shard_map/ppermute | solution.py:301
  25.0 1.3 %collective-permute-start.3 = (f32[136,128]{1,0:T(8,128)S(1)}, f32[136,128]{1,0:T(8,128)S(1)}, u32[]{:S(2)}, u32[]{:S(2)}) collective-permute-start(f32[136,128]{1,0:T(8,128)S(1)} %get-tuple-element.24.refs_0_), channel_id=1, source_target_pairs={{0,16},{1,17},{2,18},{3,19},{4,20},{5,21},{6,22},{7,23},{8,24},{9,... | collective-permute-start | bytes 208904 | tf_op jit(solution)/shard_map/ppermute | solution.py:298
  26.3 0.6 %collective-permute-done.6.refs_4_ = f32[136,128]{1,0:T(8,128)S(1)} collective-permute-done((f32[136,128]{1,0:T(8,128)S(1)}, f32[136,128]{1,0:T(8,128)S(1)}, u32[]{:S(2)}, u32[]{:S(2)}) %collective-permute-start.6) | collective-permute-done | bytes 69664 | tf_op jit(solution)/shard_map/ppermute | solution.py:301
  27.1 0.3 merge.1.attended
  27.5 1.3 %collective-permute-start.7 = (bf16[8,2048]{1,0:T(8,128)(2,1)S(1)}, bf16[8,2048]{1,0:T(8,128)(2,1)S(1)}, u32[]{:S(2)}, u32[]{:S(2)}) collective-permute-start(bf16[8,2048]{1,0:T(8,128)(2,1)S(1)} %merge.1.attended), channel_id=1, source_target_pairs={{16,0},{17,1},{18,2},{19,3},{20,4},{21,5},{22,6},{23,7},{24,8},{25... | collective-permute-start | bytes 98312 | tf_op jit(solution)/shard_map/ppermute | solution.py:311
  28.8 3.5 %collective-permute-done.7.partner = bf16[8,2048]{1,0:T(8,128)(2,1)S(1)} collective-permute-done((bf16[8,2048]{1,0:T(8,128)(2,1)S(1)}, bf16[8,2048]{1,0:T(8,128)(2,1)S(1)}, u32[]{:S(2)}, u32[]{:S(2)}) %collective-permute-start.7) | collective-permute-done | bytes 32800 | tf_op jit(solution)/shard_map/ppermute | solution.py:311
  32.2 1.7 %project.1 = (f32[8,1024]{1,0:T(8,128)S(1)}, f32[8,1024]{1,0:T(8,128)S(1)}, f32[8,1024]{1,0:T(8,128)S(1)}) custom-call(bf16[8,2048]{1,0:T(8,128)(2,1)S(1)} %merge.1.attended, bf16[8,2048]{1,0:T(8,128)(2,1)S(1)} %collective-permute-done.7.partner, bf16[2048,4096]{1,0:T(8,128)(2,1)S(1)} %copy-done), custom_call_target="tpu_custom_call" | custom-call | flops 201326592 | bytes 12582912 | tf_op jit(solution)/shard_map/project/pallas_call | solution.py:315
  33.9 1.5 %collective-permute-start.8 = (f32[8,1024]{1,0:T(8,128)S(1)}, f32[8,1024]{1,0:T(8,128)S(1)}, u32[]{:S(2)}, u32[]{:S(2)}) collective-permute-start(f32[8,1024]{1,0:T(8,128)S(1)} %get-tuple-element.28), channel_id=1, source_target_pairs={{0,1},{1,2},{2,3},{3,0},{4,5},{5,6},{6,7},{7,4},{8,9},{9,10},{10,1... | collective-permute-start | bytes 98312 | tf_op jit(solution)/shard_map/ppermute | solution.py:329
  35.5 1.5 %collective-permute-start.9 = (f32[8,1024]{1,0:T(8,128)S(1)}, f32[8,1024]{1,0:T(8,128)S(1)}, u32[]{:S(2)}, u32[]{:S(2)}) collective-permute-start(f32[8,1024]{1,0:T(8,128)S(1)} %get-tuple-element.29), channel_id=1, source_target_pairs={{0,2},{1,3},{2,0},{3,1},{4,6},{5,7},{6,4},{7,5},{8,10},{9,11},{10,... | collective-permute-start | bytes 98312 | tf_op jit(solution)/shard_map/ppermute | solution.py:329
  37.0 1.4 %collective-permute-start.10 = (f32[8,1024]{1,0:T(8,128)S(1)}, f32[8,1024]{1,0:T(8,128)S(1)}, u32[]{:S(2)}, u32[]{:S(2)}) collective-permute-start(f32[8,1024]{1,0:T(8,128)S(1)} %get-tuple-element.30), channel_id=1, source_target_pairs={{0,3},{1,0},{2,1},{3,2},{4,7},{5,4},{6,5},{7,6},{8,11},{9,8},{10,9... | collective-permute-start | bytes 98312 | tf_op jit(solution)/shard_map/ppermute | solution.py:329
  38.4 0.6 %project_own.1 = f32[8,1024]{1,0:T(8,128)S(1)} custom-call(bf16[8,2048]{1,0:T(8,128)(2,1)S(1)} %merge.1.attended, bf16[8,2048]{1,0:T(8,128)(2,1)S(1)} %collective-permute-done.7.partner, bf16[2048,4096]{1,0:T(8,128)(2,1)S(1)} %copy-done), custom_call_target="tpu_custom_call" | custom-call | flops 67108864 | bytes 4194304 | tf_op jit(solution)/shard_map/project_own/pallas_call | solution.py:315
  39.1 0.3 collective-permute-done.9
  39.4 1.5 %collective-permute-done.10 = f32[8,1024]{1,0:T(8,128)S(1)} collective-permute-done((f32[8,1024]{1,0:T(8,128)S(1)}, f32[8,1024]{1,0:T(8,128)S(1)}, u32[]{:S(2)}, u32[]{:S(2)}) %collective-permute-start.10) | collective-permute-done | bytes 32800 | tf_op jit(solution)/shard_map/ppermute | solution.py:329
  40.9 0.6 %fusion.1 = bf16[1,8,1024]{2,1,0:T(8,128)(2,1)} fusion(f32[8,1024]{1,0:T(8,128)S(1)} %collective-permute-done.10, f32[8,1024]{1,0:T(8,128)S(1)} %collective-permute-done.9, f32[8,1024]{1,0:T(8,128)S(1)} %project_own.1, f32[8,1024]{1,0:T(8,128)S(1)} %collective-permute-done.8), kind=kLoop, calls=%fused_computation.3 | loop fusion | flops 32768 | bytes 147456 | tf_op jit(solution)/shard_map/broadcast_in_dim | solution.py:331
  (7 shorter events, 0.3 us)
Async XLA Ops:
  0.9 8.2 %collective-permute-start.2 = (bf16[8,2688]{1,0:T(8,128)(2,1)S(1)}, bf16[8,2688]{1,0:T(8,128)(2,1)S(1)}, u32[]{:S(2)}, u32[]{:S(2)}) collective-permute-start(bf16[8,2688]{1,0:T(8,128)(2,1)S(1)} %fusion.qa), channel_id=1, source_target_pairs={{16,12},{20,0},{24,4},{28,8},{17,13},{21,1},{25,5},{29,9},{18,14},... | collective-permute-start | bytes 129032 | tf_op jit(solution)/shard_map/ppermute | solution.py:255
  2.2 7.8 %collective-permute-start.1 = (bf16[8,2688]{1,0:T(8,128)(2,1)S(1)}, bf16[8,2688]{1,0:T(8,128)(2,1)S(1)}, u32[]{:S(2)}, u32[]{:S(2)}) collective-permute-start(bf16[8,2688]{1,0:T(8,128)(2,1)S(1)} %fusion.qa), channel_id=1, source_target_pairs={{16,8},{20,12},{24,0},{28,4},{17,9},{21,13},{25,1},{29,5},{18,10},... | collective-permute-start | bytes 129032 | tf_op jit(solution)/shard_map/ppermute | solution.py:255
  3.5 8.8 %collective-permute-start = (bf16[8,2688]{1,0:T(8,128)(2,1)S(1)}, bf16[8,2688]{1,0:T(8,128)(2,1)S(1)}, u32[]{:S(2)}, u32[]{:S(2)}) collective-permute-start(bf16[8,2688]{1,0:T(8,128)(2,1)S(1)} %fusion.qa), channel_id=1, source_target_pairs={{16,4},{20,8},{24,12},{28,0},{17,5},{21,9},{25,13},{29,1},{18,6},{... | collective-permute-start | bytes 129032 | tf_op jit(solution)/shard_map/ppermute | solution.py:255
  4.8 27.4 %copy-start = (bf16[2048,4096]{1,0:T(8,128)(2,1)S(1)}, bf16[2048,4096]{1,0:T(8,128)(2,1)}, u32[]{:S(2)}) copy-start(bf16[2048,4096]{1,0:T(8,128)(2,1)} %weight.3) | copy-start | bytes 50331652
  14.0 12.3 %collective-permute-start.4 = (f32[136,128]{1,0:T(8,128)S(1)}, f32[136,128]{1,0:T(8,128)S(1)}, u32[]{:S(2)}, u32[]{:S(2)}) collective-permute-start(f32[136,128]{1,0:T(8,128)S(1)} %get-tuple-element.25), channel_id=1, source_target_pairs={{0,28},{4,16},{8,20},{12,24},{1,29},{5,17},{9,21},{13,25},{2,30},{... | collective-permute-start | bytes 208904 | tf_op jit(solution)/shard_map/ppermute | solution.py:301
  22.3 4.0 %collective-permute-start.5 = (f32[136,128]{1,0:T(8,128)S(1)}, f32[136,128]{1,0:T(8,128)S(1)}, u32[]{:S(2)}, u32[]{:S(2)}) collective-permute-start(f32[136,128]{1,0:T(8,128)S(1)} %get-tuple-element.26), channel_id=1, source_target_pairs={{0,24},{4,28},{8,16},{12,20},{1,25},{5,29},{9,17},{13,21},{2,26},{... | collective-permute-start | bytes 208904 | tf_op jit(solution)/shard_map/ppermute | solution.py:301
  23.7 3.2 %collective-permute-start.6 = (f32[136,128]{1,0:T(8,128)S(1)}, f32[136,128]{1,0:T(8,128)S(1)}, u32[]{:S(2)}, u32[]{:S(2)}) collective-permute-start(f32[136,128]{1,0:T(8,128)S(1)} %get-tuple-element.27), channel_id=1, source_target_pairs={{0,20},{4,24},{8,28},{12,16},{1,21},{5,25},{9,29},{13,17},{2,22},{... | collective-permute-start | bytes 208904 | tf_op jit(solution)/shard_map/ppermute | solution.py:301
  25.0 2.2 %collective-permute-start.3 = (f32[136,128]{1,0:T(8,128)S(1)}, f32[136,128]{1,0:T(8,128)S(1)}, u32[]{:S(2)}, u32[]{:S(2)}) collective-permute-start(f32[136,128]{1,0:T(8,128)S(1)} %get-tuple-element.24.refs_0_), channel_id=1, source_target_pairs={{0,16},{1,17},{2,18},{3,19},{4,20},{5,21},{6,22},{7,23},{8,24},{9,... | collective-permute-start | bytes 208904 | tf_op jit(solution)/shard_map/ppermute | solution.py:298
  27.5 4.8 %collective-permute-start.7 = (bf16[8,2048]{1,0:T(8,128)(2,1)S(1)}, bf16[8,2048]{1,0:T(8,128)(2,1)S(1)}, u32[]{:S(2)}, u32[]{:S(2)}) collective-permute-start(bf16[8,2048]{1,0:T(8,128)(2,1)S(1)} %merge.1.attended), channel_id=1, source_target_pairs={{16,0},{17,1},{18,2},{19,3},{20,4},{21,5},{22,6},{23,7},{24,8},{25... | collective-permute-start | bytes 98312 | tf_op jit(solution)/shard_map/ppermute | solution.py:311
  33.9 5.1 %collective-permute-start.8 = (f32[8,1024]{1,0:T(8,128)S(1)}, f32[8,1024]{1,0:T(8,128)S(1)}, u32[]{:S(2)}, u32[]{:S(2)}) collective-permute-start(f32[8,1024]{1,0:T(8,128)S(1)} %get-tuple-element.28), channel_id=1, source_target_pairs={{0,1},{1,2},{2,3},{3,0},{4,5},{5,6},{6,7},{7,4},{8,9},{9,10},{10,1... | collective-permute-start | bytes 98312 | tf_op jit(solution)/shard_map/ppermute | solution.py:329
  35.5 3.9 %collective-permute-start.9 = (f32[8,1024]{1,0:T(8,128)S(1)}, f32[8,1024]{1,0:T(8,128)S(1)}, u32[]{:S(2)}, u32[]{:S(2)}) collective-permute-start(f32[8,1024]{1,0:T(8,128)S(1)} %get-tuple-element.29), channel_id=1, source_target_pairs={{0,2},{1,3},{2,0},{3,1},{4,6},{5,7},{6,4},{7,5},{8,10},{9,11},{10,... | collective-permute-start | bytes 98312 | tf_op jit(solution)/shard_map/ppermute | solution.py:329
  37.0 3.9 %collective-permute-start.10 = (f32[8,1024]{1,0:T(8,128)S(1)}, f32[8,1024]{1,0:T(8,128)S(1)}, u32[]{:S(2)}, u32[]{:S(2)}) collective-permute-start(f32[8,1024]{1,0:T(8,128)S(1)} %get-tuple-element.30), channel_id=1, source_target_pairs={{0,3},{1,0},{2,1},{3,2},{4,7},{5,4},{6,5},{7,6},{8,11},{9,8},{10,9... | collective-permute-start | bytes 98312 | tf_op jit(solution)/shard_map/ppermute | solution.py:329

commit v4 on v3

--- a/solution.py
+++ b/solution.py
@@ -252,7 +252,9 @@
     integers = place(tables[0], wide) + high + low
     qa = place(queries[0], 0) + place(new_kv[0], fresh_at) + integers.astype(jnp.bfloat16)
     asked = [
-        lax.ppermute(qa, ("role", "group"), [(groups + i, (i + k) % groups) for i in range(groups)])
+        lax.ppermute(
+            qa, ("role", "group"), [pair for i in range(groups) for pair in ((groups + i, (i + k) % groups), (i, groups + i))]
+        )
         for k in range(1, groups)
     ]
     part_shape = jax.ShapeDtypeStruct((heads * rows + 8, HD), jnp.float32)
@@ -295,11 +297,10 @@
         name="owned",
     )(chosen, entries, *asked)
     mine, theirs = lax.optimization_barrier((mine, theirs))
-    parts = [mine, lax.ppermute(mine, "role", [(0, 1)])]
+    parts = [mine, lax.ppermute(mine, "role", [(0, 1), (1, 0)])]
     for k in range(1, groups):
-        parts.append(
-            lax.ppermute(theirs[k - 1], ("role", "group"), [(i, groups + (i - k) % groups) for i in range(groups)])
-        )
+        pairs = [pair for i in range(groups) for pair in ((i, groups + (i - k) % groups), (groups + i, i))]
+        parts.append(lax.ppermute(theirs[k - 1], ("role", "group"), pairs))
     attended = pl.pallas_call(
         functools.partial(merge_kernel, heads, rows),
         out_shape=jax.ShapeDtypeStruct((rows, wide), jnp.bfloat16),
@@ -308,7 +309,7 @@
         compiler_params=pltpu.CompilerParams(vmem_limit_bytes=8 * MIB),
         name="merge",
     )(*parts)
-    partner = lax.ppermute(attended, "role", [(1, 0)])
+    partner = lax.ppermute(attended, "role", [(0, 1), (1, 0)])
     share = out_weight.shape[1] // tps
 
     def project(steps, name):

time: 42.2 us -> 36.2 us (0.86); the launches traced: 41.5 us -> 36.2 us
  waiting for transfers between devices: 9.39 us -> 6.52 us
  starting transfers between devices: 21.9 us -> 19.5 us
    ppermute x8, waiting for transfers between devices: 7.55 us -> 4.69 us  [the longest x3 2.85 us: per_device(): parts.append(lax.ppermute(theirs[k - 1], ('role', 'group'), pairs))]
    ppermute x8, starting transfers between devices: 17.4 us -> 15.1 us  [the longest x3 6.65 us: per_device(): parts.append(lax.ppermute(theirs[k - 1], ('role', 'group'), pairs))]
  transfers between devices with their start and end apart: 11 -> 11, of which waited for: 7 -> 7; matrix products, arithmetic and copies ran while one was open for 0% -> 0% of each run, Pallas kernels for 12% -> 13%
where the time goes in v4:
time: 36.2 us
  starting transfers between devices  19.5 us (54%)
  Pallas kernels  8.59 us (24%)
  waiting for transfers between devices  6.52 us (18%)
  other arithmetic  1.52 us (4%)
    ppermute x3, starting transfers between devices, per_device(): parts.append(lax.ppermute(theirs[k - 1], ('role', 'group'), pairs))  6.65 us
    ppermute x3, starting transfers between devices, per_device(): lax.ppermute(qa, ('role', 'group'), [pair for i in range(groups) for pair...  5.17 us
    ppermute x3, starting transfers between devices, per_device(): lax.ppermute(part, 'tp', [(i, (i + d) % tps) for i in range(tps)])  4.46 us
    pallas_call x1, Pallas kernels, per_device(): pl.pallas_call(functools.partial(first_kernel, held, per_held, groups, ma...  4.24 us
    ppermute x3, waiting for transfers between devices, per_device(): parts.append(lax.ppermute(theirs[k - 1], ('role', 'group'), pairs))  2.85 us
    ppermute x1, starting transfers between devices, per_device(): partner = lax.ppermute(attended, 'role', [(0, 1), (1, 0)])  2.74 us
    pallas_call x2, Pallas kernels, project(): pl.pallas_call(functools.partial(project_kernel, steps), out_shape=[jax.S...  2.37 us
    ppermute x3, waiting for transfers between devices, per_device(): lax.ppermute(part, 'tp', [(i, (i + d) % tps) for i in range(tps)])  1.83 us
  transfers between devices with their start and end apart: 11, of which 7 were waited for; matrix products, arithmetic and copies ran while one was open for 0% of the time, Pallas kernels for 13%

profile of v4, /device:TPU:0, one launch (start us, length us, event | category | flops | bytes accessed | tf_op | source)
XLA Modules:
  0.0 36.2 jit_solution(12535550886762869398)
XLA Ops:
  0.0 0.9 %fusion.qa = bf16[8,2688]{1,0:T(8,128)(2,1)S(1)} fusion(s32[1,8]{1,0:T(1,128)} %param.11, s32[8,8]{1,0:T(8,128)} %bitcast.9, bf16[8,512]{1,0:T(8,128)(2,1)} %bitcast.8, bf16[8,2048]{1,0:T(8,128)(2,1)} %bitcast.7), kind=kLoop, calls=%fused_computation.1 | loop fusion | flops 236544 | bytes 84256 | tf_op jit(solution)/shard_map/add | solution.py:253
  0.9 0.5 %collective-permute-start.2 = (bf16[8,2688]{1,0:T(8,128)(2,1)S(1)}, bf16[8,2688]{1,0:T(8,128)(2,1)S(1)}, u32[]{:S(2)}, u32[]{:S(2)}) collective-permute-start(bf16[8,2688]{1,0:T(8,128)(2,1)S(1)} %fusion.qa), channel_id=1, source_target_pairs={{16,12},{0,16},{20,0},{4,20},{24,4},{8,24},{28,8},{12,28},{17,13},... | collective-permute-start | bytes 129032 | tf_op jit(solution)/shard_map/ppermute | solution.py:255
  1.4 4.7 %collective-permute-start.1 = (bf16[8,2688]{1,0:T(8,128)(2,1)S(1)}, bf16[8,2688]{1,0:T(8,128)(2,1)S(1)}, u32[]{:S(2)}, u32[]{:S(2)}) collective-permute-start(bf16[8,2688]{1,0:T(8,128)(2,1)S(1)} %fusion.qa), channel_id=1, source_target_pairs={{16,8},{0,16},{20,12},{4,20},{24,0},{8,24},{28,4},{12,28},{17,9},{... | collective-permute-start | bytes 129032 | tf_op jit(solution)/shard_map/ppermute | solution.py:255
  6.1 0.0 collective-permute-start
  6.1 4.2 %resident.1 = (f32[136,128]{1,0:T(8,128)S(1)}, bf16[24,128,512]{2,1,0:T(8,128)(2,1)S(1)}, f32[24,128]{1,0:T(8,128)S(1)}) custom-call(bf16[8,2688]{1,0:T(8,128)(2,1)S(1)} %fusion.qa, s32[3,4,12]{2,1,0:T(4,128)} %bitcast.12, s32[4,6]{1,0:T(4,128)} %wanted_hbm.1, s32[8,8]{1,0:T(8,128)} %bitcast.10, bf16[64,128,512]{2,1,0:T(8,128)(2,1)} %bitcast.11), custom_call_target="tpu_custom_call" | custom-call | flops 4000000000 | bytes 12582912 | tf_op jit(solution)/shard_map/resident/pallas_call | solution.py:265
  10.3 0.0 collective-permute-done.2.refs_2_
  10.3 1.0 %collective-permute-done.refs_0_ = bf16[8,2688]{1,0:T(8,128)(2,1)S(1)} collective-permute-done((bf16[8,2688]{1,0:T(8,128)(2,1)S(1)}, bf16[8,2688]{1,0:T(8,128)(2,1)S(1)}, u32[]{:S(2)}, u32[]{:S(2)}) %collective-permute-start) | collective-permute-done | bytes 43040 | tf_op jit(solution)/shard_map/ppermute | solution.py:255
  11.3 1.7 %owned.1 = (f32[136,128]{1,0:T(8,128)S(1)}, f32[136,128]{1,0:T(8,128)S(1)}, f32[136,128]{1,0:T(8,128)S(1)}) custom-call(bf16[24,128,512]{2,1,0:T(8,128)(2,1)S(1)} %get-tuple-element.19.chosen, f32[24,128]{1,0:T(8,128)S(1)} %get-tuple-element.20.entries, bf16[8,2688]{1,0:T(8,128)(2,1)S(1)} %collective-permute-done.refs_0_, ...), custom_call_target="tpu_custom_call" | custom-call | flops 4000000000 | bytes 8388608 | tf_op jit(solution)/shard_map/owned/pallas_call | solution.py:290
  13.0 6.6 %collective-permute-start.4 = (f32[136,128]{1,0:T(8,128)S(1)}, f32[136,128]{1,0:T(8,128)S(1)}, u32[]{:S(2)}, u32[]{:S(2)}) collective-permute-start(f32[136,128]{1,0:T(8,128)S(1)} %get-tuple-element.25), channel_id=1, source_target_pairs={{0,28},{16,0},{4,16},{20,4},{8,20},{24,8},{12,24},{28,12},{1,29},{... | collective-permute-start | bytes 208904 | tf_op jit(solution)/shard_map/ppermute | solution.py:303
  19.6 0.5 %collective-permute-start.3 = (f32[136,128]{1,0:T(8,128)S(1)}, f32[136,128]{1,0:T(8,128)S(1)}, u32[]{:S(2)}, u32[]{:S(2)}) collective-permute-start(f32[136,128]{1,0:T(8,128)S(1)} %get-tuple-element.24.refs_0_), channel_id=1, source_target_pairs={{0,16},{16,0},{1,17},{17,1},{2,18},{18,2},{3,19},{19,3},{4,20},{20... | collective-permute-start | bytes 208904 | tf_op jit(solution)/shard_map/ppermute | solution.py:300
  20.1 1.4 %collective-permute-done.4.refs_2_ = f32[136,128]{1,0:T(8,128)S(1)} collective-permute-done((f32[136,128]{1,0:T(8,128)S(1)}, f32[136,128]{1,0:T(8,128)S(1)}, u32[]{:S(2)}, u32[]{:S(2)}) %collective-permute-start.4) | collective-permute-done | bytes 69664 | tf_op jit(solution)/shard_map/ppermute | solution.py:303
  21.6 0.7 %collective-permute-done.5.refs_3_ = f32[136,128]{1,0:T(8,128)S(1)} collective-permute-done((f32[136,128]{1,0:T(8,128)S(1)}, f32[136,128]{1,0:T(8,128)S(1)}, u32[]{:S(2)}, u32[]{:S(2)}) %collective-permute-start.5) | collective-permute-done | bytes 69664 | tf_op jit(solution)/shard_map/ppermute | solution.py:303
  22.2 0.7 %collective-permute-done.6.refs_4_ = f32[136,128]{1,0:T(8,128)S(1)} collective-permute-done((f32[136,128]{1,0:T(8,128)S(1)}, f32[136,128]{1,0:T(8,128)S(1)}, u32[]{:S(2)}, u32[]{:S(2)}) %collective-permute-start.6) | collective-permute-done | bytes 69664 | tf_op jit(solution)/shard_map/ppermute | solution.py:303
  23.0 0.3 merge.1.attended
  23.3 2.7 %collective-permute-start.7 = (bf16[8,2048]{1,0:T(8,128)(2,1)S(1)}, bf16[8,2048]{1,0:T(8,128)(2,1)S(1)}, u32[]{:S(2)}, u32[]{:S(2)}) collective-permute-start(bf16[8,2048]{1,0:T(8,128)(2,1)S(1)} %merge.1.attended), channel_id=1, source_target_pairs={{0,16},{16,0},{1,17},{17,1},{2,18},{18,2},{3,19},{19,3},{4,20},{20... | collective-permute-start | bytes 98312 | tf_op jit(solution)/shard_map/ppermute | solution.py:312
  26.1 0.9 %collective-permute-done.7.partner = bf16[8,2048]{1,0:T(8,128)(2,1)S(1)} collective-permute-done((bf16[8,2048]{1,0:T(8,128)(2,1)S(1)}, bf16[8,2048]{1,0:T(8,128)(2,1)S(1)}, u32[]{:S(2)}, u32[]{:S(2)}) %collective-permute-start.7) | collective-permute-done | bytes 32800 | tf_op jit(solution)/shard_map/ppermute | solution.py:312
  26.9 1.7 %project.1 = (f32[8,1024]{1,0:T(8,128)S(1)}, f32[8,1024]{1,0:T(8,128)S(1)}, f32[8,1024]{1,0:T(8,128)S(1)}) custom-call(bf16[8,2048]{1,0:T(8,128)(2,1)S(1)} %merge.1.attended, bf16[8,2048]{1,0:T(8,128)(2,1)S(1)} %collective-permute-done.7.partner, bf16[2048,4096]{1,0:T(8,128)(2,1)S(1)} %copy-done), custom_call_target="tpu_custom_call" | custom-call | flops 201326592 | bytes 12582912 | tf_op jit(solution)/shard_map/project/pallas_call | solution.py:316
  28.7 1.5 %collective-permute-start.8 = (f32[8,1024]{1,0:T(8,128)S(1)}, f32[8,1024]{1,0:T(8,128)S(1)}, u32[]{:S(2)}, u32[]{:S(2)}) collective-permute-start(f32[8,1024]{1,0:T(8,128)S(1)} %get-tuple-element.28), channel_id=1, source_target_pairs={{0,1},{1,2},{2,3},{3,0},{4,5},{5,6},{6,7},{7,4},{8,9},{9,10},{10,1... | collective-permute-start | bytes 98312 | tf_op jit(solution)/shard_map/ppermute | solution.py:330
  30.2 1.5 %collective-permute-start.9 = (f32[8,1024]{1,0:T(8,128)S(1)}, f32[8,1024]{1,0:T(8,128)S(1)}, u32[]{:S(2)}, u32[]{:S(2)}) collective-permute-start(f32[8,1024]{1,0:T(8,128)S(1)} %get-tuple-element.29), channel_id=1, source_target_pairs={{0,2},{1,3},{2,0},{3,1},{4,6},{5,7},{6,4},{7,5},{8,10},{9,11},{10,... | collective-permute-start | bytes 98312 | tf_op jit(solution)/shard_map/ppermute | solution.py:330
  31.7 1.4 %collective-permute-start.10 = (f32[8,1024]{1,0:T(8,128)S(1)}, f32[8,1024]{1,0:T(8,128)S(1)}, u32[]{:S(2)}, u32[]{:S(2)}) collective-permute-start(f32[8,1024]{1,0:T(8,128)S(1)} %get-tuple-element.30), channel_id=1, source_target_pairs={{0,3},{1,0},{2,1},{3,2},{4,7},{5,4},{6,5},{7,6},{8,11},{9,8},{10,9... | collective-permute-start | bytes 98312 | tf_op jit(solution)/shard_map/ppermute | solution.py:330
  33.1 0.6 %project_own.1 = f32[8,1024]{1,0:T(8,128)S(1)} custom-call(bf16[8,2048]{1,0:T(8,128)(2,1)S(1)} %merge.1.attended, bf16[8,2048]{1,0:T(8,128)(2,1)S(1)} %collective-permute-done.7.partner, bf16[2048,4096]{1,0:T(8,128)(2,1)S(1)} %copy-done), custom_call_target="tpu_custom_call" | custom-call | flops 67108864 | bytes 4194304 | tf_op jit(solution)/shard_map/project_own/pallas_call | solution.py:316
  33.8 0.3 collective-permute-done.9
  34.1 1.5 %collective-permute-done.10 = f32[8,1024]{1,0:T(8,128)S(1)} collective-permute-done((f32[8,1024]{1,0:T(8,128)S(1)}, f32[8,1024]{1,0:T(8,128)S(1)}, u32[]{:S(2)}, u32[]{:S(2)}) %collective-permute-start.10) | collective-permute-done | bytes 32800 | tf_op jit(solution)/shard_map/ppermute | solution.py:330
  35.6 0.6 %fusion.1 = bf16[1,8,1024]{2,1,0:T(8,128)(2,1)} fusion(f32[8,1024]{1,0:T(8,128)S(1)} %collective-permute-done.10, f32[8,1024]{1,0:T(8,128)S(1)} %collective-permute-done.9, f32[8,1024]{1,0:T(8,128)S(1)} %project_own.1, f32[8,1024]{1,0:T(8,128)S(1)} %collective-permute-done.8), kind=kLoop, calls=%fused_computation.3 | loop fusion | flops 32768 | bytes 147456 | tf_op jit(solution)/shard_map/broadcast_in_dim | solution.py:332
  (7 shorter events, 0.0 us)
Async XLA Ops:
  0.9 9.4 %collective-permute-start.2 = (bf16[8,2688]{1,0:T(8,128)(2,1)S(1)}, bf16[8,2688]{1,0:T(8,128)(2,1)S(1)}, u32[]{:S(2)}, u32[]{:S(2)}) collective-permute-start(bf16[8,2688]{1,0:T(8,128)(2,1)S(1)} %fusion.qa), channel_id=1, source_target_pairs={{16,12},{0,16},{20,0},{4,20},{24,4},{8,24},{28,8},{12,28},{17,13},... | collective-permute-start | bytes 129032 | tf_op jit(solution)/shard_map/ppermute | solution.py:255
  1.4 9.0 %collective-permute-start.1 = (bf16[8,2688]{1,0:T(8,128)(2,1)S(1)}, bf16[8,2688]{1,0:T(8,128)(2,1)S(1)}, u32[]{:S(2)}, u32[]{:S(2)}) collective-permute-start(bf16[8,2688]{1,0:T(8,128)(2,1)S(1)} %fusion.qa), channel_id=1, source_target_pairs={{16,8},{0,16},{20,12},{4,20},{24,0},{8,24},{28,4},{12,28},{17,9},{... | collective-permute-start | bytes 129032 | tf_op jit(solution)/shard_map/ppermute | solution.py:255
  6.1 5.2 %collective-permute-start = (bf16[8,2688]{1,0:T(8,128)(2,1)S(1)}, bf16[8,2688]{1,0:T(8,128)(2,1)S(1)}, u32[]{:S(2)}, u32[]{:S(2)}) collective-permute-start(bf16[8,2688]{1,0:T(8,128)(2,1)S(1)} %fusion.qa), channel_id=1, source_target_pairs={{16,4},{0,16},{20,8},{4,20},{24,12},{8,24},{28,0},{12,28},{17,5},{... | collective-permute-start | bytes 129032 | tf_op jit(solution)/shard_map/ppermute | solution.py:255
  6.1 20.9 %copy-start = (bf16[2048,4096]{1,0:T(8,128)(2,1)S(1)}, bf16[2048,4096]{1,0:T(8,128)(2,1)}, u32[]{:S(2)}) copy-start(bf16[2048,4096]{1,0:T(8,128)(2,1)} %weight.3) | copy-start | bytes 50331652
  13.0 8.6 %collective-permute-start.4 = (f32[136,128]{1,0:T(8,128)S(1)}, f32[136,128]{1,0:T(8,128)S(1)}, u32[]{:S(2)}, u32[]{:S(2)}) collective-permute-start(f32[136,128]{1,0:T(8,128)S(1)} %get-tuple-element.25), channel_id=1, source_target_pairs={{0,28},{16,0},{4,16},{20,4},{8,20},{24,8},{12,24},{28,12},{1,29},{... | collective-permute-start | bytes 208904 | tf_op jit(solution)/shard_map/ppermute | solution.py:303
  19.6 2.6 %collective-permute-start.5 = (f32[136,128]{1,0:T(8,128)S(1)}, f32[136,128]{1,0:T(8,128)S(1)}, u32[]{:S(2)}, u32[]{:S(2)}) collective-permute-start(f32[136,128]{1,0:T(8,128)S(1)} %get-tuple-element.26), channel_id=1, source_target_pairs={{0,24},{16,0},{4,28},{20,4},{8,16},{24,8},{12,20},{28,12},{1,25},{... | collective-permute-start | bytes 208904 | tf_op jit(solution)/shard_map/ppermute | solution.py:303
  19.6 3.4 %collective-permute-start.6 = (f32[136,128]{1,0:T(8,128)S(1)}, f32[136,128]{1,0:T(8,128)S(1)}, u32[]{:S(2)}, u32[]{:S(2)}) collective-permute-start(f32[136,128]{1,0:T(8,128)S(1)} %get-tuple-element.27), channel_id=1, source_target_pairs={{0,20},{16,0},{4,24},{20,4},{8,28},{24,8},{12,16},{28,12},{1,21},{... | collective-permute-start | bytes 208904 | tf_op jit(solution)/shard_map/ppermute | solution.py:303
  19.6 3.4 %collective-permute-start.3 = (f32[136,128]{1,0:T(8,128)S(1)}, f32[136,128]{1,0:T(8,128)S(1)}, u32[]{:S(2)}, u32[]{:S(2)}) collective-permute-start(f32[136,128]{1,0:T(8,128)S(1)} %get-tuple-element.24.refs_0_), channel_id=1, source_target_pairs={{0,16},{16,0},{1,17},{17,1},{2,18},{18,2},{3,19},{19,3},{4,20},{20... | collective-permute-start | bytes 208904 | tf_op jit(solution)/shard_map/ppermute | solution.py:300
  23.3 3.6 %collective-permute-start.7 = (bf16[8,2048]{1,0:T(8,128)(2,1)S(1)}, bf16[8,2048]{1,0:T(8,128)(2,1)S(1)}, u32[]{:S(2)}, u32[]{:S(2)}) collective-permute-start(bf16[8,2048]{1,0:T(8,128)(2,1)S(1)} %merge.1.attended), channel_id=1, source_target_pairs={{0,16},{16,0},{1,17},{17,1},{2,18},{18,2},{3,19},{19,3},{4,20},{20... | collective-permute-start | bytes 98312 | tf_op jit(solution)/shard_map/ppermute | solution.py:312
  28.7 5.1 %collective-permute-start.8 = (f32[8,1024]{1,0:T(8,128)S(1)}, f32[8,1024]{1,0:T(8,128)S(1)}, u32[]{:S(2)}, u32[]{:S(2)}) collective-permute-start(f32[8,1024]{1,0:T(8,128)S(1)} %get-tuple-element.28), channel_id=1, source_target_pairs={{0,1},{1,2},{2,3},{3,0},{4,5},{5,6},{6,7},{7,4},{8,9},{9,10},{10,1... | collective-permute-start | bytes 98312 | tf_op jit(solution)/shard_map/ppermute | solution.py:330
  30.2 3.9 %collective-permute-start.9 = (f32[8,1024]{1,0:T(8,128)S(1)}, f32[8,1024]{1,0:T(8,128)S(1)}, u32[]{:S(2)}, u32[]{:S(2)}) collective-permute-start(f32[8,1024]{1,0:T(8,128)S(1)} %get-tuple-element.29), channel_id=1, source_target_pairs={{0,2},{1,3},{2,0},{3,1},{4,6},{5,7},{6,4},{7,5},{8,10},{9,11},{10,... | collective-permute-start | bytes 98312 | tf_op jit(solution)/shard_map/ppermute | solution.py:330
  31.7 3.9 %collective-permute-start.10 = (f32[8,1024]{1,0:T(8,128)S(1)}, f32[8,1024]{1,0:T(8,128)S(1)}, u32[]{:S(2)}, u32[]{:S(2)}) collective-permute-start(f32[8,1024]{1,0:T(8,128)S(1)} %get-tuple-element.30), channel_id=1, source_target_pairs={{0,3},{1,0},{2,1},{3,2},{4,7},{5,4},{6,5},{7,6},{8,11},{9,8},{10,9... | collective-permute-start | bytes 98312 | tf_op jit(solution)/shard_map/ppermute | solution.py:330

commit v5 on v4

--- a/solution.py
+++ b/solution.py
@@ -18,6 +18,7 @@
 NEG = -1e30
 SCALE = 1.0 / math.sqrt(HD)
 PARTS = CAP + CAPP
+CHUNK = 8
 MIB = 2**20
 
 
@@ -83,51 +84,75 @@
     write_part(out, acc, top, total, held, per_held)
 
 
-def resident_part(qa, fresh_at, send, tables, maxp, group, kv, pages, sems, out, held, per_held):
+def resident_part(qa, fresh_at, send, tables, lengths, maxp, group, kv, pages, flags, listed, scores, sems, out, held, per_held):
     rows = qa.shape[0]
     slots = kv.shape[0]
-    copies = []
+    for i in range(slots):
+        flags[i] = 0
+    for o in range(send.shape[1]):
+        for i in range(send.shape[2]):
+            flags[jnp.where(send[1, o, i] == group, send[2, o, i], slots)] = 1
+    listed_count = jnp.int32(0)
     for r in range(rows):
         for e in range(maxp):
             slot = tables[r, e]
-            slot = jnp.where(slot < slots, slot, 0)
-            copy = pltpu.make_async_copy(kv.at[slot], pages.at[r, e], sems.at[r, e])
-            copy.start()
-            copies.append(copy)
+            tokens = jnp.minimum(lengths[0, r] - e * PAGE, PAGE)
+            here = jnp.logical_and(slot < slots, flags[jnp.minimum(slot, slots - 1)] == 0)
+            needed = jnp.logical_and(tokens > 0, here)
+            listed[0, listed_count] = slot
+            listed[1, listed_count] = r
+            listed[2, listed_count] = tokens
+            listed_count = listed_count + needed.astype(jnp.int32)
+    for i in range(CHUNK):
+        listed[0, listed_count + i] = 0
+        listed[1, listed_count + i] = 0
+        listed[2, listed_count + i] = 0
+    chunks = (listed_count + CHUNK - 1) // CHUNK
+
+    def page_copy(i):
+        return pltpu.make_async_copy(kv.at[listed[0, i]], pages.at[i], sems.at[i])
+
+    def start(c, _):
+        for i in range(CHUNK):
+            page_copy(c * CHUNK + i).start()
+        return 0
+
+    lax.fori_loop(0, chunks, start, 0)
     q = query_block(qa, held, per_held)
-    tab, cnt = entry_rows(qa, held, per_held, maxp)
     count = q.shape[0]
-    gone = tab >= slots
-    for o in range(send.shape[1]):
-        for i in range(send.shape[2]):
-            slot = jnp.where(send[1, o, i] == group, send[2, o, i], -1)
-            gone = jnp.logical_or(gone, tab == slot.astype(jnp.float32))
-    cnt = jnp.where(gone, 0.0, cnt)
     lane_row = lax.rem(lax.broadcasted_iota(jnp.int32, (1, count), 1), rows)
-    token = lax.broadcasted_iota(jnp.int32, (PAGE, count), 0).astype(jnp.float32)
+    token = lax.broadcasted_iota(jnp.int32, (PAGE, count), 0)
     fresh = qa[:, fresh_at : fresh_at + 2 * held * HD].astype(jnp.float32)
     fresh = jnp.concatenate([fresh, jnp.zeros_like(fresh)], 0).astype(jnp.bfloat16)
     own_mask = lax.broadcasted_iota(jnp.int32, (2 * rows, count), 0) == lane_row
-    own = dot(lanes_of(fresh, 0, held), q, 1, 1) * SCALE
-    own_top = jnp.max(jnp.where(own_mask, own, NEG), 0, keepdims=True)
-    tops, total, acc = own_top, 0.0, 0.0
-    for r in range(rows):
-        for e in range(maxp):
-            copies[r * maxp + e].wait()
-        valid = jnp.where(lane_row == r, cnt, 0.0)
-        mask = jnp.concatenate([token < valid[e : e + 1] for e in range(maxp)], 0)
-        keys = jnp.concatenate([lanes_of(pages.at[r, e], 0, held) for e in range(maxp)], 0)
-        values = jnp.concatenate([lanes_of(pages.at[r, e], 1, held) for e in range(maxp)], 0)
+    own = jnp.where(own_mask, dot(lanes_of(fresh, 0, held), q, 1, 1) * SCALE, NEG)
+
+    def score(c, top):
+        first = c * CHUNK
+        masks = []
+        for i in range(CHUNK):
+            page_copy(first + i).wait()
+            masks.append(token < jnp.where(lane_row == listed[1, first + i], listed[2, first + i], 0))
+        mask = jnp.concatenate(masks, 0)
+        keys = jnp.concatenate([lanes_of(pages.at[first + i], 0, held) for i in range(CHUNK)], 0)
         s = jnp.where(mask, dot(keys, q, 1, 1) * SCALE, NEG)
-        top = jnp.maximum(jnp.max(s, 0, keepdims=True), own_top)
-        p = jnp.where(mask, jnp.exp(s - top), 0.0)
-        total = total + jnp.sum(p, 0, keepdims=True)
-        tops = jnp.maximum(tops, top)
-        acc = acc + dot(p.astype(jnp.bfloat16), values, 0, 0)
-    lift = jnp.where(own_mask, jnp.exp(own - tops), 0.0)
-    total = total + jnp.sum(lift, 0, keepdims=True)
-    acc = acc + dot(lift.astype(jnp.bfloat16), lanes_of(fresh, 1, held), 0, 0)
-    write_part(out, acc, tops, total, held, per_held)
+        scores[c] = s
+        return jnp.maximum(top, jnp.max(s, 0, keepdims=True))
+
+    top = lax.fori_loop(0, chunks, score, jnp.max(own, 0, keepdims=True))
+
+    def weigh(c, carry):
+        total, acc = carry
+        first = c * CHUNK
+        p = jnp.exp(scores[c] - top)
+        values = jnp.concatenate([lanes_of(pages.at[first + i], 1, held) for i in range(CHUNK)], 0)
+        return total + jnp.sum(p, 0, keepdims=True), acc + dot(p.astype(jnp.bfloat16), values, 0, 0)
+
+    lift = jnp.exp(own - top)
+    total = jnp.sum(lift, 0, keepdims=True)
+    acc = dot(lift.astype(jnp.bfloat16), lanes_of(fresh, 1, held), 0, 0)
+    total, acc = lax.fori_loop(0, chunks, weigh, (total, acc))
+    write_part(out, acc, top, total, held, per_held)
 
 
 def list_pages(send, wanted, owner, target, slots, page_list, slot_list, base):
@@ -137,33 +162,27 @@
     at = jnp.int32(base)
     for i in range(send.shape[2]):
         hit = send[1, owner, i] == target
-
-        @pl.when(hit)
-        def _(at=at, i=i):
-            page_list[at] = send[0, owner, i]
-            slot_list[at] = send[2, owner, i]
-
+        page_list[at] = send[0, owner, i]
+        slot_list[at] = jnp.where(hit, send[2, owner, i], -1)
         at = at + hit.astype(jnp.int32)
     at = jnp.int32(base + CAP)
+    page_list[at] = 0
+    slot_list[at] = -1
     for i in range(wanted.shape[1]):
-        page = wanted[target, i]
-        first = owner * PRE_DEV
-        hit = jnp.logical_and(page >= first, page < first + PRE_DEV)
-
-        @pl.when(hit)
-        def _(at=at, i=i, page=page):
-            page_list[at] = page - owner * PRE_DEV
-            slot_list[at] = slots + i
-
+        page = wanted[target, i] - owner * PRE_DEV
+        hit = jnp.logical_and(page >= 0, page < PRE_DEV)
+        page_list[at] = jnp.where(hit, page, 0)
+        slot_list[at] = jnp.where(hit, slots + i, -1)
         at = at + hit.astype(jnp.int32)
 
 
-def first_kernel(held, per_held, groups, maxp, qa, send_hbm, wanted_hbm, tables_hbm, kv, *refs):
-    out, chosen, entries, pages, send, wanted, tables, page_list, slot_list, list_sems, chosen_sems, sems = refs
+def first_kernel(held, per_held, groups, maxp, qa, send_hbm, wanted_hbm, tables_hbm, lengths_hbm, kv, *refs):
+    out, chosen, entries, pages, scores, send, wanted, tables, lengths = refs[:9]
+    flags, listed, page_list, slot_list, list_sems, chosen_sems, sems = refs[9:]
     group = lax.axis_index("group")
     prefill = lax.axis_index("role") == 0
     fresh_at = held * per_held * HD + LANES
-    lists = ((send_hbm, send), (wanted_hbm, wanted), (tables_hbm, tables))
+    lists = ((send_hbm, send), (wanted_hbm, wanted), (tables_hbm, tables), (lengths_hbm, lengths))
     copies = [pltpu.make_async_copy(a, b, list_sems.at[i]) for i, (a, b) in enumerate(lists)]
     for copy in copies:
         copy.start()
@@ -191,7 +210,9 @@
 
     @pl.when(jnp.logical_not(prefill))
     def _():
-        resident_part(qa, fresh_at, send, tables, maxp, group, kv, pages, sems, out, held, per_held)
+        resident_part(
+            qa, fresh_at, send, tables, lengths, maxp, group, kv, pages, flags, listed, scores, sems, out, held, per_held
+        )
 
 
 def second_kernel(held, per_held, maxp, count, chosen, entries, *refs):
@@ -262,6 +283,8 @@
     hbm = pl.BlockSpec(memory_space=pltpu.HBM)
     page_shape = stored.shape[1:]
     chosen_count = groups * PARTS
+    read_count = -(-rows * maxp // CHUNK) * CHUNK
+    lists = [send, wanted, tables[0], lengths]
     mine, chosen, entries = pl.pallas_call(
         functools.partial(first_kernel, held, per_held, groups, maxp),
         out_shape=[
@@ -269,23 +292,27 @@
             jax.ShapeDtypeStruct((chosen_count,) + page_shape, jnp.bfloat16),
             jax.ShapeDtypeStruct((chosen_count, LANES), jnp.float32),
         ],
-        in_specs=[vmem, hbm, hbm, hbm, hbm],
+        in_specs=[vmem] + [hbm] * 5,
         out_specs=[vmem] * 3,
         scratch_shapes=[
-            pltpu.VMEM((rows, maxp) + page_shape, jnp.bfloat16),
+            pltpu.VMEM((read_count,) + page_shape, jnp.bfloat16),
+            pltpu.VMEM((read_count // CHUNK, CHUNK * PAGE, heads * rows), jnp.float32),
             pltpu.SMEM(send.shape, jnp.int32),
             pltpu.SMEM(wanted.shape, jnp.int32),
             pltpu.SMEM(tables.shape[1:], jnp.int32),
-            pltpu.SMEM((chosen_count,), jnp.int32),
-            pltpu.SMEM((chosen_count,), jnp.int32),
-            pltpu.SemaphoreType.DMA((3,)),
+            pltpu.SMEM(lengths.shape, jnp.int32),
+            pltpu.SMEM((slots + 1,), jnp.int32),
+            pltpu.SMEM((3, read_count + CHUNK), jnp.int32),
+            pltpu.SMEM((chosen_count + 1,), jnp.int32),
+            pltpu.SMEM((chosen_count + 1,), jnp.int32),
+            pltpu.SemaphoreType.DMA((len(lists),)),
             pltpu.SemaphoreType.DMA((chosen_count,)),
-            pltpu.SemaphoreType.DMA((rows, maxp)),
+            pltpu.SemaphoreType.DMA((read_count,)),
         ],
         compiler_params=pltpu.CompilerParams(vmem_limit_bytes=24 * MIB),
         cost_estimate=pl.CostEstimate(flops=4 * 10**9, bytes_accessed=12 * MIB, transcendentals=10**6),
         name="resident",
-    )(qa, *[pltpu.with_memory_space_constraint(x, pltpu.HBM) for x in (send, wanted, tables[0], stored)])
+    )(qa, *[pltpu.with_memory_space_constraint(x, pltpu.HBM) for x in lists + [stored]])
     count = groups - 1
     theirs = pl.pallas_call(
         functools.partial(second_kernel, held, per_held, maxp, count),

time: 36.2 us -> 32.7 us (0.903)
  starting transfers between devices: 19.5 us -> 16.2 us
    ppermute x3, starting transfers between devices: 6.65 us -> 3.34 us  [per_device(): parts.append(lax.ppermute(theirs[k - 1], ('role', 'group'), pairs))]
  transfers between devices with their start and end apart: 11 -> 11, of which waited for: 7 -> 7; matrix products, arithmetic and copies ran while one was open for 0% -> 0% of each run, Pallas kernels for 13% -> 15%
where the time goes in v5:
time: 32.7 us; the launch traced here: 32.9 us
  starting transfers between devices  16.2 us (50%)
  Pallas kernels  8.55 us (26%)
  waiting for transfers between devices  6.54 us (20%)
  other arithmetic  1.52 us (5%)
    ppermute x3, starting transfers between devices, per_device(): lax.ppermute(qa, ('role', 'group'), [pair for i in range(groups) for pair...  5.17 us
    ppermute x3, starting transfers between devices, per_device(): lax.ppermute(part, 'tp', [(i, (i + d) % tps) for i in range(tps)])  4.48 us
    pallas_call x1, Pallas kernels, per_device(): pl.pallas_call(functools.partial(first_kernel, held, per_held, groups, ma...  4.21 us
    ppermute x3, starting transfers between devices, per_device(): parts.append(lax.ppermute(theirs[k - 1], ('role', 'group'), pairs))  3.34 us
    ppermute x3, waiting for transfers between devices, per_device(): parts.append(lax.ppermute(theirs[k - 1], ('role', 'group'), pairs))  2.85 us
    ppermute x1, starting transfers between devices, per_device(): partner = lax.ppermute(attended, 'role', [(0, 1), (1, 0)])  2.74 us
    pallas_call x2, Pallas kernels, project(): pl.pallas_call(functools.partial(project_kernel, steps), out_shape=[jax.S...  2.37 us
    ppermute x3, waiting for transfers between devices, per_device(): lax.ppermute(part, 'tp', [(i, (i + d) % tps) for i in range(tps)])  1.82 us
  transfers between devices with their start and end apart: 11, of which 7 were waited for; matrix products, arithmetic and copies ran while one was open for 0% of the time, Pallas kernels for 15%

profile of v5, /device:TPU:0, one launch (start us, length us, event | category | flops | bytes accessed | tf_op | source)
XLA Modules:
  0.0 32.9 jit_solution(9399419909029218183)
XLA Ops:
  0.0 0.9 %fusion.qa = bf16[8,2688]{1,0:T(8,128)(2,1)S(1)} fusion(s32[1,8]{1,0:T(1,128)} %lengths_hbm.1, s32[8,8]{1,0:T(8,128)} %bitcast.9, bf16[8,512]{1,0:T(8,128)(2,1)} %bitcast.8, bf16[8,2048]{1,0:T(8,128)(2,1)} %bitcast.7), kind=kLoop, calls=%fused_computation.1 | loop fusion | flops 236544 | bytes 84256 | tf_op jit(solution)/shard_map/add | solution.py:274
  0.9 0.5 %collective-permute-start.2 = (bf16[8,2688]{1,0:T(8,128)(2,1)S(1)}, bf16[8,2688]{1,0:T(8,128)(2,1)S(1)}, u32[]{:S(2)}, u32[]{:S(2)}) collective-permute-start(bf16[8,2688]{1,0:T(8,128)(2,1)S(1)} %fusion.qa), channel_id=1, source_target_pairs={{16,12},{0,16},{20,0},{4,20},{24,4},{8,24},{28,8},{12,28},{17,13},... | collective-permute-start | bytes 129032 | tf_op jit(solution)/shard_map/ppermute | solution.py:276
  1.4 4.7 %collective-permute-start.1 = (bf16[8,2688]{1,0:T(8,128)(2,1)S(1)}, bf16[8,2688]{1,0:T(8,128)(2,1)S(1)}, u32[]{:S(2)}, u32[]{:S(2)}) collective-permute-start(bf16[8,2688]{1,0:T(8,128)(2,1)S(1)} %fusion.qa), channel_id=1, source_target_pairs={{16,8},{0,16},{20,12},{4,20},{24,0},{8,24},{28,4},{12,28},{17,9},{... | collective-permute-start | bytes 129032 | tf_op jit(solution)/shard_map/ppermute | solution.py:276
  6.1 4.2 %resident.1 = (f32[136,128]{1,0:T(8,128)S(1)}, bf16[24,128,512]{2,1,0:T(8,128)(2,1)S(1)}, f32[24,128]{1,0:T(8,128)S(1)}) custom-call(bf16[8,2688]{1,0:T(8,128)(2,1)S(1)} %fusion.qa, s32[3,4,12]{2,1,0:T(4,128)} %bitcast.12, s32[4,6]{1,0:T(4,128)} %wanted_hbm.1, s32[8,8]{1,0:T(8,128)} %bitcast.10, s32[1,8]{1,0:T(1,128)} %lengths_hbm.1, ...), custom_call_target="tpu_custom_call" | custom-call | flops 4000000000 | bytes 12582912 | tf_op jit(solution)/shard_map/resident/pallas_call | solution.py:288
  10.3 0.0 collective-permute-done.2.refs_2_
  10.3 0.0 collective-permute-done.1.refs_1_
  10.3 1.0 %collective-permute-done.refs_0_ = bf16[8,2688]{1,0:T(8,128)(2,1)S(1)} collective-permute-done((bf16[8,2688]{1,0:T(8,128)(2,1)S(1)}, bf16[8,2688]{1,0:T(8,128)(2,1)S(1)}, u32[]{:S(2)}, u32[]{:S(2)}) %collective-permute-start) | collective-permute-done | bytes 43040 | tf_op jit(solution)/shard_map/ppermute | solution.py:276
  11.3 1.7 %owned.1 = (f32[136,128]{1,0:T(8,128)S(1)}, f32[136,128]{1,0:T(8,128)S(1)}, f32[136,128]{1,0:T(8,128)S(1)}) custom-call(bf16[24,128,512]{2,1,0:T(8,128)(2,1)S(1)} %get-tuple-element.19.chosen, f32[24,128]{1,0:T(8,128)S(1)} %get-tuple-element.20.entries, bf16[8,2688]{1,0:T(8,128)(2,1)S(1)} %collective-permute-done.refs_0_, ...), custom_call_target="tpu_custom_call" | custom-call | flops 4000000000 | bytes 8388608 | tf_op jit(solution)/shard_map/owned/pallas_call | solution.py:317
  13.0 3.3 %collective-permute-start.4 = (f32[136,128]{1,0:T(8,128)S(1)}, f32[136,128]{1,0:T(8,128)S(1)}, u32[]{:S(2)}, u32[]{:S(2)}) collective-permute-start(f32[136,128]{1,0:T(8,128)S(1)} %get-tuple-element.25), channel_id=1, source_target_pairs={{0,28},{16,0},{4,16},{20,4},{8,20},{24,8},{12,24},{28,12},{1,29},{... | collective-permute-start | bytes 208904 | tf_op jit(solution)/shard_map/ppermute | solution.py:330
  16.3 0.5 %collective-permute-start.3 = (f32[136,128]{1,0:T(8,128)S(1)}, f32[136,128]{1,0:T(8,128)S(1)}, u32[]{:S(2)}, u32[]{:S(2)}) collective-permute-start(f32[136,128]{1,0:T(8,128)S(1)} %get-tuple-element.24.refs_0_), channel_id=1, source_target_pairs={{0,16},{16,0},{1,17},{17,1},{2,18},{18,2},{3,19},{19,3},{4,20},{20... | collective-permute-start | bytes 208904 | tf_op jit(solution)/shard_map/ppermute | solution.py:327
  16.8 1.4 %collective-permute-done.4.refs_2_ = f32[136,128]{1,0:T(8,128)S(1)} collective-permute-done((f32[136,128]{1,0:T(8,128)S(1)}, f32[136,128]{1,0:T(8,128)S(1)}, u32[]{:S(2)}, u32[]{:S(2)}) %collective-permute-start.4) | collective-permute-done | bytes 69664 | tf_op jit(solution)/shard_map/ppermute | solution.py:330
  18.3 0.7 %collective-permute-done.5.refs_3_ = f32[136,128]{1,0:T(8,128)S(1)} collective-permute-done((f32[136,128]{1,0:T(8,128)S(1)}, f32[136,128]{1,0:T(8,128)S(1)}, u32[]{:S(2)}, u32[]{:S(2)}) %collective-permute-start.5) | collective-permute-done | bytes 69664 | tf_op jit(solution)/shard_map/ppermute | solution.py:330
  18.9 0.7 %collective-permute-done.6.refs_4_ = f32[136,128]{1,0:T(8,128)S(1)} collective-permute-done((f32[136,128]{1,0:T(8,128)S(1)}, f32[136,128]{1,0:T(8,128)S(1)}, u32[]{:S(2)}, u32[]{:S(2)}) %collective-permute-start.6) | collective-permute-done | bytes 69664 | tf_op jit(solution)/shard_map/ppermute | solution.py:330
  19.7 0.3 merge.1.attended
  20.0 2.7 %collective-permute-start.7 = (bf16[8,2048]{1,0:T(8,128)(2,1)S(1)}, bf16[8,2048]{1,0:T(8,128)(2,1)S(1)}, u32[]{:S(2)}, u32[]{:S(2)}) collective-permute-start(bf16[8,2048]{1,0:T(8,128)(2,1)S(1)} %merge.1.attended), channel_id=1, source_target_pairs={{0,16},{16,0},{1,17},{17,1},{2,18},{18,2},{3,19},{19,3},{4,20},{20... | collective-permute-start | bytes 98312 | tf_op jit(solution)/shard_map/ppermute | solution.py:339
  22.8 0.9 %collective-permute-done.7.partner = bf16[8,2048]{1,0:T(8,128)(2,1)S(1)} collective-permute-done((bf16[8,2048]{1,0:T(8,128)(2,1)S(1)}, bf16[8,2048]{1,0:T(8,128)(2,1)S(1)}, u32[]{:S(2)}, u32[]{:S(2)}) %collective-permute-start.7) | collective-permute-done | bytes 32800 | tf_op jit(solution)/shard_map/ppermute | solution.py:339
  23.6 1.7 %project.1 = (f32[8,1024]{1,0:T(8,128)S(1)}, f32[8,1024]{1,0:T(8,128)S(1)}, f32[8,1024]{1,0:T(8,128)S(1)}) custom-call(bf16[8,2048]{1,0:T(8,128)(2,1)S(1)} %merge.1.attended, bf16[8,2048]{1,0:T(8,128)(2,1)S(1)} %collective-permute-done.7.partner, bf16[2048,4096]{1,0:T(8,128)(2,1)S(1)} %copy-done), custom_call_target="tpu_custom_call" | custom-call | flops 201326592 | bytes 12582912 | tf_op jit(solution)/shard_map/project/pallas_call | solution.py:343
  25.3 1.5 %collective-permute-start.8 = (f32[8,1024]{1,0:T(8,128)S(1)}, f32[8,1024]{1,0:T(8,128)S(1)}, u32[]{:S(2)}, u32[]{:S(2)}) collective-permute-start(f32[8,1024]{1,0:T(8,128)S(1)} %get-tuple-element.28), channel_id=1, source_target_pairs={{0,1},{1,2},{2,3},{3,0},{4,5},{5,6},{6,7},{7,4},{8,9},{9,10},{10,1... | collective-permute-start | bytes 98312 | tf_op jit(solution)/shard_map/ppermute | solution.py:357
  26.9 1.5 %collective-permute-start.9 = (f32[8,1024]{1,0:T(8,128)S(1)}, f32[8,1024]{1,0:T(8,128)S(1)}, u32[]{:S(2)}, u32[]{:S(2)}) collective-permute-start(f32[8,1024]{1,0:T(8,128)S(1)} %get-tuple-element.29), channel_id=1, source_target_pairs={{0,2},{1,3},{2,0},{3,1},{4,6},{5,7},{6,4},{7,5},{8,10},{9,11},{10,... | collective-permute-start | bytes 98312 | tf_op jit(solution)/shard_map/ppermute | solution.py:357
  28.4 1.4 %collective-permute-start.10 = (f32[8,1024]{1,0:T(8,128)S(1)}, f32[8,1024]{1,0:T(8,128)S(1)}, u32[]{:S(2)}, u32[]{:S(2)}) collective-permute-start(f32[8,1024]{1,0:T(8,128)S(1)} %get-tuple-element.30), channel_id=1, source_target_pairs={{0,3},{1,0},{2,1},{3,2},{4,7},{5,4},{6,5},{7,6},{8,11},{9,8},{10,9... | collective-permute-start | bytes 98312 | tf_op jit(solution)/shard_map/ppermute | solution.py:357
  29.8 0.6 %project_own.1 = f32[8,1024]{1,0:T(8,128)S(1)} custom-call(bf16[8,2048]{1,0:T(8,128)(2,1)S(1)} %merge.1.attended, bf16[8,2048]{1,0:T(8,128)(2,1)S(1)} %collective-permute-done.7.partner, bf16[2048,4096]{1,0:T(8,128)(2,1)S(1)} %copy-done), custom_call_target="tpu_custom_call" | custom-call | flops 67108864 | bytes 4194304 | tf_op jit(solution)/shard_map/project_own/pallas_call | solution.py:343
  30.5 0.3 collective-permute-done.9
  30.8 1.5 %collective-permute-done.10 = f32[8,1024]{1,0:T(8,128)S(1)} collective-permute-done((f32[8,1024]{1,0:T(8,128)S(1)}, f32[8,1024]{1,0:T(8,128)S(1)}, u32[]{:S(2)}, u32[]{:S(2)}) %collective-permute-start.10) | collective-permute-done | bytes 32800 | tf_op jit(solution)/shard_map/ppermute | solution.py:357
  32.3 0.6 %fusion.1 = bf16[1,8,1024]{2,1,0:T(8,128)(2,1)} fusion(f32[8,1024]{1,0:T(8,128)S(1)} %collective-permute-done.10, f32[8,1024]{1,0:T(8,128)S(1)} %collective-permute-done.9, f32[8,1024]{1,0:T(8,128)S(1)} %project_own.1, f32[8,1024]{1,0:T(8,128)S(1)} %collective-permute-done.8), kind=kLoop, calls=%fused_computation.3 | loop fusion | flops 32768 | bytes 147456 | tf_op jit(solution)/shard_map/broadcast_in_dim | solution.py:359
  (7 shorter events, 0.0 us)
Async XLA Ops:
  0.9 9.4 %collective-permute-start.2 = (bf16[8,2688]{1,0:T(8,128)(2,1)S(1)}, bf16[8,2688]{1,0:T(8,128)(2,1)S(1)}, u32[]{:S(2)}, u32[]{:S(2)}) collective-permute-start(bf16[8,2688]{1,0:T(8,128)(2,1)S(1)} %fusion.qa), channel_id=1, source_target_pairs={{16,12},{0,16},{20,0},{4,20},{24,4},{8,24},{28,8},{12,28},{17,13},... | collective-permute-start | bytes 129032 | tf_op jit(solution)/shard_map/ppermute | solution.py:276
  1.4 8.9 %collective-permute-start.1 = (bf16[8,2688]{1,0:T(8,128)(2,1)S(1)}, bf16[8,2688]{1,0:T(8,128)(2,1)S(1)}, u32[]{:S(2)}, u32[]{:S(2)}) collective-permute-start(bf16[8,2688]{1,0:T(8,128)(2,1)S(1)} %fusion.qa), channel_id=1, source_target_pairs={{16,8},{0,16},{20,12},{4,20},{24,0},{8,24},{28,4},{12,28},{17,9},{... | collective-permute-start | bytes 129032 | tf_op jit(solution)/shard_map/ppermute | solution.py:276
  6.1 5.2 %collective-permute-start = (bf16[8,2688]{1,0:T(8,128)(2,1)S(1)}, bf16[8,2688]{1,0:T(8,128)(2,1)S(1)}, u32[]{:S(2)}, u32[]{:S(2)}) collective-permute-start(bf16[8,2688]{1,0:T(8,128)(2,1)S(1)} %fusion.qa), channel_id=1, source_target_pairs={{16,4},{0,16},{20,8},{4,20},{24,12},{8,24},{28,0},{12,28},{17,5},{... | collective-permute-start | bytes 129032 | tf_op jit(solution)/shard_map/ppermute | solution.py:276
  6.1 17.5 %copy-start = (bf16[2048,4096]{1,0:T(8,128)(2,1)S(1)}, bf16[2048,4096]{1,0:T(8,128)(2,1)}, u32[]{:S(2)}) copy-start(bf16[2048,4096]{1,0:T(8,128)(2,1)} %weight.3) | copy-start | bytes 50331652
  13.0 5.3 %collective-permute-start.4 = (f32[136,128]{1,0:T(8,128)S(1)}, f32[136,128]{1,0:T(8,128)S(1)}, u32[]{:S(2)}, u32[]{:S(2)}) collective-permute-start(f32[136,128]{1,0:T(8,128)S(1)} %get-tuple-element.25), channel_id=1, source_target_pairs={{0,28},{16,0},{4,16},{20,4},{8,20},{24,8},{12,24},{28,12},{1,29},{... | collective-permute-start | bytes 208904 | tf_op jit(solution)/shard_map/ppermute | solution.py:330
  16.3 2.6 %collective-permute-start.5 = (f32[136,128]{1,0:T(8,128)S(1)}, f32[136,128]{1,0:T(8,128)S(1)}, u32[]{:S(2)}, u32[]{:S(2)}) collective-permute-start(f32[136,128]{1,0:T(8,128)S(1)} %get-tuple-element.26), channel_id=1, source_target_pairs={{0,24},{16,0},{4,28},{20,4},{8,16},{24,8},{12,20},{28,12},{1,25},{... | collective-permute-start | bytes 208904 | tf_op jit(solution)/shard_map/ppermute | solution.py:330
  16.3 3.4 %collective-permute-start.6 = (f32[136,128]{1,0:T(8,128)S(1)}, f32[136,128]{1,0:T(8,128)S(1)}, u32[]{:S(2)}, u32[]{:S(2)}) collective-permute-start(f32[136,128]{1,0:T(8,128)S(1)} %get-tuple-element.27), channel_id=1, source_target_pairs={{0,20},{16,0},{4,24},{20,4},{8,28},{24,8},{12,16},{28,12},{1,21},{... | collective-permute-start | bytes 208904 | tf_op jit(solution)/shard_map/ppermute | solution.py:330
  16.3 3.4 %collective-permute-start.3 = (f32[136,128]{1,0:T(8,128)S(1)}, f32[136,128]{1,0:T(8,128)S(1)}, u32[]{:S(2)}, u32[]{:S(2)}) collective-permute-start(f32[136,128]{1,0:T(8,128)S(1)} %get-tuple-element.24.refs_0_), channel_id=1, source_target_pairs={{0,16},{16,0},{1,17},{17,1},{2,18},{18,2},{3,19},{19,3},{4,20},{20... | collective-permute-start | bytes 208904 | tf_op jit(solution)/shard_map/ppermute | solution.py:327
  20.0 3.6 %collective-permute-start.7 = (bf16[8,2048]{1,0:T(8,128)(2,1)S(1)}, bf16[8,2048]{1,0:T(8,128)(2,1)S(1)}, u32[]{:S(2)}, u32[]{:S(2)}) collective-permute-start(bf16[8,2048]{1,0:T(8,128)(2,1)S(1)} %merge.1.attended), channel_id=1, source_target_pairs={{0,16},{16,0},{1,17},{17,1},{2,18},{18,2},{3,19},{19,3},{4,20},{20... | collective-permute-start | bytes 98312 | tf_op jit(solution)/shard_map/ppermute | solution.py:339
  25.3 5.1 %collective-permute-start.8 = (f32[8,1024]{1,0:T(8,128)S(1)}, f32[8,1024]{1,0:T(8,128)S(1)}, u32[]{:S(2)}, u32[]{:S(2)}) collective-permute-start(f32[8,1024]{1,0:T(8,128)S(1)} %get-tuple-element.28), channel_id=1, source_target_pairs={{0,1},{1,2},{2,3},{3,0},{4,5},{5,6},{6,7},{7,4},{8,9},{9,10},{10,1... | collective-permute-start | bytes 98312 | tf_op jit(solution)/shard_map/ppermute | solution.py:357
  26.9 3.9 %collective-permute-start.9 = (f32[8,1024]{1,0:T(8,128)S(1)}, f32[8,1024]{1,0:T(8,128)S(1)}, u32[]{:S(2)}, u32[]{:S(2)}) collective-permute-start(f32[8,1024]{1,0:T(8,128)S(1)} %get-tuple-element.29), channel_id=1, source_target_pairs={{0,2},{1,3},{2,0},{3,1},{4,6},{5,7},{6,4},{7,5},{8,10},{9,11},{10,... | collective-permute-start | bytes 98312 | tf_op jit(solution)/shard_map/ppermute | solution.py:357
  28.4 3.9 %collective-permute-start.10 = (f32[8,1024]{1,0:T(8,128)S(1)}, f32[8,1024]{1,0:T(8,128)S(1)}, u32[]{:S(2)}, u32[]{:S(2)}) collective-permute-start(f32[8,1024]{1,0:T(8,128)S(1)} %get-tuple-element.30), channel_id=1, source_target_pairs={{0,3},{1,0},{2,1},{3,2},{4,7},{5,4},{6,5},{7,6},{8,11},{9,8},{10,9... | collective-permute-start | bytes 98312 | tf_op jit(solution)/shard_map/ppermute | solution.py:357

commit v6 on v5

--- a/solution.py
+++ b/solution.py
@@ -19,6 +19,7 @@
 SCALE = 1.0 / math.sqrt(HD)
 PARTS = CAP + CAPP
 CHUNK = 8
+BLOCK = 8
 MIB = 2**20
 
 
@@ -84,40 +85,9 @@
     write_part(out, acc, top, total, held, per_held)
 
 
-def resident_part(qa, fresh_at, send, tables, lengths, maxp, group, kv, pages, flags, listed, scores, sems, out, held, per_held):
+def resident_part(qa, fresh_at, lists_ready, send, tables, lengths, maxp, group, kv, pages, flags, listed, sems, out, held, per_held):
     rows = qa.shape[0]
     slots = kv.shape[0]
-    for i in range(slots):
-        flags[i] = 0
-    for o in range(send.shape[1]):
-        for i in range(send.shape[2]):
-            flags[jnp.where(send[1, o, i] == group, send[2, o, i], slots)] = 1
-    listed_count = jnp.int32(0)
-    for r in range(rows):
-        for e in range(maxp):
-            slot = tables[r, e]
-            tokens = jnp.minimum(lengths[0, r] - e * PAGE, PAGE)
-            here = jnp.logical_and(slot < slots, flags[jnp.minimum(slot, slots - 1)] == 0)
-            needed = jnp.logical_and(tokens > 0, here)
-            listed[0, listed_count] = slot
-            listed[1, listed_count] = r
-            listed[2, listed_count] = tokens
-            listed_count = listed_count + needed.astype(jnp.int32)
-    for i in range(CHUNK):
-        listed[0, listed_count + i] = 0
-        listed[1, listed_count + i] = 0
-        listed[2, listed_count + i] = 0
-    chunks = (listed_count + CHUNK - 1) // CHUNK
-
-    def page_copy(i):
-        return pltpu.make_async_copy(kv.at[listed[0, i]], pages.at[i], sems.at[i])
-
-    def start(c, _):
-        for i in range(CHUNK):
-            page_copy(c * CHUNK + i).start()
-        return 0
-
-    lax.fori_loop(0, chunks, start, 0)
     q = query_block(qa, held, per_held)
     count = q.shape[0]
     lane_row = lax.rem(lax.broadcasted_iota(jnp.int32, (1, count), 1), rows)
@@ -126,32 +96,71 @@
     fresh = jnp.concatenate([fresh, jnp.zeros_like(fresh)], 0).astype(jnp.bfloat16)
     own_mask = lax.broadcasted_iota(jnp.int32, (2 * rows, count), 0) == lane_row
     own = jnp.where(own_mask, dot(lanes_of(fresh, 0, held), q, 1, 1) * SCALE, NEG)
-
-    def score(c, top):
-        first = c * CHUNK
-        masks = []
-        for i in range(CHUNK):
-            page_copy(first + i).wait()
-            masks.append(token < jnp.where(lane_row == listed[1, first + i], listed[2, first + i], 0))
-        mask = jnp.concatenate(masks, 0)
-        keys = jnp.concatenate([lanes_of(pages.at[first + i], 0, held) for i in range(CHUNK)], 0)
-        s = jnp.where(mask, dot(keys, q, 1, 1) * SCALE, NEG)
-        scores[c] = s
-        return jnp.maximum(top, jnp.max(s, 0, keepdims=True))
-
-    top = lax.fori_loop(0, chunks, score, jnp.max(own, 0, keepdims=True))
-
-    def weigh(c, carry):
-        total, acc = carry
-        first = c * CHUNK
-        p = jnp.exp(scores[c] - top)
-        values = jnp.concatenate([lanes_of(pages.at[first + i], 1, held) for i in range(CHUNK)], 0)
-        return total + jnp.sum(p, 0, keepdims=True), acc + dot(p.astype(jnp.bfloat16), values, 0, 0)
-
-    lift = jnp.exp(own - top)
-    total = jnp.sum(lift, 0, keepdims=True)
-    acc = dot(lift.astype(jnp.bfloat16), lanes_of(fresh, 1, held), 0, 0)
-    total, acc = lax.fori_loop(0, chunks, weigh, (total, acc))
+    own_top = jnp.max(own, 0, keepdims=True)
+    lift = jnp.exp(own - own_top)
+    own_total = jnp.sum(lift, 0, keepdims=True)
+    own_acc = dot(lift.astype(jnp.bfloat16), lanes_of(fresh, 1, held), 0, 0)
+    for i in range(slots):
+        flags[i] = 0
+
+    lists_ready()
+    for o in range(send.shape[1]):
+        for i in range(send.shape[2]):
+            flags[jnp.where(send[1, o, i] == group, send[2, o, i], slots)] = 1
+
+    def page_copy(slot, i):
+        return pltpu.make_async_copy(kv.at[slot], pages.at[i], sems.at[i])
+
+    listed_count = jnp.int32(0)
+    for r in range(rows):
+        length = lengths[0, r]
+        for e in range(maxp):
+            slot = tables[r, e]
+            tokens = jnp.minimum(length - e * PAGE, PAGE)
+            here = jnp.logical_and(slot < slots, flags[jnp.minimum(slot, slots - 1)] == 0)
+            needed = jnp.logical_and(tokens > 0, here)
+            listed[0, listed_count] = r
+            listed[1, listed_count] = tokens
+
+            @pl.when(needed)
+            def _(slot=slot, at=listed_count):
+                page_copy(slot, at).start()
+
+            listed_count = listed_count + needed.astype(jnp.int32)
+    chunks = (listed_count + CHUNK - 1) // CHUNK
+
+    def fill(i, _):
+        listed[0, i] = 0
+        listed[1, i] = 0
+        page_copy(0, i).start()
+        return 0
+
+    lax.fori_loop(listed_count, chunks * CHUNK, fill, 0)
+
+    def step(c, carry):
+        old_top, total, acc = carry
+        blocks = [c * CHUNK + b for b in range(0, CHUNK, BLOCK)]
+        scores, top = [], old_top
+        for first in blocks:
+            masks = []
+            for i in range(BLOCK):
+                masks.append(token < jnp.where(lane_row == listed[0, first + i], listed[1, first + i], 0))
+            for i in range(BLOCK):
+                page_copy(0, first + i).wait()
+            keys = jnp.concatenate([lanes_of(pages.at[first + i], 0, held) for i in range(BLOCK)], 0)
+            scores.append(jnp.where(jnp.concatenate(masks, 0), dot(keys, q, 1, 1) * SCALE, NEG))
+            top = jnp.maximum(top, jnp.max(scores[-1], 0, keepdims=True))
+        fade = jnp.exp(old_top - top)
+        total = total * fade
+        acc = acc * jnp.broadcast_to(fade, (8, count)).T[:, :1]
+        for first, s in zip(blocks, scores):
+            p = jnp.exp(s - top)
+            total = total + jnp.sum(p, 0, keepdims=True)
+            values = jnp.concatenate([lanes_of(pages.at[first + i], 1, held) for i in range(BLOCK)], 0)
+            acc = acc + dot(p.astype(jnp.bfloat16), values, 0, 0)
+        return top, total, acc
+
+    top, total, acc = lax.fori_loop(0, chunks, step, (own_top, own_total, own_acc))
     write_part(out, acc, top, total, held, per_held)
 
 
@@ -177,8 +186,8 @@
 
 
 def first_kernel(held, per_held, groups, maxp, qa, send_hbm, wanted_hbm, tables_hbm, lengths_hbm, kv, *refs):
-    out, chosen, entries, pages, scores, send, wanted, tables, lengths = refs[:9]
-    flags, listed, page_list, slot_list, list_sems, chosen_sems, sems = refs[9:]
+    out, chosen, entries, pages, send, wanted, tables, lengths = refs[:8]
+    flags, listed, page_list, slot_list, list_sems, chosen_sems, sems = refs[8:]
     group = lax.axis_index("group")
     prefill = lax.axis_index("role") == 0
     fresh_at = held * per_held * HD + LANES
@@ -186,11 +195,14 @@
     copies = [pltpu.make_async_copy(a, b, list_sems.at[i]) for i, (a, b) in enumerate(lists)]
     for copy in copies:
         copy.start()
-    for copy in copies:
-        copy.wait()
+
+    def lists_ready():
+        for copy in copies:
+            copy.wait()
 
     @pl.when(prefill)
     def _():
+        lists_ready()
         copies = []
         for k in range(groups):
             target = lax.rem(group - k + groups, groups)
@@ -211,12 +223,12 @@
     @pl.when(jnp.logical_not(prefill))
     def _():
         resident_part(
-            qa, fresh_at, send, tables, lengths, maxp, group, kv, pages, flags, listed, scores, sems, out, held, per_held
+            qa, fresh_at, lists_ready, send, tables, lengths, maxp, group, kv, pages, flags, listed, sems, out, held, per_held
         )
 
 
 def second_kernel(held, per_held, maxp, count, chosen, entries, *refs):
-    qas, outs = refs[:count], refs[count:]
+    qas, outs = refs[:count][::-1], refs[count:]
 
     @pl.when(lax.axis_index("role") == 0)
     def _():
@@ -242,12 +254,11 @@
 
 
 def project_kernel(steps, attended, partner, weight, *outs):
-    tps = lax.axis_size("tp")
     share = outs[0].shape[1]
     here = jnp.where(lax.axis_index("role") == 0, partner[...].astype(jnp.float32), attended[...].astype(jnp.float32))
     here = here.astype(jnp.bfloat16)
     for d, out in zip(steps, outs):
-        first = lax.rem(lax.axis_index("tp") + d, tps) * share
+        first = lax.bitwise_xor(lax.axis_index("tp"), d) * share
         columns = pl.ds(pl.multiple_of(first, LANES), share)
         out[...] = jnp.dot(here, weight[:, columns], preferred_element_type=jnp.float32)
 
@@ -272,12 +283,10 @@
     low = jnp.bitwise_and(place(lengths, wide + maxp + rows), 7)
     integers = place(tables[0], wide) + high + low
     qa = place(queries[0], 0) + place(new_kv[0], fresh_at) + integers.astype(jnp.bfloat16)
-    asked = [
-        lax.ppermute(
-            qa, ("role", "group"), [pair for i in range(groups) for pair in ((groups + i, (i + k) % groups), (i, groups + i))]
-        )
-        for k in range(1, groups)
-    ]
+    asked = []
+    for k in range(1, groups):
+        pairs = [pair for i in range(groups) for pair in ((groups + i, (i + k) % groups), (i, groups + i))]
+        asked.append(lax.ppermute(qa, ("role", "group"), pairs))
     part_shape = jax.ShapeDtypeStruct((heads * rows + 8, HD), jnp.float32)
     vmem = pl.BlockSpec(memory_space=pltpu.VMEM)
     hbm = pl.BlockSpec(memory_space=pltpu.HBM)
@@ -296,13 +305,12 @@
         out_specs=[vmem] * 3,
         scratch_shapes=[
             pltpu.VMEM((read_count,) + page_shape, jnp.bfloat16),
-            pltpu.VMEM((read_count // CHUNK, CHUNK * PAGE, heads * rows), jnp.float32),
             pltpu.SMEM(send.shape, jnp.int32),
             pltpu.SMEM(wanted.shape, jnp.int32),
             pltpu.SMEM(tables.shape[1:], jnp.int32),
             pltpu.SMEM(lengths.shape, jnp.int32),
             pltpu.SMEM((slots + 1,), jnp.int32),
-            pltpu.SMEM((3, read_count + CHUNK), jnp.int32),
+            pltpu.SMEM((2, read_count), jnp.int32),
             pltpu.SMEM((chosen_count + 1,), jnp.int32),
             pltpu.SMEM((chosen_count + 1,), jnp.int32),
             pltpu.SemaphoreType.DMA((len(lists),)),
@@ -310,9 +318,9 @@
             pltpu.SemaphoreType.DMA((read_count,)),
         ],
         compiler_params=pltpu.CompilerParams(vmem_limit_bytes=24 * MIB),
-        cost_estimate=pl.CostEstimate(flops=4 * 10**9, bytes_accessed=12 * MIB, transcendentals=10**6),
         name="resident",
     )(qa, *[pltpu.with_memory_space_constraint(x, pltpu.HBM) for x in lists + [stored]])
+    out_weight, chosen, entries, mine = lax.optimization_barrier((out_weight, chosen, entries, mine))
     count = groups - 1
     theirs = pl.pallas_call(
         functools.partial(second_kernel, held, per_held, maxp, count),
@@ -322,7 +330,7 @@
         compiler_params=pltpu.CompilerParams(vmem_limit_bytes=16 * MIB),
         cost_estimate=pl.CostEstimate(flops=4 * 10**9, bytes_accessed=8 * MIB, transcendentals=10**6),
         name="owned",
-    )(chosen, entries, *asked)
+    )(chosen, entries, *reversed(asked))
     mine, theirs = lax.optimization_barrier((mine, theirs))
     parts = [mine, lax.ppermute(mine, "role", [(0, 1), (1, 0)])]
     for k in range(1, groups):
@@ -354,7 +362,7 @@
 
     steps = list(range(1, tps))
     sent = project(steps, "project")
-    arrived = [lax.ppermute(part, "tp", [(i, (i + d) % tps) for i in range(tps)]) for d, part in zip(steps, sent)]
+    arrived = [lax.ppermute(part, "tp", [(i, i ^ d) for i in range(tps)]) for d, part in zip(steps, sent)]
     total = functools.reduce(jnp.add, arrived, project([0], "project_own")[0])
     return total.astype(jnp.bfloat16)[None]
 

time: 32.7 us -> 31.9 us (0.976); the launches traced: 32.9 us -> 31.4 us
  starting transfers between devices: 16.2 us -> 14.2 us
  waiting for transfers between devices: 6.54 us -> 6.99 us
    ppermute x6, starting transfers between devices: 9.64 us -> 7.71 us  [the longest x3 4.21 us: per_device(): asked.append(lax.ppermute(qa, ('role', 'group'), pairs))]
    ppermute x6, waiting for transfers between devices: 2.83 us -> 3.7 us  [the longest x3 3.7 us: per_device(): lax.ppermute(part, 'tp', [(i, i ^ d) for i in range(tps)])]
    ppermute x1, starting transfers between devices: 0.51 us -> 0.01 us  [per_device(): parts = [mine, lax.ppermute(mine, 'role', [(0, 1), (1, 0)])]]
    ppermute x3, starting transfers between devices: 3.34 us -> 3.77 us  [per_device(): parts.append(lax.ppermute(theirs[k - 1], ('role', 'group'), pairs))]
    ppermute x3, waiting for transfers between devices: 2.85 us -> 2.43 us  [per_device(): parts.append(lax.ppermute(theirs[k - 1], ('role', 'group'), pairs))]
  transfers between devices with their start and end apart: 11 -> 11, of which waited for: 7 -> 6; matrix products, arithmetic and copies ran while one was open for 0% -> 0% of each run, Pallas kernels for 15% -> 15%
where the time goes in v6:
time: 31.9 us; the launch traced here: 31.4 us
  starting transfers between devices  14.2 us (45%)
  Pallas kernels  8.56 us (27%)
  waiting for transfers between devices  6.99 us (22%)
  other arithmetic  1.52 us (5%)
    ppermute x3, starting transfers between devices, per_device(): asked.append(lax.ppermute(qa, ('role', 'group'), pairs))  4.21 us
    pallas_call x1, Pallas kernels, per_device(): pl.pallas_call(functools.partial(first_kernel, held, per_held, groups, ma...  4.2 us
    ppermute x3, starting transfers between devices, per_device(): parts.append(lax.ppermute(theirs[k - 1], ('role', 'group'), pairs))  3.77 us
    ppermute x3, waiting for transfers between devices, per_device(): lax.ppermute(part, 'tp', [(i, i ^ d) for i in range(tps)])  3.7 us
    ppermute x3, starting transfers between devices, per_device(): lax.ppermute(part, 'tp', [(i, i ^ d) for i in range(tps)])  3.5 us
    ppermute x1, starting transfers between devices, per_device(): partner = lax.ppermute(attended, 'role', [(0, 1), (1, 0)])  2.74 us
    ppermute x3, waiting for transfers between devices, per_device(): parts.append(lax.ppermute(theirs[k - 1], ('role', 'group'), pairs))  2.43 us
    pallas_call x2, Pallas kernels, project(): pl.pallas_call(functools.partial(project_kernel, steps), out_shape=[jax.S...  2.37 us
  transfers between devices with their start and end apart: 11, of which 6 were waited for; matrix products, arithmetic and copies ran while one was open for 0% of the time, Pallas kernels for 15%

profile of v6, /device:TPU:0, one launch (start us, length us, event | category | flops | bytes accessed | tf_op | source)
XLA Modules:
  0.0 31.4 jit_solution(8282352365318659464)
XLA Ops:
  0.0 0.9 %fusion.qa = bf16[8,2688]{1,0:T(8,128)(2,1)S(1)} fusion(s32[1,8]{1,0:T(1,128)} %lengths_hbm.1, s32[8,8]{1,0:T(8,128)} %bitcast.9, bf16[8,512]{1,0:T(8,128)(2,1)} %bitcast.11, bf16[8,2048]{1,0:T(8,128)(2,1)} %bitcast.8), kind=kLoop, calls=%fused_computation.1 | loop fusion | flops 236544 | bytes 84256 | tf_op jit(solution)/shard_map/add | solution.py:285
  0.9 0.5 %collective-permute-start.2 = (bf16[8,2688]{1,0:T(8,128)(2,1)S(1)}, bf16[8,2688]{1,0:T(8,128)(2,1)S(1)}, u32[]{:S(2)}, u32[]{:S(2)}) collective-permute-start(bf16[8,2688]{1,0:T(8,128)(2,1)S(1)} %fusion.qa), channel_id=1, source_target_pairs={{16,4},{0,16},{20,8},{4,20},{24,12},{8,24},{28,0},{12,28},{17,5},{... | collective-permute-start | bytes 129032 | tf_op jit(solution)/shard_map/ppermute | solution.py:289
  1.4 2.7 %collective-permute-start.1 = (bf16[8,2688]{1,0:T(8,128)(2,1)S(1)}, bf16[8,2688]{1,0:T(8,128)(2,1)S(1)}, u32[]{:S(2)}, u32[]{:S(2)}) collective-permute-start(bf16[8,2688]{1,0:T(8,128)(2,1)S(1)} %fusion.qa), channel_id=1, source_target_pairs={{16,8},{0,16},{20,12},{4,20},{24,0},{8,24},{28,4},{12,28},{17,9},{... | collective-permute-start | bytes 129032 | tf_op jit(solution)/shard_map/ppermute | solution.py:289
  4.0 1.1 %collective-permute-start = (bf16[8,2688]{1,0:T(8,128)(2,1)S(1)}, bf16[8,2688]{1,0:T(8,128)(2,1)S(1)}, u32[]{:S(2)}, u32[]{:S(2)}) collective-permute-start(bf16[8,2688]{1,0:T(8,128)(2,1)S(1)} %fusion.qa), channel_id=1, source_target_pairs={{16,12},{0,16},{20,0},{4,20},{24,4},{8,24},{28,8},{12,28},{17,13},... | collective-permute-start | bytes 129032 | tf_op jit(solution)/shard_map/ppermute | solution.py:289
  5.1 4.2 %resident.1 = (f32[136,128]{1,0:T(8,128)S(1)}, bf16[24,128,512]{2,1,0:T(8,128)(2,1)S(1)}, f32[24,128]{1,0:T(8,128)S(1)}) custom-call(bf16[8,2688]{1,0:T(8,128)(2,1)S(1)} %fusion.qa, s32[3,4,12]{2,1,0:T(4,128)} %bitcast.12, s32[4,6]{1,0:T(4,128)} %wanted_hbm.1, s32[8,8]{1,0:T(8,128)} %bitcast.10, s32[1,8]{1,0:T(1,128)} %lengths_hbm.1, ...), custom_call_target="tpu_custom_call" | custom-call | tf_op jit(solution)/shard_map/resident/pallas_call | solution.py:297
  9.3 0.0 collective-permute-done.2.refs_2_
  9.3 0.0 collective-permute-done.1.refs_1_
  9.4 1.7 %owned.1 = (f32[136,128]{1,0:T(8,128)S(1)}, f32[136,128]{1,0:T(8,128)S(1)}, f32[136,128]{1,0:T(8,128)S(1)}) custom-call(bf16[24,128,512]{2,1,0:T(8,128)(2,1)S(1)} %get-tuple-element.26.chosen, f32[24,128]{1,0:T(8,128)S(1)} %get-tuple-element.27.entries, bf16[8,2688]{1,0:T(8,128)(2,1)S(1)} %collective-permute-done.refs_0_, ...), custom_call_target="tpu_custom_call" | custom-call | flops 4000000000 | bytes 8388608 | tf_op jit(solution)/shard_map/owned/pallas_call | solution.py:325
  11.0 2.8 %collective-permute-start.4 = (f32[136,128]{1,0:T(8,128)S(1)}, f32[136,128]{1,0:T(8,128)S(1)}, u32[]{:S(2)}, u32[]{:S(2)}) collective-permute-start(f32[136,128]{1,0:T(8,128)S(1)} %get-tuple-element.32), channel_id=1, source_target_pairs={{0,28},{16,0},{4,16},{20,4},{8,20},{24,8},{12,24},{28,12},{1,29},{... | collective-permute-start | bytes 208904 | tf_op jit(solution)/shard_map/ppermute | solution.py:338
  13.9 0.9 %collective-permute-start.6 = (f32[136,128]{1,0:T(8,128)S(1)}, f32[136,128]{1,0:T(8,128)S(1)}, u32[]{:S(2)}, u32[]{:S(2)}) collective-permute-start(f32[136,128]{1,0:T(8,128)S(1)} %get-tuple-element.34), channel_id=1, source_target_pairs={{0,20},{16,0},{4,24},{20,4},{8,28},{24,8},{12,16},{28,12},{1,21},{... | collective-permute-start | bytes 208904 | tf_op jit(solution)/shard_map/ppermute | solution.py:338
  14.8 1.0 %collective-permute-done.4.refs_2_ = f32[136,128]{1,0:T(8,128)S(1)} collective-permute-done((f32[136,128]{1,0:T(8,128)S(1)}, f32[136,128]{1,0:T(8,128)S(1)}, u32[]{:S(2)}, u32[]{:S(2)}) %collective-permute-start.4) | collective-permute-done | bytes 69664 | tf_op jit(solution)/shard_map/ppermute | solution.py:338
  15.8 0.7 %collective-permute-done.5.refs_3_ = f32[136,128]{1,0:T(8,128)S(1)} collective-permute-done((f32[136,128]{1,0:T(8,128)S(1)}, f32[136,128]{1,0:T(8,128)S(1)}, u32[]{:S(2)}, u32[]{:S(2)}) %collective-permute-start.5) | collective-permute-done | bytes 69664 | tf_op jit(solution)/shard_map/ppermute | solution.py:338
  16.5 0.7 %collective-permute-done.6.refs_4_ = f32[136,128]{1,0:T(8,128)S(1)} collective-permute-done((f32[136,128]{1,0:T(8,128)S(1)}, f32[136,128]{1,0:T(8,128)S(1)}, u32[]{:S(2)}, u32[]{:S(2)}) %collective-permute-start.6) | collective-permute-done | bytes 69664 | tf_op jit(solution)/shard_map/ppermute | solution.py:338
  17.2 0.3 merge.1.attended
  17.6 2.7 %collective-permute-start.7 = (bf16[8,2048]{1,0:T(8,128)(2,1)S(1)}, bf16[8,2048]{1,0:T(8,128)(2,1)S(1)}, u32[]{:S(2)}, u32[]{:S(2)}) collective-permute-start(bf16[8,2048]{1,0:T(8,128)(2,1)S(1)} %merge.1.attended), channel_id=1, source_target_pairs={{0,16},{16,0},{1,17},{17,1},{2,18},{18,2},{3,19},{19,3},{4,20},{20... | collective-permute-start | bytes 98312 | tf_op jit(solution)/shard_map/ppermute | solution.py:347
  20.3 0.9 %collective-permute-done.7.partner = bf16[8,2048]{1,0:T(8,128)(2,1)S(1)} collective-permute-done((bf16[8,2048]{1,0:T(8,128)(2,1)S(1)}, bf16[8,2048]{1,0:T(8,128)(2,1)S(1)}, u32[]{:S(2)}, u32[]{:S(2)}) %collective-permute-start.7) | collective-permute-done | bytes 32800 | tf_op jit(solution)/shard_map/ppermute | solution.py:347
  21.2 1.7 %project.1 = (f32[8,1024]{1,0:T(8,128)S(1)}, f32[8,1024]{1,0:T(8,128)S(1)}, f32[8,1024]{1,0:T(8,128)S(1)}) custom-call(bf16[8,2048]{1,0:T(8,128)(2,1)S(1)} %merge.1.attended, bf16[8,2048]{1,0:T(8,128)(2,1)S(1)} %collective-permute-done.7.partner, bf16[2048,4096]{1,0:T(8,128)(2,1)S(1)} %copy-done), custom_call_target="tpu_custom_call" | custom-call | flops 201326592 | bytes 12582912 | tf_op jit(solution)/shard_map/project/pallas_call | solution.py:351
  22.9 1.5 %collective-permute-start.8 = (f32[8,1024]{1,0:T(8,128)S(1)}, f32[8,1024]{1,0:T(8,128)S(1)}, u32[]{:S(2)}, u32[]{:S(2)}) collective-permute-start(f32[8,1024]{1,0:T(8,128)S(1)} %get-tuple-element.36), channel_id=1, source_target_pairs={{0,1},{1,0},{2,3},{3,2},{4,5},{5,4},{6,7},{7,6},{8,9},{9,8},{10,11... | collective-permute-start | bytes 98312 | tf_op jit(solution)/shard_map/ppermute | solution.py:365
  24.4 1.5 %collective-permute-start.9 = (f32[8,1024]{1,0:T(8,128)S(1)}, f32[8,1024]{1,0:T(8,128)S(1)}, u32[]{:S(2)}, u32[]{:S(2)}) collective-permute-start(f32[8,1024]{1,0:T(8,128)S(1)} %get-tuple-element.37), channel_id=1, source_target_pairs={{0,2},{1,3},{2,0},{3,1},{4,6},{5,7},{6,4},{7,5},{8,10},{9,11},{10,... | collective-permute-start | bytes 98312 | tf_op jit(solution)/shard_map/ppermute | solution.py:365
  25.9 0.5 %collective-permute-start.10 = (f32[8,1024]{1,0:T(8,128)S(1)}, f32[8,1024]{1,0:T(8,128)S(1)}, u32[]{:S(2)}, u32[]{:S(2)}) collective-permute-start(f32[8,1024]{1,0:T(8,128)S(1)} %get-tuple-element.38), channel_id=1, source_target_pairs={{0,3},{1,2},{2,1},{3,0},{4,7},{5,6},{6,5},{7,4},{8,11},{9,10},{10,... | collective-permute-start | bytes 98312 | tf_op jit(solution)/shard_map/ppermute | solution.py:365
  26.4 0.6 %project_own.1 = f32[8,1024]{1,0:T(8,128)S(1)} custom-call(bf16[8,2048]{1,0:T(8,128)(2,1)S(1)} %merge.1.attended, bf16[8,2048]{1,0:T(8,128)(2,1)S(1)} %collective-permute-done.7.partner, bf16[2048,4096]{1,0:T(8,128)(2,1)S(1)} %copy-done), custom_call_target="tpu_custom_call" | custom-call | flops 67108864 | bytes 4194304 | tf_op jit(solution)/shard_map/project_own/pallas_call | solution.py:351
  27.0 1.3 %collective-permute-done.9 = f32[8,1024]{1,0:T(8,128)S(1)} collective-permute-done((f32[8,1024]{1,0:T(8,128)S(1)}, f32[8,1024]{1,0:T(8,128)S(1)}, u32[]{:S(2)}, u32[]{:S(2)}) %collective-permute-start.9) | collective-permute-done | bytes 32800 | tf_op jit(solution)/shard_map/ppermute | solution.py:365
  28.3 2.4 %collective-permute-done.10 = f32[8,1024]{1,0:T(8,128)S(1)} collective-permute-done((f32[8,1024]{1,0:T(8,128)S(1)}, f32[8,1024]{1,0:T(8,128)S(1)}, u32[]{:S(2)}, u32[]{:S(2)}) %collective-permute-start.10) | collective-permute-done | bytes 32800 | tf_op jit(solution)/shard_map/ppermute | solution.py:365
  30.7 0.6 %fusion.1 = bf16[1,8,1024]{2,1,0:T(8,128)(2,1)} fusion(f32[8,1024]{1,0:T(8,128)S(1)} %collective-permute-done.10, f32[8,1024]{1,0:T(8,128)S(1)} %collective-permute-done.9, f32[8,1024]{1,0:T(8,128)S(1)} %project_own.1, f32[8,1024]{1,0:T(8,128)S(1)} %collective-permute-done.8), kind=kLoop, calls=%fused_computation.3 | loop fusion | flops 32768 | bytes 147456 | tf_op jit(solution)/shard_map/broadcast_in_dim | solution.py:367
  (7 shorter events, 0.0 us)
Async XLA Ops:
  0.9 8.4 %collective-permute-start.2 = (bf16[8,2688]{1,0:T(8,128)(2,1)S(1)}, bf16[8,2688]{1,0:T(8,128)(2,1)S(1)}, u32[]{:S(2)}, u32[]{:S(2)}) collective-permute-start(bf16[8,2688]{1,0:T(8,128)(2,1)S(1)} %fusion.qa), channel_id=1, source_target_pairs={{16,4},{0,16},{20,8},{4,20},{24,12},{8,24},{28,0},{12,28},{17,5},{... | collective-permute-start | bytes 129032 | tf_op jit(solution)/shard_map/ppermute | solution.py:289
  1.4 8.0 %collective-permute-start.1 = (bf16[8,2688]{1,0:T(8,128)(2,1)S(1)}, bf16[8,2688]{1,0:T(8,128)(2,1)S(1)}, u32[]{:S(2)}, u32[]{:S(2)}) collective-permute-start(bf16[8,2688]{1,0:T(8,128)(2,1)S(1)} %fusion.qa), channel_id=1, source_target_pairs={{16,8},{0,16},{20,12},{4,20},{24,0},{8,24},{28,4},{12,28},{17,9},{... | collective-permute-start | bytes 129032 | tf_op jit(solution)/shard_map/ppermute | solution.py:289
  4.0 5.3 %collective-permute-start = (bf16[8,2688]{1,0:T(8,128)(2,1)S(1)}, bf16[8,2688]{1,0:T(8,128)(2,1)S(1)}, u32[]{:S(2)}, u32[]{:S(2)}) collective-permute-start(bf16[8,2688]{1,0:T(8,128)(2,1)S(1)} %fusion.qa), channel_id=1, source_target_pairs={{16,12},{0,16},{20,0},{4,20},{24,4},{8,24},{28,8},{12,28},{17,13},... | collective-permute-start | bytes 129032 | tf_op jit(solution)/shard_map/ppermute | solution.py:289
  5.1 16.1 %copy-start = (bf16[2048,4096]{1,0:T(8,128)(2,1)S(1)}, bf16[2048,4096]{1,0:T(8,128)(2,1)}, u32[]{:S(2)}) copy-start(bf16[2048,4096]{1,0:T(8,128)(2,1)} %weight.1) | copy-start | bytes 50331652
  11.0 4.8 %collective-permute-start.4 = (f32[136,128]{1,0:T(8,128)S(1)}, f32[136,128]{1,0:T(8,128)S(1)}, u32[]{:S(2)}, u32[]{:S(2)}) collective-permute-start(f32[136,128]{1,0:T(8,128)S(1)} %get-tuple-element.32), channel_id=1, source_target_pairs={{0,28},{16,0},{4,16},{20,4},{8,20},{24,8},{12,24},{28,12},{1,29},{... | collective-permute-start | bytes 208904 | tf_op jit(solution)/shard_map/ppermute | solution.py:338
  13.9 2.6 %collective-permute-start.5 = (f32[136,128]{1,0:T(8,128)S(1)}, f32[136,128]{1,0:T(8,128)S(1)}, u32[]{:S(2)}, u32[]{:S(2)}) collective-permute-start(f32[136,128]{1,0:T(8,128)S(1)} %get-tuple-element.33), channel_id=1, source_target_pairs={{0,24},{16,0},{4,28},{20,4},{8,16},{24,8},{12,20},{28,12},{1,25},{... | collective-permute-start | bytes 208904 | tf_op jit(solution)/shard_map/ppermute | solution.py:338
  13.9 3.4 %collective-permute-start.6 = (f32[136,128]{1,0:T(8,128)S(1)}, f32[136,128]{1,0:T(8,128)S(1)}, u32[]{:S(2)}, u32[]{:S(2)}) collective-permute-start(f32[136,128]{1,0:T(8,128)S(1)} %get-tuple-element.34), channel_id=1, source_target_pairs={{0,20},{16,0},{4,24},{20,4},{8,28},{24,8},{12,16},{28,12},{1,21},{... | collective-permute-start | bytes 208904 | tf_op jit(solution)/shard_map/ppermute | solution.py:338
  14.8 2.4 %collective-permute-start.3 = (f32[136,128]{1,0:T(8,128)S(1)}, f32[136,128]{1,0:T(8,128)S(1)}, u32[]{:S(2)}, u32[]{:S(2)}) collective-permute-start(f32[136,128]{1,0:T(8,128)S(1)} %get-tuple-element.31.refs_0_), channel_id=1, source_target_pairs={{0,16},{16,0},{1,17},{17,1},{2,18},{18,2},{3,19},{19,3},{4,20},{20... | collective-permute-start | bytes 208904 | tf_op jit(solution)/shard_map/ppermute | solution.py:335
  17.6 3.6 %collective-permute-start.7 = (bf16[8,2048]{1,0:T(8,128)(2,1)S(1)}, bf16[8,2048]{1,0:T(8,128)(2,1)S(1)}, u32[]{:S(2)}, u32[]{:S(2)}) collective-permute-start(bf16[8,2048]{1,0:T(8,128)(2,1)S(1)} %merge.1.attended), channel_id=1, source_target_pairs={{0,16},{16,0},{1,17},{17,1},{2,18},{18,2},{3,19},{19,3},{4,20},{20... | collective-permute-start | bytes 98312 | tf_op jit(solution)/shard_map/ppermute | solution.py:347
  22.9 4.2 %collective-permute-start.8 = (f32[8,1024]{1,0:T(8,128)S(1)}, f32[8,1024]{1,0:T(8,128)S(1)}, u32[]{:S(2)}, u32[]{:S(2)}) collective-permute-start(f32[8,1024]{1,0:T(8,128)S(1)} %get-tuple-element.36), channel_id=1, source_target_pairs={{0,1},{1,0},{2,3},{3,2},{4,5},{5,4},{6,7},{7,6},{8,9},{9,8},{10,11... | collective-permute-start | bytes 98312 | tf_op jit(solution)/shard_map/ppermute | solution.py:365
  24.4 3.9 %collective-permute-start.9 = (f32[8,1024]{1,0:T(8,128)S(1)}, f32[8,1024]{1,0:T(8,128)S(1)}, u32[]{:S(2)}, u32[]{:S(2)}) collective-permute-start(f32[8,1024]{1,0:T(8,128)S(1)} %get-tuple-element.37), channel_id=1, source_target_pairs={{0,2},{1,3},{2,0},{3,1},{4,6},{5,7},{6,4},{7,5},{8,10},{9,11},{10,... | collective-permute-start | bytes 98312 | tf_op jit(solution)/shard_map/ppermute | solution.py:365
  25.9 4.8 %collective-permute-start.10 = (f32[8,1024]{1,0:T(8,128)S(1)}, f32[8,1024]{1,0:T(8,128)S(1)}, u32[]{:S(2)}, u32[]{:S(2)}) collective-permute-start(f32[8,1024]{1,0:T(8,128)S(1)} %get-tuple-element.38), channel_id=1, source_target_pairs={{0,3},{1,2},{2,1},{3,0},{4,7},{5,6},{6,5},{7,4},{8,11},{9,10},{10,... | collective-permute-start | bytes 98312 | tf_op jit(solution)/shard_map/ppermute | solution.py:365

commit v7 on v6

--- a/solution.py
+++ b/solution.py
@@ -254,11 +254,12 @@
 
 
 def project_kernel(steps, attended, partner, weight, *outs):
+    tps = lax.axis_size("tp")
     share = outs[0].shape[1]
     here = jnp.where(lax.axis_index("role") == 0, partner[...].astype(jnp.float32), attended[...].astype(jnp.float32))
     here = here.astype(jnp.bfloat16)
     for d, out in zip(steps, outs):
-        first = lax.bitwise_xor(lax.axis_index("tp"), d) * share
+        first = lax.rem(lax.axis_index("tp") + d, tps) * share
         columns = pl.ds(pl.multiple_of(first, LANES), share)
         out[...] = jnp.dot(here, weight[:, columns], preferred_element_type=jnp.float32)
 
@@ -328,7 +329,7 @@
         in_specs=[vmem] * (2 + count),
         out_specs=[vmem] * count,
         compiler_params=pltpu.CompilerParams(vmem_limit_bytes=16 * MIB),
-        cost_estimate=pl.CostEstimate(flops=4 * 10**9, bytes_accessed=8 * MIB, transcendentals=10**6),
+        cost_estimate=pl.CostEstimate(flops=4 * 10**10, bytes_accessed=8 * MIB, transcendentals=10**6),
         name="owned",
     )(chosen, entries, *reversed(asked))
     mine, theirs = lax.optimization_barrier((mine, theirs))
@@ -362,7 +363,7 @@
 
     steps = list(range(1, tps))
     sent = project(steps, "project")
-    arrived = [lax.ppermute(part, "tp", [(i, i ^ d) for i in range(tps)]) for d, part in zip(steps, sent)]
+    arrived = [lax.ppermute(part, "tp", [(i, (i + d) % tps) for i in range(tps)]) for d, part in zip(steps, sent)]
     total = functools.reduce(jnp.add, arrived, project([0], "project_own")[0])
     return total.astype(jnp.bfloat16)[None]
 

time: 31.9 us -> 30.7 us (0.962); the launches traced: 31.4 us -> 30.8 us
  waiting for transfers between devices: 6.99 us -> 5.56 us
  starting transfers between devices: 14.2 us -> 15.5 us
  Pallas kernels: 8.56 us -> 8.11 us
    ppermute x3, waiting for transfers between devices: 3.7 us -> 1.84 us  [per_device(): lax.ppermute(part, 'tp', [(i, (i + d) % tps) for i in range(tps)])]
    ppermute x3, starting transfers between devices: 3.5 us -> 4.46 us  [per_device(): lax.ppermute(part, 'tp', [(i, (i + d) % tps) for i in range(tps)])]
    pallas_call x1, Pallas kernels: 4.2 us -> 3.74 us  [per_device(): pl.pallas_call(functools.partial(first_kernel, held, per_held, groups, ma...]
    ppermute x3, waiting for transfers between devices: 2.43 us -> 2.85 us  [per_device(): parts.append(lax.ppermute(theirs[k - 1], ('role', 'group'), pairs))]
    ppermute x1, starting transfers between devices: 0.01 us -> 0.41 us  [per_device(): parts = [mine, lax.ppermute(mine, 'role', [(0, 1), (1, 0)])]]
  transfers between devices with their start and end apart: 11 -> 11, of which waited for: 6 -> 6; matrix products, arithmetic and copies ran while one was open for 0% -> 0% of each run, Pallas kernels for 15% -> 14%
where the time goes in v7:
time: 30.7 us; the launch traced here: 30.8 us
  starting transfers between devices  15.5 us (50%)
  Pallas kernels  8.11 us (26%)
  waiting for transfers between devices  5.56 us (18%)
  other arithmetic  1.52 us (5%)
    ppermute x3, starting transfers between devices, per_device(): lax.ppermute(part, 'tp', [(i, (i + d) % tps) for i in range(tps)])  4.46 us
    ppermute x3, starting transfers between devices, per_device(): asked.append(lax.ppermute(qa, ('role', 'group'), pairs))  4.21 us
    pallas_call x1, Pallas kernels, per_device(): pl.pallas_call(functools.partial(first_kernel, held, per_held, groups, ma...  3.74 us
    ppermute x3, starting transfers between devices, per_device(): parts.append(lax.ppermute(theirs[k - 1], ('role', 'group'), pairs))  3.67 us
    ppermute x3, waiting for transfers between devices, per_device(): parts.append(lax.ppermute(theirs[k - 1], ('role', 'group'), pairs))  2.85 us
    ppermute x1, starting transfers between devices, per_device(): partner = lax.ppermute(attended, 'role', [(0, 1), (1, 0)])  2.74 us
    pallas_call x2, Pallas kernels, project(): pl.pallas_call(functools.partial(project_kernel, steps), out_shape=[jax.S...  2.38 us
    ppermute x3, waiting for transfers between devices, per_device(): lax.ppermute(part, 'tp', [(i, (i + d) % tps) for i in range(tps)])  1.84 us
  transfers between devices with their start and end apart: 11, of which 6 were waited for; matrix products, arithmetic and copies ran while one was open for 0% of the time, Pallas kernels for 14%

profile of v7, /device:TPU:0, one launch (start us, length us, event | category | flops | bytes accessed | tf_op | source)
XLA Modules:
  0.0 30.8 jit_solution(1130471558503150183)
XLA Ops:
  0.0 0.9 %fusion.qa = bf16[8,2688]{1,0:T(8,128)(2,1)S(1)} fusion(s32[1,8]{1,0:T(1,128)} %lengths_hbm.1, s32[8,8]{1,0:T(8,128)} %bitcast.11, bf16[8,512]{1,0:T(8,128)(2,1)} %bitcast.13, bf16[8,2048]{1,0:T(8,128)(2,1)} %bitcast.10), kind=kLoop, calls=%fused_computation.1 | loop fusion | flops 236544 | bytes 84256 | tf_op jit(solution)/shard_map/add | solution.py:286
  0.9 0.5 %collective-permute-start.2 = (bf16[8,2688]{1,0:T(8,128)(2,1)S(1)}, bf16[8,2688]{1,0:T(8,128)(2,1)S(1)}, u32[]{:S(2)}, u32[]{:S(2)}) collective-permute-start(bf16[8,2688]{1,0:T(8,128)(2,1)S(1)} %fusion.qa), channel_id=1, source_target_pairs={{16,4},{0,16},{20,8},{4,20},{24,12},{8,24},{28,0},{12,28},{17,5},{... | collective-permute-start | bytes 129032 | tf_op jit(solution)/shard_map/ppermute | solution.py:290
  1.4 2.7 %collective-permute-start.1 = (bf16[8,2688]{1,0:T(8,128)(2,1)S(1)}, bf16[8,2688]{1,0:T(8,128)(2,1)S(1)}, u32[]{:S(2)}, u32[]{:S(2)}) collective-permute-start(bf16[8,2688]{1,0:T(8,128)(2,1)S(1)} %fusion.qa), channel_id=1, source_target_pairs={{16,8},{0,16},{20,12},{4,20},{24,0},{8,24},{28,4},{12,28},{17,9},{... | collective-permute-start | bytes 129032 | tf_op jit(solution)/shard_map/ppermute | solution.py:290
  4.0 1.1 %collective-permute-start = (bf16[8,2688]{1,0:T(8,128)(2,1)S(1)}, bf16[8,2688]{1,0:T(8,128)(2,1)S(1)}, u32[]{:S(2)}, u32[]{:S(2)}) collective-permute-start(bf16[8,2688]{1,0:T(8,128)(2,1)S(1)} %fusion.qa), channel_id=1, source_target_pairs={{16,12},{0,16},{20,0},{4,20},{24,4},{8,24},{28,8},{12,28},{17,13},... | collective-permute-start | bytes 129032 | tf_op jit(solution)/shard_map/ppermute | solution.py:290
  5.1 3.7 %resident.1 = (f32[136,128]{1,0:T(8,128)S(1)}, bf16[24,128,512]{2,1,0:T(8,128)(2,1)S(1)}, f32[24,128]{1,0:T(8,128)S(1)}) custom-call(bf16[8,2688]{1,0:T(8,128)(2,1)S(1)} %fusion.qa, s32[3,4,12]{2,1,0:T(4,128)} %bitcast.14, s32[4,6]{1,0:T(4,128)} %wanted_hbm.1, s32[8,8]{1,0:T(8,128)} %bitcast.12, s32[1,8]{1,0:T(1,128)} %lengths_hbm.1, ...), custom_call_target="tpu_custom_call" | custom-call | tf_op jit(solution)/shard_map/resident/pallas_call | solution.py:298
  8.9 0.0 slice-start
  8.9 1.7 %owned.1 = (f32[136,128]{1,0:T(8,128)S(1)}, f32[136,128]{1,0:T(8,128)S(1)}, f32[136,128]{1,0:T(8,128)S(1)}) custom-call(bf16[24,128,512]{2,1,0:T(8,128)(2,1)S(1)} %get-tuple-element.26.chosen, f32[24,128]{1,0:T(8,128)S(1)} %get-tuple-element.27.entries, bf16[8,2688]{1,0:T(8,128)(2,1)S(1)} %collective-permute-done.refs_0_, ...), custom_call_target="tpu_custom_call" | custom-call | flops 40000000000 | bytes 8388608 | tf_op jit(solution)/shard_map/owned/pallas_call | solution.py:326
  10.6 3.6 %collective-permute-start.4 = (f32[136,128]{1,0:T(8,128)S(1)}, f32[136,128]{1,0:T(8,128)S(1)}, u32[]{:S(2)}, u32[]{:S(2)}) collective-permute-start(f32[136,128]{1,0:T(8,128)S(1)} %get-tuple-element.32), channel_id=1, source_target_pairs={{0,28},{16,0},{4,16},{20,4},{8,20},{24,8},{12,24},{28,12},{1,29},{... | collective-permute-start | bytes 208904 | tf_op jit(solution)/shard_map/ppermute | solution.py:339
  14.2 0.1 collective-permute-start.6
  14.3 0.4 %collective-permute-start.3 = (f32[136,128]{1,0:T(8,128)S(1)}, f32[136,128]{1,0:T(8,128)S(1)}, u32[]{:S(2)}, u32[]{:S(2)}) collective-permute-start(f32[136,128]{1,0:T(8,128)S(1)} %get-tuple-element.31.refs_0_), channel_id=1, source_target_pairs={{0,16},{16,0},{1,17},{17,1},{2,18},{18,2},{3,19},{19,3},{4,20},{20... | collective-permute-start | bytes 208904 | tf_op jit(solution)/shard_map/ppermute | solution.py:336
  14.7 1.4 %collective-permute-done.4.refs_2_ = f32[136,128]{1,0:T(8,128)S(1)} collective-permute-done((f32[136,128]{1,0:T(8,128)S(1)}, f32[136,128]{1,0:T(8,128)S(1)}, u32[]{:S(2)}, u32[]{:S(2)}) %collective-permute-start.4) | collective-permute-done | bytes 69664 | tf_op jit(solution)/shard_map/ppermute | solution.py:339
  16.1 0.7 %collective-permute-done.5.refs_3_ = f32[136,128]{1,0:T(8,128)S(1)} collective-permute-done((f32[136,128]{1,0:T(8,128)S(1)}, f32[136,128]{1,0:T(8,128)S(1)}, u32[]{:S(2)}, u32[]{:S(2)}) %collective-permute-start.5) | collective-permute-done | bytes 69664 | tf_op jit(solution)/shard_map/ppermute | solution.py:339
  16.8 0.7 %collective-permute-done.6.refs_4_ = f32[136,128]{1,0:T(8,128)S(1)} collective-permute-done((f32[136,128]{1,0:T(8,128)S(1)}, f32[136,128]{1,0:T(8,128)S(1)}, u32[]{:S(2)}, u32[]{:S(2)}) %collective-permute-start.6) | collective-permute-done | bytes 69664 | tf_op jit(solution)/shard_map/ppermute | solution.py:339
  17.6 0.3 %merge.1.attended = bf16[8,2048]{1,0:T(8,128)(2,1)S(1)} custom-call(f32[136,128]{1,0:T(8,128)S(1)} %get-tuple-element.31.refs_0_, f32[136,128]{1,0:T(8,128)S(1)} %collective-permute-done.3.refs_1_, f32[136,128]{1,0:T(8,128)S(1)} %collective-permute-done.4.refs_2_, f32[136,128]{1,0:T(8,128)S(1)} %collective-permute-done.5.refs_3_, ...), custom_call_target="tpu_custom_call" | custom-call | tf_op jit(solution)/shard_map/merge/pallas_call | solution.py:340
  17.9 2.7 %collective-permute-start.7 = (bf16[8,2048]{1,0:T(8,128)(2,1)S(1)}, bf16[8,2048]{1,0:T(8,128)(2,1)S(1)}, u32[]{:S(2)}, u32[]{:S(2)}) collective-permute-start(bf16[8,2048]{1,0:T(8,128)(2,1)S(1)} %merge.1.attended), channel_id=1, source_target_pairs={{0,16},{16,0},{1,17},{17,1},{2,18},{18,2},{3,19},{19,3},{4,20},{20... | collective-permute-start | bytes 98312 | tf_op jit(solution)/shard_map/ppermute | solution.py:348
  20.6 0.9 %collective-permute-done.7.partner = bf16[8,2048]{1,0:T(8,128)(2,1)S(1)} collective-permute-done((bf16[8,2048]{1,0:T(8,128)(2,1)S(1)}, bf16[8,2048]{1,0:T(8,128)(2,1)S(1)}, u32[]{:S(2)}, u32[]{:S(2)}) %collective-permute-start.7) | collective-permute-done | bytes 32800 | tf_op jit(solution)/shard_map/ppermute | solution.py:348
  21.5 1.7 %project.1 = (f32[8,1024]{1,0:T(8,128)S(1)}, f32[8,1024]{1,0:T(8,128)S(1)}, f32[8,1024]{1,0:T(8,128)S(1)}) custom-call(bf16[8,2048]{1,0:T(8,128)(2,1)S(1)} %merge.1.attended, bf16[8,2048]{1,0:T(8,128)(2,1)S(1)} %collective-permute-done.7.partner, bf16[2048,4096]{1,0:T(8,128)(2,1)S(1)} %bitcast.8), custom_call_target="tpu_custom_call" | custom-call | flops 201326592 | bytes 12582912 | tf_op jit(solution)/shard_map/project/pallas_call | solution.py:352
  23.2 1.5 %collective-permute-start.8 = (f32[8,1024]{1,0:T(8,128)S(1)}, f32[8,1024]{1,0:T(8,128)S(1)}, u32[]{:S(2)}, u32[]{:S(2)}) collective-permute-start(f32[8,1024]{1,0:T(8,128)S(1)} %get-tuple-element.36), channel_id=1, source_target_pairs={{0,1},{1,2},{2,3},{3,0},{4,5},{5,6},{6,7},{7,4},{8,9},{9,10},{10,1... | collective-permute-start | bytes 98312 | tf_op jit(solution)/shard_map/ppermute | solution.py:366
  24.8 1.5 %collective-permute-start.9 = (f32[8,1024]{1,0:T(8,128)S(1)}, f32[8,1024]{1,0:T(8,128)S(1)}, u32[]{:S(2)}, u32[]{:S(2)}) collective-permute-start(f32[8,1024]{1,0:T(8,128)S(1)} %get-tuple-element.37), channel_id=1, source_target_pairs={{0,2},{1,3},{2,0},{3,1},{4,6},{5,7},{6,4},{7,5},{8,10},{9,11},{10,... | collective-permute-start | bytes 98312 | tf_op jit(solution)/shard_map/ppermute | solution.py:366
  26.3 1.4 %collective-permute-start.10 = (f32[8,1024]{1,0:T(8,128)S(1)}, f32[8,1024]{1,0:T(8,128)S(1)}, u32[]{:S(2)}, u32[]{:S(2)}) collective-permute-start(f32[8,1024]{1,0:T(8,128)S(1)} %get-tuple-element.38), channel_id=1, source_target_pairs={{0,3},{1,0},{2,1},{3,2},{4,7},{5,4},{6,5},{7,6},{8,11},{9,8},{10,9... | collective-permute-start | bytes 98312 | tf_op jit(solution)/shard_map/ppermute | solution.py:366
  27.7 0.6 %project_own.1 = f32[8,1024]{1,0:T(8,128)S(1)} custom-call(bf16[8,2048]{1,0:T(8,128)(2,1)S(1)} %merge.1.attended, bf16[8,2048]{1,0:T(8,128)(2,1)S(1)} %collective-permute-done.7.partner, bf16[2048,4096]{1,0:T(8,128)(2,1)S(1)} %bitcast.8), custom_call_target="tpu_custom_call" | custom-call | flops 67108864 | bytes 4194304 | tf_op jit(solution)/shard_map/project_own/pallas_call | solution.py:352
  28.3 0.3 %collective-permute-done.9 = f32[8,1024]{1,0:T(8,128)S(1)} collective-permute-done((f32[8,1024]{1,0:T(8,128)S(1)}, f32[8,1024]{1,0:T(8,128)S(1)}, u32[]{:S(2)}, u32[]{:S(2)}) %collective-permute-start.9) | collective-permute-done | bytes 32800 | tf_op jit(solution)/shard_map/ppermute | solution.py:366
  28.7 1.5 %collective-permute-done.10 = f32[8,1024]{1,0:T(8,128)S(1)} collective-permute-done((f32[8,1024]{1,0:T(8,128)S(1)}, f32[8,1024]{1,0:T(8,128)S(1)}, u32[]{:S(2)}, u32[]{:S(2)}) %collective-permute-start.10) | collective-permute-done | bytes 32800 | tf_op jit(solution)/shard_map/ppermute | solution.py:366
  30.2 0.6 %fusion.1 = bf16[1,8,1024]{2,1,0:T(8,128)(2,1)} fusion(f32[8,1024]{1,0:T(8,128)S(1)} %collective-permute-done.10, f32[8,1024]{1,0:T(8,128)S(1)} %collective-permute-done.9, f32[8,1024]{1,0:T(8,128)S(1)} %project_own.1, f32[8,1024]{1,0:T(8,128)S(1)} %collective-permute-done.8), kind=kLoop, calls=%fused_computation.3 | loop fusion | flops 32768 | bytes 147456 | tf_op jit(solution)/shard_map/broadcast_in_dim | solution.py:368
  (14 shorter events, 0.0 us)
Async XLA Ops:
  0.9 8.0 %collective-permute-start.2 = (bf16[8,2688]{1,0:T(8,128)(2,1)S(1)}, bf16[8,2688]{1,0:T(8,128)(2,1)S(1)}, u32[]{:S(2)}, u32[]{:S(2)}) collective-permute-start(bf16[8,2688]{1,0:T(8,128)(2,1)S(1)} %fusion.qa), channel_id=1, source_target_pairs={{16,4},{0,16},{20,8},{4,20},{24,12},{8,24},{28,0},{12,28},{17,5},{... | collective-permute-start | bytes 129032 | tf_op jit(solution)/shard_map/ppermute | solution.py:290
  1.4 7.6 %collective-permute-start.1 = (bf16[8,2688]{1,0:T(8,128)(2,1)S(1)}, bf16[8,2688]{1,0:T(8,128)(2,1)S(1)}, u32[]{:S(2)}, u32[]{:S(2)}) collective-permute-start(bf16[8,2688]{1,0:T(8,128)(2,1)S(1)} %fusion.qa), channel_id=1, source_target_pairs={{16,8},{0,16},{20,12},{4,20},{24,0},{8,24},{28,4},{12,28},{17,9},{... | collective-permute-start | bytes 129032 | tf_op jit(solution)/shard_map/ppermute | solution.py:290
  4.0 4.9 %collective-permute-start = (bf16[8,2688]{1,0:T(8,128)(2,1)S(1)}, bf16[8,2688]{1,0:T(8,128)(2,1)S(1)}, u32[]{:S(2)}, u32[]{:S(2)}) collective-permute-start(bf16[8,2688]{1,0:T(8,128)(2,1)S(1)} %fusion.qa), channel_id=1, source_target_pairs={{16,12},{0,16},{20,0},{4,20},{24,4},{8,24},{28,8},{12,28},{17,13},... | collective-permute-start | bytes 129032 | tf_op jit(solution)/shard_map/ppermute | solution.py:290
  8.9 12.6 %slice-start = ((s8[16777216]{0:T(1024)(128)(4,1)}), s8[4194304]{0:T(1024)(128)(4,1)S(1)}, s32[]{:S(2)}) async-start(s8[16777216]{0:T(1024)(128)(4,1)} %bitcast.7), calls=%async_computation | async-start | bytes 8388608
  8.9 12.6 %slice-start.1 = ((s8[16777216]{0:T(1024)(128)(4,1)}), s8[4194304]{0:T(1024)(128)(4,1)S(1)}, s32[]{:S(2)}) async-start(s8[16777216]{0:T(1024)(128)(4,1)} %bitcast.7), calls=%async_computation.1 | async-start | bytes 8388608
  8.9 12.6 %slice-start.2 = ((s8[16777216]{0:T(1024)(128)(4,1)}), s8[4194304]{0:T(1024)(128)(4,1)S(1)}, s32[]{:S(2)}) async-start(s8[16777216]{0:T(1024)(128)(4,1)} %bitcast.7), calls=%async_computation.2 | async-start | bytes 8388608
  8.9 12.6 %slice-start.3 = ((s8[16777216]{0:T(1024)(128)(4,1)}), s8[4194304]{0:T(1024)(128)(4,1)S(1)}, s32[]{:S(2)}) async-start(s8[16777216]{0:T(1024)(128)(4,1)} %bitcast.7), calls=%async_computation.3 | async-start | bytes 8388608
  10.6 5.5 %collective-permute-start.4 = (f32[136,128]{1,0:T(8,128)S(1)}, f32[136,128]{1,0:T(8,128)S(1)}, u32[]{:S(2)}, u32[]{:S(2)}) collective-permute-start(f32[136,128]{1,0:T(8,128)S(1)} %get-tuple-element.32), channel_id=1, source_target_pairs={{0,28},{16,0},{4,16},{20,4},{8,20},{24,8},{12,24},{28,12},{1,29},{... | collective-permute-start | bytes 208904 | tf_op jit(solution)/shard_map/ppermute | solution.py:339
  14.2 2.6 %collective-permute-start.5 = (f32[136,128]{1,0:T(8,128)S(1)}, f32[136,128]{1,0:T(8,128)S(1)}, u32[]{:S(2)}, u32[]{:S(2)}) collective-permute-start(f32[136,128]{1,0:T(8,128)S(1)} %get-tuple-element.33), channel_id=1, source_target_pairs={{0,24},{16,0},{4,28},{20,4},{8,16},{24,8},{12,20},{28,12},{1,25},{... | collective-permute-start | bytes 208904 | tf_op jit(solution)/shard_map/ppermute | solution.py:339
  14.2 3.4 %collective-permute-start.6 = (f32[136,128]{1,0:T(8,128)S(1)}, f32[136,128]{1,0:T(8,128)S(1)}, u32[]{:S(2)}, u32[]{:S(2)}) collective-permute-start(f32[136,128]{1,0:T(8,128)S(1)} %get-tuple-element.34), channel_id=1, source_target_pairs={{0,20},{16,0},{4,24},{20,4},{8,28},{24,8},{12,16},{28,12},{1,21},{... | collective-permute-start | bytes 208904 | tf_op jit(solution)/shard_map/ppermute | solution.py:339
  14.3 3.3 %collective-permute-start.3 = (f32[136,128]{1,0:T(8,128)S(1)}, f32[136,128]{1,0:T(8,128)S(1)}, u32[]{:S(2)}, u32[]{:S(2)}) collective-permute-start(f32[136,128]{1,0:T(8,128)S(1)} %get-tuple-element.31.refs_0_), channel_id=1, source_target_pairs={{0,16},{16,0},{1,17},{17,1},{2,18},{18,2},{3,19},{19,3},{4,20},{20... | collective-permute-start | bytes 208904 | tf_op jit(solution)/shard_map/ppermute | solution.py:336
  17.9 3.6 %collective-permute-start.7 = (bf16[8,2048]{1,0:T(8,128)(2,1)S(1)}, bf16[8,2048]{1,0:T(8,128)(2,1)S(1)}, u32[]{:S(2)}, u32[]{:S(2)}) collective-permute-start(bf16[8,2048]{1,0:T(8,128)(2,1)S(1)} %merge.1.attended), channel_id=1, source_target_pairs={{0,16},{16,0},{1,17},{17,1},{2,18},{18,2},{3,19},{19,3},{4,20},{20... | collective-permute-start | bytes 98312 | tf_op jit(solution)/shard_map/ppermute | solution.py:348
  23.2 5.1 %collective-permute-start.8 = (f32[8,1024]{1,0:T(8,128)S(1)}, f32[8,1024]{1,0:T(8,128)S(1)}, u32[]{:S(2)}, u32[]{:S(2)}) collective-permute-start(f32[8,1024]{1,0:T(8,128)S(1)} %get-tuple-element.36), channel_id=1, source_target_pairs={{0,1},{1,2},{2,3},{3,0},{4,5},{5,6},{6,7},{7,4},{8,9},{9,10},{10,1... | collective-permute-start | bytes 98312 | tf_op jit(solution)/shard_map/ppermute | solution.py:366
  24.8 3.9 %collective-permute-start.9 = (f32[8,1024]{1,0:T(8,128)S(1)}, f32[8,1024]{1,0:T(8,128)S(1)}, u32[]{:S(2)}, u32[]{:S(2)}) collective-permute-start(f32[8,1024]{1,0:T(8,128)S(1)} %get-tuple-element.37), channel_id=1, source_target_pairs={{0,2},{1,3},{2,0},{3,1},{4,6},{5,7},{6,4},{7,5},{8,10},{9,11},{10,... | collective-permute-start | bytes 98312 | tf_op jit(solution)/shard_map/ppermute | solution.py:366
  26.3 3.9 %collective-permute-start.10 = (f32[8,1024]{1,0:T(8,128)S(1)}, f32[8,1024]{1,0:T(8,128)S(1)}, u32[]{:S(2)}, u32[]{:S(2)}) collective-permute-start(f32[8,1024]{1,0:T(8,128)S(1)} %get-tuple-element.38), channel_id=1, source_target_pairs={{0,3},{1,0},{2,1},{3,2},{4,7},{5,4},{6,5},{7,6},{8,11},{9,8},{10,9... | collective-permute-start | bytes 98312 | tf_op jit(solution)/shard_map/ppermute | solution.py:366

commit v8 on v7

--- a/solution.py
+++ b/solution.py
@@ -19,7 +19,7 @@
 SCALE = 1.0 / math.sqrt(HD)
 PARTS = CAP + CAPP
 CHUNK = 8
-BLOCK = 8
+STATS = 16
 MIB = 2**20
 
 
@@ -56,13 +56,23 @@
     return jnp.concatenate([page[:, (2 * j + first) * HD : (2 * j + first + 1) * HD] for j in range(held)], 1)
 
 
+def pieces(x):
+    high = x.astype(jnp.bfloat16).astype(jnp.float32)
+    middle = (x - high).astype(jnp.bfloat16).astype(jnp.float32)
+    return [high, middle, x - high - middle]
+
+
 def write_part(out, acc, top, total, held, per_held):
     count = acc.shape[0]
     band = count // held
-    for j in range(held):
-        out[j * band : (j + 1) * band, :] = acc[j * band : (j + 1) * band, j * HD : (j + 1) * HD]
-    out[count : count + 1, :count] = top
-    out[count + 1 : count + 2, :count] = total
+    out[:count, :] = jnp.concatenate(
+        [acc[j * band : (j + 1) * band, j * HD : (j + 1) * HD] for j in range(held)], 0
+    ).astype(out.dtype)
+    rows = pieces(top) + pieces(total)
+    block = jnp.concatenate(rows + [jnp.zeros((STATS - len(rows), count), jnp.float32)], 0)
+    if count < LANES:
+        block = jnp.concatenate([block, jnp.zeros((STATS, LANES - count), jnp.float32)], 1)
+    out[count:, :] = block.astype(out.dtype)
 
 
 def owner_part(qa, pages, entries, out, held, per_held, maxp):
@@ -85,7 +95,9 @@
     write_part(out, acc, top, total, held, per_held)
 
 
-def resident_part(qa, fresh_at, lists_ready, send, tables, lengths, maxp, group, kv, pages, flags, listed, sems, out, held, per_held):
+def resident_part(
+    span, qa, fresh_at, lists_ready, send, tables, lengths, maxp, group, kv, pages, flags, listed, sems, out, held, per_held
+):
     rows = qa.shape[0]
     slots = kv.shape[0]
     q = query_block(qa, held, per_held)
@@ -97,7 +109,8 @@
     own_mask = lax.broadcasted_iota(jnp.int32, (2 * rows, count), 0) == lane_row
     own = jnp.where(own_mask, dot(lanes_of(fresh, 0, held), q, 1, 1) * SCALE, NEG)
     own_top = jnp.max(own, 0, keepdims=True)
-    lift = jnp.exp(own - own_top)
+    here = jnp.logical_and(lane_row >= span[0], lane_row < span[1])
+    lift = jnp.where(here, jnp.exp(own - own_top), 0.0)
     own_total = jnp.sum(lift, 0, keepdims=True)
     own_acc = dot(lift.astype(jnp.bfloat16), lanes_of(fresh, 1, held), 0, 0)
     for i in range(slots):
@@ -112,7 +125,7 @@
         return pltpu.make_async_copy(kv.at[slot], pages.at[i], sems.at[i])
 
     listed_count = jnp.int32(0)
-    for r in range(rows):
+    for r in range(*span):
         length = lengths[0, r]
         for e in range(maxp):
             slot = tables[r, e]
@@ -138,27 +151,22 @@
     lax.fori_loop(listed_count, chunks * CHUNK, fill, 0)
 
     def step(c, carry):
-        old_top, total, acc = carry
-        blocks = [c * CHUNK + b for b in range(0, CHUNK, BLOCK)]
-        scores, top = [], old_top
-        for first in blocks:
-            masks = []
-            for i in range(BLOCK):
-                masks.append(token < jnp.where(lane_row == listed[0, first + i], listed[1, first + i], 0))
-            for i in range(BLOCK):
-                page_copy(0, first + i).wait()
-            keys = jnp.concatenate([lanes_of(pages.at[first + i], 0, held) for i in range(BLOCK)], 0)
-            scores.append(jnp.where(jnp.concatenate(masks, 0), dot(keys, q, 1, 1) * SCALE, NEG))
-            top = jnp.maximum(top, jnp.max(scores[-1], 0, keepdims=True))
-        fade = jnp.exp(old_top - top)
-        total = total * fade
-        acc = acc * jnp.broadcast_to(fade, (8, count)).T[:, :1]
-        for first, s in zip(blocks, scores):
-            p = jnp.exp(s - top)
-            total = total + jnp.sum(p, 0, keepdims=True)
-            values = jnp.concatenate([lanes_of(pages.at[first + i], 1, held) for i in range(BLOCK)], 0)
-            acc = acc + dot(p.astype(jnp.bfloat16), values, 0, 0)
-        return top, total, acc
+        top, total, acc = carry
+        first = c * CHUNK
+        masks = []
+        for i in range(CHUNK):
+            masks.append(token < jnp.where(lane_row == listed[0, first + i], listed[1, first + i], 0))
+        for i in range(CHUNK):
+            page_copy(0, first + i).wait()
+        keys = jnp.concatenate([lanes_of(pages.at[first + i], 0, held) for i in range(CHUNK)], 0)
+        values = jnp.concatenate([lanes_of(pages.at[first + i], 1, held) for i in range(CHUNK)], 0)
+        s = jnp.where(jnp.concatenate(masks, 0), dot(keys, q, 1, 1) * SCALE, NEG)
+        new_top = jnp.maximum(top, jnp.max(s, 0, keepdims=True))
+        p = jnp.exp(s - new_top)
+        fade = jnp.exp(top - new_top)
+        total = total * fade + jnp.sum(p, 0, keepdims=True)
+        acc = acc * jnp.broadcast_to(fade, (8, count)).T[:, :1] + dot(p.astype(jnp.bfloat16), values, 0, 0)
+        return new_top, total, acc
 
     top, total, acc = lax.fori_loop(0, chunks, step, (own_top, own_total, own_acc))
     write_part(out, acc, top, total, held, per_held)
@@ -185,20 +193,26 @@
         at = at + hit.astype(jnp.int32)
 
 
-def first_kernel(held, per_held, groups, maxp, qa, send_hbm, wanted_hbm, tables_hbm, lengths_hbm, kv, *refs):
-    out, chosen, entries, pages, send, wanted, tables, lengths = refs[:8]
-    flags, listed, page_list, slot_list, list_sems, chosen_sems, sems = refs[8:]
+def copy_lists(pairs, sems):
+    copies = [pltpu.make_async_copy(a, b, sems.at[i]) for i, (a, b) in enumerate(pairs)]
+    for copy in copies:
+        copy.start()
+
+    def ready():
+        for copy in copies:
+            copy.wait()
+
+    return ready
+
+
+def first_kernel(span, held, per_held, groups, maxp, qa, send_hbm, wanted_hbm, tables_hbm, lengths_hbm, kv, *refs):
+    out, sent, chosen, entries, pages, send, wanted, tables, lengths = refs[:9]
+    flags, listed, page_list, slot_list, list_sems, chosen_sems, sems = refs[9:]
     group = lax.axis_index("group")
     prefill = lax.axis_index("role") == 0
     fresh_at = held * per_held * HD + LANES
     lists = ((send_hbm, send), (wanted_hbm, wanted), (tables_hbm, tables), (lengths_hbm, lengths))
-    copies = [pltpu.make_async_copy(a, b, list_sems.at[i]) for i, (a, b) in enumerate(lists)]
-    for copy in copies:
-        copy.start()
-
-    def lists_ready():
-        for copy in copies:
-            copy.wait()
+    lists_ready = copy_lists(lists, list_sems)
 
     @pl.when(prefill)
     def _():
@@ -216,14 +230,27 @@
                 entries[at : at + 1, :] = jnp.full((1, LANES), entry, jnp.float32)
         for copy in copies[:PARTS]:
             copy.wait()
-        owner_part(qa, chosen.at[pl.ds(0, PARTS)], entries[:PARTS, :], out, held, per_held, maxp)
+        owner_part(qa, chosen.at[pl.ds(0, PARTS)], entries[:PARTS, :], sent, held, per_held, maxp)
         for copy in copies[PARTS:]:
             copy.wait()
 
     @pl.when(jnp.logical_not(prefill))
     def _():
         resident_part(
-            qa, fresh_at, lists_ready, send, tables, lengths, maxp, group, kv, pages, flags, listed, sems, out, held, per_held
+            span, qa, fresh_at, lists_ready, send, tables, lengths, maxp, group, kv, pages, flags, listed, sems, out, held, per_held
+        )
+
+
+def third_kernel(span, held, per_held, maxp, qa, send_hbm, tables_hbm, lengths_hbm, kv, *refs):
+    out, pages, send, tables, lengths, flags, listed, list_sems, sems = refs
+    group = lax.axis_index("group")
+    fresh_at = held * per_held * HD + LANES
+
+    @pl.when(lax.axis_index("role") == 1)
+    def _():
+        lists_ready = copy_lists(((send_hbm, send), (tables_hbm, tables), (lengths_hbm, lengths)), list_sems)
+        resident_part(
+            span, qa, fresh_at, lists_ready, send, tables, lengths, maxp, group, kv, pages, flags, listed, sems, out, held, per_held
         )
 
 
@@ -243,12 +270,13 @@
     parts, out = refs[:-1], refs[-1]
     count = heads * rows
     pad = -len(parts) % 8
-    tops = jnp.concatenate([part[count : count + 1, :count] for part in parts], 0)
-    totals = jnp.concatenate([part[count + 1 : count + 2, :count] for part in parts], 0)
+    stats = [part[count:, :].astype(jnp.float32)[:, :count] for part in parts]
+    tops = jnp.concatenate([s[0:1] + (s[1:2] + s[2:3]) for s in stats], 0)
+    totals = jnp.concatenate([s[3:4] + (s[4:5] + s[5:6]) for s in stats], 0)
     factors = jnp.exp(tops - jnp.max(tops, 0, keepdims=True))
     factors = factors / jnp.sum(factors * totals, 0, keepdims=True)
     factors = jnp.concatenate([factors, jnp.zeros((pad, count), jnp.float32)], 0).T
-    terms = [factors[:, i : i + 1] * part[:count, :] for i, part in enumerate(parts)]
+    terms = [factors[:, i : i + 1] * part[:count, :].astype(jnp.float32) for i, part in enumerate(parts)]
     merged = functools.reduce(jnp.add, terms)
     out[...] = jnp.concatenate([merged[h * rows : (h + 1) * rows] for h in range(heads)], 1).astype(out.dtype)
 
@@ -288,52 +316,71 @@
     for k in range(1, groups):
         pairs = [pair for i in range(groups) for pair in ((groups + i, (i + k) % groups), (i, groups + i))]
         asked.append(lax.ppermute(qa, ("role", "group"), pairs))
-    part_shape = jax.ShapeDtypeStruct((heads * rows + 8, HD), jnp.float32)
+    part_shape = jax.ShapeDtypeStruct((heads * rows + STATS, HD), jnp.float32)
+    sent_shape = jax.ShapeDtypeStruct(part_shape.shape, jnp.bfloat16)
     vmem = pl.BlockSpec(memory_space=pltpu.VMEM)
     hbm = pl.BlockSpec(memory_space=pltpu.HBM)
     page_shape = stored.shape[1:]
     chosen_count = groups * PARTS
-    read_count = -(-rows * maxp // CHUNK) * CHUNK
+    half = (rows + 1) // 2
+    read_count = -(-half * maxp // CHUNK) * CHUNK
     lists = [send, wanted, tables[0], lengths]
-    mine, chosen, entries = pl.pallas_call(
-        functools.partial(first_kernel, held, per_held, groups, maxp),
+    pinned = [pltpu.with_memory_space_constraint(x, pltpu.HBM) for x in lists + [stored]]
+    smem = [pltpu.SMEM(x.shape, jnp.int32) for x in lists]
+    reading = [pltpu.SMEM((slots + 1,), jnp.int32), pltpu.SMEM((2, read_count), jnp.int32)]
+    mine, mine_sent, chosen, entries = pl.pallas_call(
+        functools.partial(first_kernel, (0, half), held, per_held, groups, maxp),
         out_shape=[
             part_shape,
+            sent_shape,
             jax.ShapeDtypeStruct((chosen_count,) + page_shape, jnp.bfloat16),
             jax.ShapeDtypeStruct((chosen_count, LANES), jnp.float32),
         ],
         in_specs=[vmem] + [hbm] * 5,
-        out_specs=[vmem] * 3,
+        out_specs=[vmem] * 4,
         scratch_shapes=[
             pltpu.VMEM((read_count,) + page_shape, jnp.bfloat16),
-            pltpu.SMEM(send.shape, jnp.int32),
-            pltpu.SMEM(wanted.shape, jnp.int32),
-            pltpu.SMEM(tables.shape[1:], jnp.int32),
-            pltpu.SMEM(lengths.shape, jnp.int32),
-            pltpu.SMEM((slots + 1,), jnp.int32),
-            pltpu.SMEM((2, read_count), jnp.int32),
+            *smem,
+            *reading,
             pltpu.SMEM((chosen_count + 1,), jnp.int32),
             pltpu.SMEM((chosen_count + 1,), jnp.int32),
             pltpu.SemaphoreType.DMA((len(lists),)),
             pltpu.SemaphoreType.DMA((chosen_count,)),
             pltpu.SemaphoreType.DMA((read_count,)),
         ],
-        compiler_params=pltpu.CompilerParams(vmem_limit_bytes=24 * MIB),
+        compiler_params=pltpu.CompilerParams(vmem_limit_bytes=20 * MIB),
         name="resident",
-    )(qa, *[pltpu.with_memory_space_constraint(x, pltpu.HBM) for x in lists + [stored]])
-    out_weight, chosen, entries, mine = lax.optimization_barrier((out_weight, chosen, entries, mine))
+    )(qa, *pinned)
     count = groups - 1
     theirs = pl.pallas_call(
         functools.partial(second_kernel, held, per_held, maxp, count),
-        out_shape=[part_shape] * count,
+        out_shape=[sent_shape] * count,
         in_specs=[vmem] * (2 + count),
         out_specs=[vmem] * count,
         compiler_params=pltpu.CompilerParams(vmem_limit_bytes=16 * MIB),
         cost_estimate=pl.CostEstimate(flops=4 * 10**10, bytes_accessed=8 * MIB, transcendentals=10**6),
         name="owned",
     )(chosen, entries, *reversed(asked))
-    mine, theirs = lax.optimization_barrier((mine, theirs))
-    parts = [mine, lax.ppermute(mine, "role", [(0, 1), (1, 0)])]
+    qa, mine_sent, theirs = lax.optimization_barrier((qa, mine_sent, theirs))
+    rest = pl.pallas_call(
+        functools.partial(third_kernel, (half, rows), held, per_held, maxp),
+        out_shape=part_shape,
+        in_specs=[vmem] + [hbm] * 4,
+        out_specs=vmem,
+        scratch_shapes=[
+            pltpu.VMEM((read_count,) + page_shape, jnp.bfloat16),
+            smem[0],
+            smem[2],
+            smem[3],
+            *reading,
+            pltpu.SemaphoreType.DMA((3,)),
+            pltpu.SemaphoreType.DMA((read_count,)),
+        ],
+        compiler_params=pltpu.CompilerParams(vmem_limit_bytes=20 * MIB),
+        cost_estimate=pl.CostEstimate(flops=4 * 10**9, bytes_accessed=8 * MIB, transcendentals=10**6),
+        name="resident_rest",
+    )(qa, pinned[0], *pinned[2:])
+    parts = [mine, rest, lax.ppermute(mine_sent, "role", [(0, 1), (1, 0)])]
     for k in range(1, groups):
         pairs = [pair for i in range(groups) for pair in ((i, groups + (i - k) % groups), (groups + i, i))]
         parts.append(lax.ppermute(theirs[k - 1], ("role", "group"), pairs))

time: 30.7 us -> 31.2 us (1.016)
  waiting for transfers between devices: 5.56 us -> 7.51 us
  starting transfers between devices: 15.5 us -> 14 us
    ppermute x3, waiting for transfers between devices: 0.01 us -> 1.77 us  [per_device(): asked.append(lax.ppermute(qa, ('role', 'group'), pairs))]
    ppermute x3, waiting for transfers between devices: 1.84 us -> 3.57 us  [per_device(): lax.ppermute(part, 'tp', [(i, (i + d) % tps) for i in range(tps)])]
    ppermute x3, waiting for transfers between devices: 2.85 us -> 1.3 us  [per_device(): parts.append(lax.ppermute(theirs[k - 1], ('role', 'group'), pairs))]
    ppermute x3, starting transfers between devices: 3.67 us -> 2.24 us  [per_device(): parts.append(lax.ppermute(theirs[k - 1], ('role', 'group'), pairs))]
    ppermute x3, starting transfers between devices: 4.21 us -> 5.17 us  [per_device(): asked.append(lax.ppermute(qa, ('role', 'group'), pairs))]
    ppermute x3, starting transfers between devices: 4.46 us -> 3.56 us  [per_device(): lax.ppermute(part, 'tp', [(i, (i + d) % tps) for i in range(tps)])]
    ppermute x1, starting transfers between devices: 0.41 us -> 0.07 us  [per_device(): parts = [mine, rest, lax.ppermute(mine_sent, 'role', [(0, 1), (1, 0)])]]
    pallas_call x1 -> x2, Pallas kernels: 3.74 us -> 3.77 us  [the longest x1 3.45 us: per_device(): pl.pallas_call(functools.partial(first_kernel, (0, half), held, per_held,...]
  transfers between devices with their start and end apart: 11 -> 11, of which waited for: 6 -> 7; matrix products, arithmetic and copies ran while one was open for 0% -> 0% of each run, Pallas kernels for 14% -> 14%
where the time goes in v8:
time: 31.2 us; the launch traced here: 31.3 us
  starting transfers between devices  14 us (45%)
  Pallas kernels  8.16 us (26%)
  waiting for transfers between devices  7.51 us (24%)
  other arithmetic  1.52 us (5%)
    ppermute x3, starting transfers between devices, per_device(): asked.append(lax.ppermute(qa, ('role', 'group'), pairs))  5.17 us
    ppermute x3, waiting for transfers between devices, per_device(): lax.ppermute(part, 'tp', [(i, (i + d) % tps) for i in range(tps)])  3.57 us
    ppermute x3, starting transfers between devices, per_device(): lax.ppermute(part, 'tp', [(i, (i + d) % tps) for i in range(tps)])  3.56 us
    pallas_call x1, Pallas kernels, per_device(): pl.pallas_call(functools.partial(first_kernel, (0, half), held, per_held,...  3.45 us
    ppermute x1, starting transfers between devices, per_device(): partner = lax.ppermute(attended, 'role', [(0, 1), (1, 0)])  2.98 us
    pallas_call x2, Pallas kernels, project(): pl.pallas_call(functools.partial(project_kernel, steps), out_shape=[jax.S...  2.39 us
    ppermute x3, starting transfers between devices, per_device(): parts.append(lax.ppermute(theirs[k - 1], ('role', 'group'), pairs))  2.24 us
    ppermute x3, waiting for transfers between devices, per_device(): asked.append(lax.ppermute(qa, ('role', 'group'), pairs))  1.77 us
  transfers between devices with their start and end apart: 11, of which 7 were waited for; matrix products, arithmetic and copies ran while one was open for 0% of the time, Pallas kernels for 14%

profile of v8, /device:TPU:0, one launch (start us, length us, event | category | flops | bytes accessed | tf_op | source)
XLA Modules:
  0.0 31.3 jit_solution(15841972138336361563)
XLA Ops:
  0.0 0.9 %fusion.qa = bf16[8,2688]{1,0:T(8,128)(2,1)S(1)} fusion(s32[1,8]{1,0:T(1,128)} %lengths_hbm.3, s32[8,8]{1,0:T(8,128)} %bitcast.12, bf16[8,512]{1,0:T(8,128)(2,1)} %bitcast.15, bf16[8,2048]{1,0:T(8,128)(2,1)} %bitcast.11), kind=kLoop, calls=%fused_computation.1 | loop fusion | flops 236544 | bytes 84256 | tf_op jit(solution)/shard_map/add | solution.py:314
  0.9 0.5 %collective-permute-start = (bf16[8,2688]{1,0:T(8,128)(2,1)S(1)}, bf16[8,2688]{1,0:T(8,128)(2,1)S(1)}, u32[]{:S(2)}, u32[]{:S(2)}) collective-permute-start(bf16[8,2688]{1,0:T(8,128)(2,1)S(1)} %fusion.qa), channel_id=1, source_target_pairs={{16,12},{0,16},{20,0},{4,20},{24,4},{8,24},{28,8},{12,28},{17,13},... | collective-permute-start | bytes 129032 | tf_op jit(solution)/shard_map/ppermute | solution.py:318
  1.4 4.7 %collective-permute-start.1 = (bf16[8,2688]{1,0:T(8,128)(2,1)S(1)}, bf16[8,2688]{1,0:T(8,128)(2,1)S(1)}, u32[]{:S(2)}, u32[]{:S(2)}) collective-permute-start(bf16[8,2688]{1,0:T(8,128)(2,1)S(1)} %fusion.qa), channel_id=1, source_target_pairs={{16,8},{0,16},{20,12},{4,20},{24,0},{8,24},{28,4},{12,28},{17,9},{... | collective-permute-start | bytes 129032 | tf_op jit(solution)/shard_map/ppermute | solution.py:318
  6.1 3.5 %resident.1 = (f32[144,128]{1,0:T(8,128)S(1)}, bf16[144,128]{1,0:T(8,128)(2,1)S(1)}, bf16[24,128,512]{2,1,0:T(8,128)(2,1)S(1)}, f32[24,128]{1,0:T(8,128)S(1)}) custom-call(bf16[8,2688]{1,0:T(8,128)(2,1)S(1)} %fusion.qa, s32[3,4,12]{2,1,0:T(4,128)} %bitcast.16, s32[4,6]{1,0:T(4,128)} %wanted_hbm.1, s32[8,8]{1,0:T(8,128)} %bitcast.13, s32[1,8]{1,0:T(1,128)} %lengths_hbm.3, ...), custom_call_target="tpu_custom_call" | custom-call | tf_op jit(solution)/shard_map/resident/pallas_call | solution.py:331
  9.6 1.8 %collective-permute-done.2.refs_2_ = bf16[8,2688]{1,0:T(8,128)(2,1)S(1)} collective-permute-done((bf16[8,2688]{1,0:T(8,128)(2,1)S(1)}, bf16[8,2688]{1,0:T(8,128)(2,1)S(1)}, u32[]{:S(2)}, u32[]{:S(2)}) %collective-permute-start.2) | collective-permute-done | bytes 43040 | tf_op jit(solution)/shard_map/ppermute | solution.py:318
  11.3 1.7 %owned.1 = (bf16[144,128]{1,0:T(8,128)(2,1)S(1)}, bf16[144,128]{1,0:T(8,128)(2,1)S(1)}, bf16[144,128]{1,0:T(8,128)(2,1)S(1)}) custom-call(bf16[24,128,512]{2,1,0:T(8,128)(2,1)S(1)} %get-tuple-element.22.chosen, f32[24,128]{1,0:T(8,128)S(1)} %get-tuple-element.23.entries, bf16[8,2688]{1,0:T(8,128)(2,1)S(1)} %collective-permute-done.refs_0_, ...), custom_call_target="tpu_custom_call" | custom-call | flops 40000000000 | bytes 8388608 | tf_op jit(solution)/shard_map/owned/pallas_call | solution.py:355
  13.0 0.1 collective-permute-start.3
  13.1 1.1 %collective-permute-start.4 = (bf16[144,128]{1,0:T(8,128)(2,1)S(1)}, bf16[144,128]{1,0:T(8,128)(2,1)S(1)}, u32[]{:S(2)}, u32[]{:S(2)}) collective-permute-start(bf16[144,128]{1,0:T(8,128)(2,1)S(1)} %get-tuple-element.29), channel_id=1, source_target_pairs={{0,28},{16,0},{4,16},{20,4},{8,20},{24,8},{12,24},{28,12},{1,29},{... | collective-permute-start | bytes 110600 | tf_op jit(solution)/shard_map/ppermute | solution.py:386
  14.2 1.1 %collective-permute-start.6 = (bf16[144,128]{1,0:T(8,128)(2,1)S(1)}, bf16[144,128]{1,0:T(8,128)(2,1)S(1)}, u32[]{:S(2)}, u32[]{:S(2)}) collective-permute-start(bf16[144,128]{1,0:T(8,128)(2,1)S(1)} %get-tuple-element.31), channel_id=1, source_target_pairs={{0,20},{16,0},{4,24},{20,4},{8,28},{24,8},{12,16},{28,12},{1,21},{... | collective-permute-start | bytes 110600 | tf_op jit(solution)/shard_map/ppermute | solution.py:386
  15.3 0.3 %resident_rest.1.refs_1_ = f32[144,128]{1,0:T(8,128)S(1)} custom-call(bf16[8,2688]{1,0:T(8,128)(2,1)S(1)} %fusion.qa, s32[3,4,12]{2,1,0:T(4,128)} %bitcast.17, s32[8,8]{1,0:T(8,128)} %bitcast.14, s32[1,8]{1,0:T(1,128)} %lengths_hbm.3, bf16[64,128,512]{2,1,0:T(8,128)(2,1)} %bitcast.10), custom_call_target="tpu_custom_call" | custom-call | flops 4000000000 | bytes 8388608 | tf_op jit(solution)/shard_map/resident_rest/pallas_call | solution.py:365
  15.7 0.2 collective-permute-done.4.refs_3_
  15.8 0.3 %collective-permute-done.5.refs_4_ = bf16[144,128]{1,0:T(8,128)(2,1)S(1)} collective-permute-done((bf16[144,128]{1,0:T(8,128)(2,1)S(1)}, bf16[144,128]{1,0:T(8,128)(2,1)S(1)}, u32[]{:S(2)}, u32[]{:S(2)}) %collective-permute-start.5) | collective-permute-done | bytes 36896 | tf_op jit(solution)/shard_map/ppermute | solution.py:386
  16.2 0.8 %collective-permute-done.6.refs_5_ = bf16[144,128]{1,0:T(8,128)(2,1)S(1)} collective-permute-done((bf16[144,128]{1,0:T(8,128)(2,1)S(1)}, bf16[144,128]{1,0:T(8,128)(2,1)S(1)}, u32[]{:S(2)}, u32[]{:S(2)}) %collective-permute-start.6) | collective-permute-done | bytes 36896 | tf_op jit(solution)/shard_map/ppermute | solution.py:386
  17.0 0.3 %merge.1.attended = bf16[8,2048]{1,0:T(8,128)(2,1)S(1)} custom-call(f32[144,128]{1,0:T(8,128)S(1)} %get-tuple-element.20.refs_0_, f32[144,128]{1,0:T(8,128)S(1)} %resident_rest.1.refs_1_, bf16[144,128]{1,0:T(8,128)(2,1)S(1)} %collective-permute-done.3.refs_2_, bf16[144,128]{1,0:T(8,128)(2,1)S(1)} %collective-permute-done.4.refs_3_, ...), custom_call_target="tpu_custom_call" | custom-call | tf_op jit(solution)/shard_map/merge/pallas_call | solution.py:387
  17.3 3.0 %collective-permute-start.7 = (bf16[8,2048]{1,0:T(8,128)(2,1)S(1)}, bf16[8,2048]{1,0:T(8,128)(2,1)S(1)}, u32[]{:S(2)}, u32[]{:S(2)}) collective-permute-start(bf16[8,2048]{1,0:T(8,128)(2,1)S(1)} %merge.1.attended), channel_id=1, source_target_pairs={{0,16},{16,0},{1,17},{17,1},{2,18},{18,2},{3,19},{19,3},{4,20},{20... | collective-permute-start | bytes 98312 | tf_op jit(solution)/shard_map/ppermute | solution.py:395
  20.3 0.9 %collective-permute-done.7.partner = bf16[8,2048]{1,0:T(8,128)(2,1)S(1)} collective-permute-done((bf16[8,2048]{1,0:T(8,128)(2,1)S(1)}, bf16[8,2048]{1,0:T(8,128)(2,1)S(1)}, u32[]{:S(2)}, u32[]{:S(2)}) %collective-permute-start.7) | collective-permute-done | bytes 32800 | tf_op jit(solution)/shard_map/ppermute | solution.py:395
  21.2 1.7 %project.1 = (f32[8,1024]{1,0:T(8,128)S(1)}, f32[8,1024]{1,0:T(8,128)S(1)}, f32[8,1024]{1,0:T(8,128)S(1)}) custom-call(bf16[8,2048]{1,0:T(8,128)(2,1)S(1)} %merge.1.attended, bf16[8,2048]{1,0:T(8,128)(2,1)S(1)} %collective-permute-done.7.partner, bf16[2048,4096]{1,0:T(8,128)(2,1)S(1)} %bitcast.8), custom_call_target="tpu_custom_call" | custom-call | flops 201326592 | bytes 12582912 | tf_op jit(solution)/shard_map/project/pallas_call | solution.py:399
  22.9 2.5 %collective-permute-start.10 = (f32[8,1024]{1,0:T(8,128)S(1)}, f32[8,1024]{1,0:T(8,128)S(1)}, u32[]{:S(2)}, u32[]{:S(2)}) collective-permute-start(f32[8,1024]{1,0:T(8,128)S(1)} %get-tuple-element.34), channel_id=1, source_target_pairs={{0,3},{1,0},{2,1},{3,2},{4,7},{5,4},{6,5},{7,6},{8,11},{9,8},{10,9... | collective-permute-start | bytes 98312 | tf_op jit(solution)/shard_map/ppermute | solution.py:413
  25.4 0.5 %collective-permute-start.9 = (f32[8,1024]{1,0:T(8,128)S(1)}, f32[8,1024]{1,0:T(8,128)S(1)}, u32[]{:S(2)}, u32[]{:S(2)}) collective-permute-start(f32[8,1024]{1,0:T(8,128)S(1)} %get-tuple-element.33), channel_id=1, source_target_pairs={{0,2},{1,3},{2,0},{3,1},{4,6},{5,7},{6,4},{7,5},{8,10},{9,11},{10,... | collective-permute-start | bytes 98312 | tf_op jit(solution)/shard_map/ppermute | solution.py:413
  25.9 0.6 %collective-permute-start.8 = (f32[8,1024]{1,0:T(8,128)S(1)}, f32[8,1024]{1,0:T(8,128)S(1)}, u32[]{:S(2)}, u32[]{:S(2)}) collective-permute-start(f32[8,1024]{1,0:T(8,128)S(1)} %get-tuple-element.32), channel_id=1, source_target_pairs={{0,1},{1,2},{2,3},{3,0},{4,5},{5,6},{6,7},{7,4},{8,9},{9,10},{10,1... | collective-permute-start | bytes 98312 | tf_op jit(solution)/shard_map/ppermute | solution.py:413
  26.5 0.6 %project_own.1 = f32[8,1024]{1,0:T(8,128)S(1)} custom-call(bf16[8,2048]{1,0:T(8,128)(2,1)S(1)} %merge.1.attended, bf16[8,2048]{1,0:T(8,128)(2,1)S(1)} %collective-permute-done.7.partner, bf16[2048,4096]{1,0:T(8,128)(2,1)S(1)} %bitcast.8), custom_call_target="tpu_custom_call" | custom-call | flops 67108864 | bytes 4194304 | tf_op jit(solution)/shard_map/project_own/pallas_call | solution.py:399
  27.1 2.5 %collective-permute-done.9 = f32[8,1024]{1,0:T(8,128)S(1)} collective-permute-done((f32[8,1024]{1,0:T(8,128)S(1)}, f32[8,1024]{1,0:T(8,128)S(1)}, u32[]{:S(2)}, u32[]{:S(2)}) %collective-permute-start.9) | collective-permute-done | bytes 32800 | tf_op jit(solution)/shard_map/ppermute | solution.py:413
  29.6 1.0 %collective-permute-done.8 = f32[8,1024]{1,0:T(8,128)S(1)} collective-permute-done((f32[8,1024]{1,0:T(8,128)S(1)}, f32[8,1024]{1,0:T(8,128)S(1)}, u32[]{:S(2)}, u32[]{:S(2)}) %collective-permute-start.8) | collective-permute-done | bytes 32800 | tf_op jit(solution)/shard_map/ppermute | solution.py:413
  30.7 0.6 %fusion.1 = bf16[1,8,1024]{2,1,0:T(8,128)(2,1)} fusion(f32[8,1024]{1,0:T(8,128)S(1)} %collective-permute-done.10, f32[8,1024]{1,0:T(8,128)S(1)} %collective-permute-done.9, f32[8,1024]{1,0:T(8,128)S(1)} %project_own.1, f32[8,1024]{1,0:T(8,128)S(1)} %collective-permute-done.8), kind=kLoop, calls=%fused_computation.3 | loop fusion | flops 32768 | bytes 147456 | tf_op jit(solution)/shard_map/broadcast_in_dim | solution.py:415
  (15 shorter events, 0.0 us)
Async XLA Ops:
  0.9 8.6 %collective-permute-start = (bf16[8,2688]{1,0:T(8,128)(2,1)S(1)}, bf16[8,2688]{1,0:T(8,128)(2,1)S(1)}, u32[]{:S(2)}, u32[]{:S(2)}) collective-permute-start(bf16[8,2688]{1,0:T(8,128)(2,1)S(1)} %fusion.qa), channel_id=1, source_target_pairs={{16,12},{0,16},{20,0},{4,20},{24,4},{8,24},{28,8},{12,28},{17,13},... | collective-permute-start | bytes 129032 | tf_op jit(solution)/shard_map/ppermute | solution.py:318
  1.4 8.2 %collective-permute-start.1 = (bf16[8,2688]{1,0:T(8,128)(2,1)S(1)}, bf16[8,2688]{1,0:T(8,128)(2,1)S(1)}, u32[]{:S(2)}, u32[]{:S(2)}) collective-permute-start(bf16[8,2688]{1,0:T(8,128)(2,1)S(1)} %fusion.qa), channel_id=1, source_target_pairs={{16,8},{0,16},{20,12},{4,20},{24,0},{8,24},{28,4},{12,28},{17,9},{... | collective-permute-start | bytes 129032 | tf_op jit(solution)/shard_map/ppermute | solution.py:318
  6.1 5.2 %collective-permute-start.2 = (bf16[8,2688]{1,0:T(8,128)(2,1)S(1)}, bf16[8,2688]{1,0:T(8,128)(2,1)S(1)}, u32[]{:S(2)}, u32[]{:S(2)}) collective-permute-start(bf16[8,2688]{1,0:T(8,128)(2,1)S(1)} %fusion.qa), channel_id=1, source_target_pairs={{16,4},{0,16},{20,8},{4,20},{24,12},{8,24},{28,0},{12,28},{17,5},{... | collective-permute-start | bytes 129032 | tf_op jit(solution)/shard_map/ppermute | solution.py:318
  11.3 9.8 %slice-start = ((s8[16777216]{0:T(1024)(128)(4,1)}), s8[4194304]{0:T(1024)(128)(4,1)S(1)}, s32[]{:S(2)}) async-start(s8[16777216]{0:T(1024)(128)(4,1)} %bitcast.7), calls=%async_computation | async-start | bytes 8388608
  11.3 9.8 %slice-start.1 = ((s8[16777216]{0:T(1024)(128)(4,1)}), s8[4194304]{0:T(1024)(128)(4,1)S(1)}, s32[]{:S(2)}) async-start(s8[16777216]{0:T(1024)(128)(4,1)} %bitcast.7), calls=%async_computation.1 | async-start | bytes 8388608
  11.3 9.8 %slice-start.2 = ((s8[16777216]{0:T(1024)(128)(4,1)}), s8[4194304]{0:T(1024)(128)(4,1)S(1)}, s32[]{:S(2)}) async-start(s8[16777216]{0:T(1024)(128)(4,1)} %bitcast.7), calls=%async_computation.2 | async-start | bytes 8388608
  11.3 9.8 %slice-start.3 = ((s8[16777216]{0:T(1024)(128)(4,1)}), s8[4194304]{0:T(1024)(128)(4,1)S(1)}, s32[]{:S(2)}) async-start(s8[16777216]{0:T(1024)(128)(4,1)} %bitcast.7), calls=%async_computation.3 | async-start | bytes 8388608
  13.0 2.6 %collective-permute-start.3 = (bf16[144,128]{1,0:T(8,128)(2,1)S(1)}, bf16[144,128]{1,0:T(8,128)(2,1)S(1)}, u32[]{:S(2)}, u32[]{:S(2)}) collective-permute-start(bf16[144,128]{1,0:T(8,128)(2,1)S(1)} %get-tuple-element.28), channel_id=1, source_target_pairs={{0,16},{16,0},{1,17},{17,1},{2,18},{18,2},{3,19},{19,3},{4,20},{20... | collective-permute-start | bytes 110600 | tf_op jit(solution)/shard_map/ppermute | solution.py:383
  13.1 2.7 %collective-permute-start.4 = (bf16[144,128]{1,0:T(8,128)(2,1)S(1)}, bf16[144,128]{1,0:T(8,128)(2,1)S(1)}, u32[]{:S(2)}, u32[]{:S(2)}) collective-permute-start(bf16[144,128]{1,0:T(8,128)(2,1)S(1)} %get-tuple-element.29), channel_id=1, source_target_pairs={{0,28},{16,0},{4,16},{20,4},{8,20},{24,8},{12,24},{28,12},{1,29},{... | collective-permute-start | bytes 110600 | tf_op jit(solution)/shard_map/ppermute | solution.py:386
  14.2 2.0 %collective-permute-start.5 = (bf16[144,128]{1,0:T(8,128)(2,1)S(1)}, bf16[144,128]{1,0:T(8,128)(2,1)S(1)}, u32[]{:S(2)}, u32[]{:S(2)}) collective-permute-start(bf16[144,128]{1,0:T(8,128)(2,1)S(1)} %get-tuple-element.30), channel_id=1, source_target_pairs={{0,24},{16,0},{4,28},{20,4},{8,16},{24,8},{12,20},{28,12},{1,25},{... | collective-permute-start | bytes 110600 | tf_op jit(solution)/shard_map/ppermute | solution.py:386
  14.2 2.8 %collective-permute-start.6 = (bf16[144,128]{1,0:T(8,128)(2,1)S(1)}, bf16[144,128]{1,0:T(8,128)(2,1)S(1)}, u32[]{:S(2)}, u32[]{:S(2)}) collective-permute-start(bf16[144,128]{1,0:T(8,128)(2,1)S(1)} %get-tuple-element.31), channel_id=1, source_target_pairs={{0,20},{16,0},{4,24},{20,4},{8,28},{24,8},{12,16},{28,12},{1,21},{... | collective-permute-start | bytes 110600 | tf_op jit(solution)/shard_map/ppermute | solution.py:386
  17.3 3.8 %collective-permute-start.7 = (bf16[8,2048]{1,0:T(8,128)(2,1)S(1)}, bf16[8,2048]{1,0:T(8,128)(2,1)S(1)}, u32[]{:S(2)}, u32[]{:S(2)}) collective-permute-start(bf16[8,2048]{1,0:T(8,128)(2,1)S(1)} %merge.1.attended), channel_id=1, source_target_pairs={{0,16},{16,0},{1,17},{17,1},{2,18},{18,2},{3,19},{19,3},{4,20},{20... | collective-permute-start | bytes 98312 | tf_op jit(solution)/shard_map/ppermute | solution.py:395
  22.9 4.2 %collective-permute-start.10 = (f32[8,1024]{1,0:T(8,128)S(1)}, f32[8,1024]{1,0:T(8,128)S(1)}, u32[]{:S(2)}, u32[]{:S(2)}) collective-permute-start(f32[8,1024]{1,0:T(8,128)S(1)} %get-tuple-element.34), channel_id=1, source_target_pairs={{0,3},{1,0},{2,1},{3,2},{4,7},{5,4},{6,5},{7,6},{8,11},{9,8},{10,9... | collective-permute-start | bytes 98312 | tf_op jit(solution)/shard_map/ppermute | solution.py:413
  25.4 4.3 %collective-permute-start.9 = (f32[8,1024]{1,0:T(8,128)S(1)}, f32[8,1024]{1,0:T(8,128)S(1)}, u32[]{:S(2)}, u32[]{:S(2)}) collective-permute-start(f32[8,1024]{1,0:T(8,128)S(1)} %get-tuple-element.33), channel_id=1, source_target_pairs={{0,2},{1,3},{2,0},{3,1},{4,6},{5,7},{6,4},{7,5},{8,10},{9,11},{10,... | collective-permute-start | bytes 98312 | tf_op jit(solution)/shard_map/ppermute | solution.py:413
  25.9 4.8 %collective-permute-start.8 = (f32[8,1024]{1,0:T(8,128)S(1)}, f32[8,1024]{1,0:T(8,128)S(1)}, u32[]{:S(2)}, u32[]{:S(2)}) collective-permute-start(f32[8,1024]{1,0:T(8,128)S(1)} %get-tuple-element.32), channel_id=1, source_target_pairs={{0,1},{1,2},{2,3},{3,0},{4,5},{5,6},{6,7},{7,4},{8,9},{9,10},{10,1... | collective-permute-start | bytes 98312 | tf_op jit(solution)/shard_map/ppermute | solution.py:413

commit v9 on v8

--- a/solution.py
+++ b/solution.py
@@ -255,7 +255,7 @@
 
 
 def second_kernel(held, per_held, maxp, count, chosen, entries, *refs):
-    qas, outs = refs[:count][::-1], refs[count:]
+    qas, outs = refs[:count], refs[count:]
 
     @pl.when(lax.axis_index("role") == 0)
     def _():
@@ -322,14 +322,14 @@
     hbm = pl.BlockSpec(memory_space=pltpu.HBM)
     page_shape = stored.shape[1:]
     chosen_count = groups * PARTS
-    half = (rows + 1) // 2
-    read_count = -(-half * maxp // CHUNK) * CHUNK
+    cut = rows - rows // 4
+    read_count = -(-cut * maxp // CHUNK) * CHUNK
     lists = [send, wanted, tables[0], lengths]
     pinned = [pltpu.with_memory_space_constraint(x, pltpu.HBM) for x in lists + [stored]]
     smem = [pltpu.SMEM(x.shape, jnp.int32) for x in lists]
     reading = [pltpu.SMEM((slots + 1,), jnp.int32), pltpu.SMEM((2, read_count), jnp.int32)]
     mine, mine_sent, chosen, entries = pl.pallas_call(
-        functools.partial(first_kernel, (0, half), held, per_held, groups, maxp),
+        functools.partial(first_kernel, (0, cut), held, per_held, groups, maxp),
         out_shape=[
             part_shape,
             sent_shape,
@@ -360,10 +360,10 @@
         compiler_params=pltpu.CompilerParams(vmem_limit_bytes=16 * MIB),
         cost_estimate=pl.CostEstimate(flops=4 * 10**10, bytes_accessed=8 * MIB, transcendentals=10**6),
         name="owned",
-    )(chosen, entries, *reversed(asked))
+    )(chosen, entries, *asked)
     qa, mine_sent, theirs = lax.optimization_barrier((qa, mine_sent, theirs))
     rest = pl.pallas_call(
-        functools.partial(third_kernel, (half, rows), held, per_held, maxp),
+        functools.partial(third_kernel, (cut, rows), held, per_held, maxp),
         out_shape=part_shape,
         in_specs=[vmem] + [hbm] * 4,
         out_specs=vmem,
@@ -411,7 +411,7 @@
     steps = list(range(1, tps))
     sent = project(steps, "project")
     arrived = [lax.ppermute(part, "tp", [(i, (i + d) % tps) for i in range(tps)]) for d, part in zip(steps, sent)]
-    total = functools.reduce(jnp.add, arrived, project([0], "project_own")[0])
+    total = functools.reduce(jnp.add, arrived[::-1], project([0], "project_own")[0])
     return total.astype(jnp.bfloat16)[None]
 
 

time: 31.2 us -> 29.9 us (0.958); the launches traced: 31.3 us -> 29.7 us
  waiting for transfers between devices: 7.51 us -> 4.47 us
  starting transfers between devices: 14 us -> 15.1 us
    ppermute x3, waiting for transfers between devices: 1.77 us -> 0.01 us  [per_device(): asked.append(lax.ppermute(qa, ('role', 'group'), pairs))]
    ppermute x3, waiting for transfers between devices: 3.57 us -> 1.84 us  [per_device(): lax.ppermute(part, 'tp', [(i, (i + d) % tps) for i in range(tps)])]
    ppermute x1, starting transfers between devices: 0.07 us -> 1.14 us  [per_device(): parts = [mine, rest, lax.ppermute(mine_sent, 'role', [(0, 1), (1, 0)])]]
    ppermute x3, starting transfers between devices: 3.56 us -> 4.53 us  [per_device(): lax.ppermute(part, 'tp', [(i, (i + d) % tps) for i in range(tps)])]
    ppermute x3, starting transfers between devices: 5.17 us -> 4.21 us  [per_device(): asked.append(lax.ppermute(qa, ('role', 'group'), pairs))]
    ppermute x3, waiting for transfers between devices: 1.3 us -> 1.77 us  [per_device(): parts.append(lax.ppermute(theirs[k - 1], ('role', 'group'), pairs))]
    ppermute x1, starting transfers between devices: 2.98 us -> 3.43 us  [per_device(): partner = lax.ppermute(attended, 'role', [(0, 1), (1, 0)])]
    ppermute x3, starting transfers between devices: 2.24 us -> 1.81 us  [per_device(): parts.append(lax.ppermute(theirs[k - 1], ('role', 'group'), pairs))]
  transfers between devices with their start and end apart: 11 -> 11, of which waited for: 7 -> 6; matrix products, arithmetic and copies ran while one was open for 0% -> 0% of each run, Pallas kernels for 14% -> 16%
where the time goes in v9:
time: 29.9 us; the launch traced here: 29.7 us
  starting transfers between devices  15.1 us (51%)
  Pallas kernels  8.44 us (28%)
  waiting for transfers between devices  4.47 us (15%)
  other arithmetic  1.52 us (5%)
    ppermute x3, starting transfers between devices, per_device(): lax.ppermute(part, 'tp', [(i, (i + d) % tps) for i in range(tps)])  4.53 us
    ppermute x3, starting transfers between devices, per_device(): asked.append(lax.ppermute(qa, ('role', 'group'), pairs))  4.21 us
    pallas_call x1, Pallas kernels, per_device(): pl.pallas_call(functools.partial(first_kernel, (0, cut), held, per_held,...  3.59 us
    ppermute x1, starting transfers between devices, per_device(): partner = lax.ppermute(attended, 'role', [(0, 1), (1, 0)])  3.43 us
    pallas_call x2, Pallas kernels, project(): pl.pallas_call(functools.partial(project_kernel, steps), out_shape=[jax.S...  2.38 us
    ppermute x3, waiting for transfers between devices, per_device(): lax.ppermute(part, 'tp', [(i, (i + d) % tps) for i in range(tps)])  1.84 us
    ppermute x3, starting transfers between devices, per_device(): parts.append(lax.ppermute(theirs[k - 1], ('role', 'group'), pairs))  1.81 us
    ppermute x3, waiting for transfers between devices, per_device(): parts.append(lax.ppermute(theirs[k - 1], ('role', 'group'), pairs))  1.77 us
  transfers between devices with their start and end apart: 11, of which 6 were waited for; matrix products, arithmetic and copies ran while one was open for 0% of the time, Pallas kernels for 16%

profile of v9, /device:TPU:0, one launch (start us, length us, event | category | flops | bytes accessed | tf_op | source)
XLA Modules:
  0.0 29.7 jit_solution(16627930869383514447)
XLA Ops:
  0.0 0.9 %fusion.qa = bf16[8,2688]{1,0:T(8,128)(2,1)S(1)} fusion(s32[1,8]{1,0:T(1,128)} %lengths_hbm.3, s32[8,8]{1,0:T(8,128)} %bitcast.12, bf16[8,512]{1,0:T(8,128)(2,1)} %bitcast.15, bf16[8,2048]{1,0:T(8,128)(2,1)} %bitcast.11), kind=kLoop, calls=%fused_computation.1 | loop fusion | flops 236544 | bytes 84256 | tf_op jit(solution)/shard_map/add | solution.py:314
  0.9 0.5 %collective-permute-start = (bf16[8,2688]{1,0:T(8,128)(2,1)S(1)}, bf16[8,2688]{1,0:T(8,128)(2,1)S(1)}, u32[]{:S(2)}, u32[]{:S(2)}) collective-permute-start(bf16[8,2688]{1,0:T(8,128)(2,1)S(1)} %fusion.qa), channel_id=1, source_target_pairs={{16,4},{0,16},{20,8},{4,20},{24,12},{8,24},{28,0},{12,28},{17,5},{... | collective-permute-start | bytes 129032 | tf_op jit(solution)/shard_map/ppermute | solution.py:318
  1.4 2.7 %collective-permute-start.1 = (bf16[8,2688]{1,0:T(8,128)(2,1)S(1)}, bf16[8,2688]{1,0:T(8,128)(2,1)S(1)}, u32[]{:S(2)}, u32[]{:S(2)}) collective-permute-start(bf16[8,2688]{1,0:T(8,128)(2,1)S(1)} %fusion.qa), channel_id=1, source_target_pairs={{16,8},{0,16},{20,12},{4,20},{24,0},{8,24},{28,4},{12,28},{17,9},{... | collective-permute-start | bytes 129032 | tf_op jit(solution)/shard_map/ppermute | solution.py:318
  4.0 1.1 %collective-permute-start.2 = (bf16[8,2688]{1,0:T(8,128)(2,1)S(1)}, bf16[8,2688]{1,0:T(8,128)(2,1)S(1)}, u32[]{:S(2)}, u32[]{:S(2)}) collective-permute-start(bf16[8,2688]{1,0:T(8,128)(2,1)S(1)} %fusion.qa), channel_id=1, source_target_pairs={{16,12},{0,16},{20,0},{4,20},{24,4},{8,24},{28,8},{12,28},{17,13},... | collective-permute-start | bytes 129032 | tf_op jit(solution)/shard_map/ppermute | solution.py:318
  5.1 3.6 %resident.1 = (f32[144,128]{1,0:T(8,128)S(1)}, bf16[144,128]{1,0:T(8,128)(2,1)S(1)}, bf16[24,128,512]{2,1,0:T(8,128)(2,1)S(1)}, f32[24,128]{1,0:T(8,128)S(1)}) custom-call(bf16[8,2688]{1,0:T(8,128)(2,1)S(1)} %fusion.qa, s32[3,4,12]{2,1,0:T(4,128)} %bitcast.16, s32[4,6]{1,0:T(4,128)} %wanted_hbm.1, s32[8,8]{1,0:T(8,128)} %bitcast.13, s32[1,8]{1,0:T(1,128)} %lengths_hbm.3, ...), custom_call_target="tpu_custom_call" | custom-call | tf_op jit(solution)/shard_map/resident/pallas_call | solution.py:331
  8.8 1.7 %owned.1 = (bf16[144,128]{1,0:T(8,128)(2,1)S(1)}, bf16[144,128]{1,0:T(8,128)(2,1)S(1)}, bf16[144,128]{1,0:T(8,128)(2,1)S(1)}) custom-call(bf16[24,128,512]{2,1,0:T(8,128)(2,1)S(1)} %get-tuple-element.22.chosen, f32[24,128]{1,0:T(8,128)S(1)} %get-tuple-element.23.entries, bf16[8,2688]{1,0:T(8,128)(2,1)S(1)} %collective-permute-done.refs_0_, ...), custom_call_target="tpu_custom_call" | custom-call | flops 40000000000 | bytes 8388608 | tf_op jit(solution)/shard_map/owned/pallas_call | solution.py:355
  10.5 1.1 %collective-permute-start.3 = (bf16[144,128]{1,0:T(8,128)(2,1)S(1)}, bf16[144,128]{1,0:T(8,128)(2,1)S(1)}, u32[]{:S(2)}, u32[]{:S(2)}) collective-permute-start(bf16[144,128]{1,0:T(8,128)(2,1)S(1)} %get-tuple-element.28), channel_id=1, source_target_pairs={{0,16},{16,0},{1,17},{17,1},{2,18},{18,2},{3,19},{19,3},{4,20},{20... | collective-permute-start | bytes 110600 | tf_op jit(solution)/shard_map/ppermute | solution.py:383
  11.6 1.7 %collective-permute-start.4 = (bf16[144,128]{1,0:T(8,128)(2,1)S(1)}, bf16[144,128]{1,0:T(8,128)(2,1)S(1)}, u32[]{:S(2)}, u32[]{:S(2)}) collective-permute-start(bf16[144,128]{1,0:T(8,128)(2,1)S(1)} %get-tuple-element.29), channel_id=1, source_target_pairs={{0,28},{16,0},{4,16},{20,4},{8,20},{24,8},{12,24},{28,12},{1,29},{... | collective-permute-start | bytes 110600 | tf_op jit(solution)/shard_map/ppermute | solution.py:386
  13.3 0.1 collective-permute-start.6
  13.4 0.5 %resident_rest.1.refs_1_ = f32[144,128]{1,0:T(8,128)S(1)} custom-call(bf16[8,2688]{1,0:T(8,128)(2,1)S(1)} %fusion.qa, s32[3,4,12]{2,1,0:T(4,128)} %bitcast.17, s32[8,8]{1,0:T(8,128)} %bitcast.14, s32[1,8]{1,0:T(1,128)} %lengths_hbm.3, bf16[64,128,512]{2,1,0:T(8,128)(2,1)} %bitcast.10), custom_call_target="tpu_custom_call" | custom-call | flops 4000000000 | bytes 8388608 | tf_op jit(solution)/shard_map/resident_rest/pallas_call | solution.py:365
  13.9 1.1 %collective-permute-done.4.refs_3_ = bf16[144,128]{1,0:T(8,128)(2,1)S(1)} collective-permute-done((bf16[144,128]{1,0:T(8,128)(2,1)S(1)}, bf16[144,128]{1,0:T(8,128)(2,1)S(1)}, u32[]{:S(2)}, u32[]{:S(2)}) %collective-permute-start.4) | collective-permute-done | bytes 36896 | tf_op jit(solution)/shard_map/ppermute | solution.py:386
  15.0 0.3 %collective-permute-done.5.refs_4_ = bf16[144,128]{1,0:T(8,128)(2,1)S(1)} collective-permute-done((bf16[144,128]{1,0:T(8,128)(2,1)S(1)}, bf16[144,128]{1,0:T(8,128)(2,1)S(1)}, u32[]{:S(2)}, u32[]{:S(2)}) %collective-permute-start.5) | collective-permute-done | bytes 36896 | tf_op jit(solution)/shard_map/ppermute | solution.py:386
  15.3 0.3 %collective-permute-done.6.refs_5_ = bf16[144,128]{1,0:T(8,128)(2,1)S(1)} collective-permute-done((bf16[144,128]{1,0:T(8,128)(2,1)S(1)}, bf16[144,128]{1,0:T(8,128)(2,1)S(1)}, u32[]{:S(2)}, u32[]{:S(2)}) %collective-permute-start.6) | collective-permute-done | bytes 36896 | tf_op jit(solution)/shard_map/ppermute | solution.py:386
  15.7 0.3 %merge.1.attended = bf16[8,2048]{1,0:T(8,128)(2,1)S(1)} custom-call(f32[144,128]{1,0:T(8,128)S(1)} %get-tuple-element.20.refs_0_, f32[144,128]{1,0:T(8,128)S(1)} %resident_rest.1.refs_1_, bf16[144,128]{1,0:T(8,128)(2,1)S(1)} %collective-permute-done.3.refs_2_, bf16[144,128]{1,0:T(8,128)(2,1)S(1)} %collective-permute-done.4.refs_3_, ...), custom_call_target="tpu_custom_call" | custom-call | tf_op jit(solution)/shard_map/merge/pallas_call | solution.py:387
  16.0 3.4 %collective-permute-start.7 = (bf16[8,2048]{1,0:T(8,128)(2,1)S(1)}, bf16[8,2048]{1,0:T(8,128)(2,1)S(1)}, u32[]{:S(2)}, u32[]{:S(2)}) collective-permute-start(bf16[8,2048]{1,0:T(8,128)(2,1)S(1)} %merge.1.attended), channel_id=1, source_target_pairs={{0,16},{16,0},{1,17},{17,1},{2,18},{18,2},{3,19},{19,3},{4,20},{20... | collective-permute-start | bytes 98312 | tf_op jit(solution)/shard_map/ppermute | solution.py:395
  19.4 0.9 %collective-permute-done.7.partner = bf16[8,2048]{1,0:T(8,128)(2,1)S(1)} collective-permute-done((bf16[8,2048]{1,0:T(8,128)(2,1)S(1)}, bf16[8,2048]{1,0:T(8,128)(2,1)S(1)}, u32[]{:S(2)}, u32[]{:S(2)}) %collective-permute-start.7) | collective-permute-done | bytes 32800 | tf_op jit(solution)/shard_map/ppermute | solution.py:395
  20.3 1.7 %project.1 = (f32[8,1024]{1,0:T(8,128)S(1)}, f32[8,1024]{1,0:T(8,128)S(1)}, f32[8,1024]{1,0:T(8,128)S(1)}) custom-call(bf16[8,2048]{1,0:T(8,128)(2,1)S(1)} %merge.1.attended, bf16[8,2048]{1,0:T(8,128)(2,1)S(1)} %collective-permute-done.7.partner, bf16[2048,4096]{1,0:T(8,128)(2,1)S(1)} %bitcast.8), custom_call_target="tpu_custom_call" | custom-call | flops 201326592 | bytes 12582912 | tf_op jit(solution)/shard_map/project/pallas_call | solution.py:399
  22.1 1.6 %collective-permute-start.10 = (f32[8,1024]{1,0:T(8,128)S(1)}, f32[8,1024]{1,0:T(8,128)S(1)}, u32[]{:S(2)}, u32[]{:S(2)}) collective-permute-start(f32[8,1024]{1,0:T(8,128)S(1)} %get-tuple-element.34), channel_id=1, source_target_pairs={{0,1},{1,2},{2,3},{3,0},{4,5},{5,6},{6,7},{7,4},{8,9},{9,10},{10,1... | collective-permute-start | bytes 98312 | tf_op jit(solution)/shard_map/ppermute | solution.py:413
  23.6 1.5 %collective-permute-start.9 = (f32[8,1024]{1,0:T(8,128)S(1)}, f32[8,1024]{1,0:T(8,128)S(1)}, u32[]{:S(2)}, u32[]{:S(2)}) collective-permute-start(f32[8,1024]{1,0:T(8,128)S(1)} %get-tuple-element.33), channel_id=1, source_target_pairs={{0,2},{1,3},{2,0},{3,1},{4,6},{5,7},{6,4},{7,5},{8,10},{9,11},{10,... | collective-permute-start | bytes 98312 | tf_op jit(solution)/shard_map/ppermute | solution.py:413
  25.2 1.4 %collective-permute-start.8 = (f32[8,1024]{1,0:T(8,128)S(1)}, f32[8,1024]{1,0:T(8,128)S(1)}, u32[]{:S(2)}, u32[]{:S(2)}) collective-permute-start(f32[8,1024]{1,0:T(8,128)S(1)} %get-tuple-element.32), channel_id=1, source_target_pairs={{0,3},{1,0},{2,1},{3,2},{4,7},{5,4},{6,5},{7,6},{8,11},{9,8},{10,9... | collective-permute-start | bytes 98312 | tf_op jit(solution)/shard_map/ppermute | solution.py:413
  26.6 0.6 %project_own.1 = f32[8,1024]{1,0:T(8,128)S(1)} custom-call(bf16[8,2048]{1,0:T(8,128)(2,1)S(1)} %merge.1.attended, bf16[8,2048]{1,0:T(8,128)(2,1)S(1)} %collective-permute-done.7.partner, bf16[2048,4096]{1,0:T(8,128)(2,1)S(1)} %bitcast.8), custom_call_target="tpu_custom_call" | custom-call | flops 67108864 | bytes 4194304 | tf_op jit(solution)/shard_map/project_own/pallas_call | solution.py:399
  27.2 0.3 %collective-permute-done.9 = f32[8,1024]{1,0:T(8,128)S(1)} collective-permute-done((f32[8,1024]{1,0:T(8,128)S(1)}, f32[8,1024]{1,0:T(8,128)S(1)}, u32[]{:S(2)}, u32[]{:S(2)}) %collective-permute-start.9) | collective-permute-done | bytes 32800 | tf_op jit(solution)/shard_map/ppermute | solution.py:413
  27.6 1.5 %collective-permute-done.8 = f32[8,1024]{1,0:T(8,128)S(1)} collective-permute-done((f32[8,1024]{1,0:T(8,128)S(1)}, f32[8,1024]{1,0:T(8,128)S(1)}, u32[]{:S(2)}, u32[]{:S(2)}) %collective-permute-start.8) | collective-permute-done | bytes 32800 | tf_op jit(solution)/shard_map/ppermute | solution.py:413
  29.1 0.6 %fusion.1 = bf16[1,8,1024]{2,1,0:T(8,128)(2,1)} fusion(f32[8,1024]{1,0:T(8,128)S(1)} %collective-permute-done.10, f32[8,1024]{1,0:T(8,128)S(1)} %collective-permute-done.9, f32[8,1024]{1,0:T(8,128)S(1)} %project_own.1, f32[8,1024]{1,0:T(8,128)S(1)} %collective-permute-done.8), kind=kLoop, calls=%fused_computation.3 | loop fusion | flops 32768 | bytes 147456 | tf_op jit(solution)/shard_map/broadcast_in_dim | solution.py:415
  (15 shorter events, 0.0 us)
Async XLA Ops:
  0.9 7.8 %collective-permute-start = (bf16[8,2688]{1,0:T(8,128)(2,1)S(1)}, bf16[8,2688]{1,0:T(8,128)(2,1)S(1)}, u32[]{:S(2)}, u32[]{:S(2)}) collective-permute-start(bf16[8,2688]{1,0:T(8,128)(2,1)S(1)} %fusion.qa), channel_id=1, source_target_pairs={{16,4},{0,16},{20,8},{4,20},{24,12},{8,24},{28,0},{12,28},{17,5},{... | collective-permute-start | bytes 129032 | tf_op jit(solution)/shard_map/ppermute | solution.py:318
  1.4 7.4 %collective-permute-start.1 = (bf16[8,2688]{1,0:T(8,128)(2,1)S(1)}, bf16[8,2688]{1,0:T(8,128)(2,1)S(1)}, u32[]{:S(2)}, u32[]{:S(2)}) collective-permute-start(bf16[8,2688]{1,0:T(8,128)(2,1)S(1)} %fusion.qa), channel_id=1, source_target_pairs={{16,8},{0,16},{20,12},{4,20},{24,0},{8,24},{28,4},{12,28},{17,9},{... | collective-permute-start | bytes 129032 | tf_op jit(solution)/shard_map/ppermute | solution.py:318
  4.0 4.7 %collective-permute-start.2 = (bf16[8,2688]{1,0:T(8,128)(2,1)S(1)}, bf16[8,2688]{1,0:T(8,128)(2,1)S(1)}, u32[]{:S(2)}, u32[]{:S(2)}) collective-permute-start(bf16[8,2688]{1,0:T(8,128)(2,1)S(1)} %fusion.qa), channel_id=1, source_target_pairs={{16,12},{0,16},{20,0},{4,20},{24,4},{8,24},{28,8},{12,28},{17,13},... | collective-permute-start | bytes 129032 | tf_op jit(solution)/shard_map/ppermute | solution.py:318
  8.7 11.6 %slice-start = ((s8[16777216]{0:T(1024)(128)(4,1)}), s8[4194304]{0:T(1024)(128)(4,1)S(1)}, s32[]{:S(2)}) async-start(s8[16777216]{0:T(1024)(128)(4,1)} %bitcast.7), calls=%async_computation | async-start | bytes 8388608
  8.8 11.5 %slice-start.1 = ((s8[16777216]{0:T(1024)(128)(4,1)}), s8[4194304]{0:T(1024)(128)(4,1)S(1)}, s32[]{:S(2)}) async-start(s8[16777216]{0:T(1024)(128)(4,1)} %bitcast.7), calls=%async_computation.1 | async-start | bytes 8388608
  8.8 11.5 %slice-start.2 = ((s8[16777216]{0:T(1024)(128)(4,1)}), s8[4194304]{0:T(1024)(128)(4,1)S(1)}, s32[]{:S(2)}) async-start(s8[16777216]{0:T(1024)(128)(4,1)} %bitcast.7), calls=%async_computation.2 | async-start | bytes 8388608
  8.8 11.5 %slice-start.3 = ((s8[16777216]{0:T(1024)(128)(4,1)}), s8[4194304]{0:T(1024)(128)(4,1)S(1)}, s32[]{:S(2)}) async-start(s8[16777216]{0:T(1024)(128)(4,1)} %bitcast.7), calls=%async_computation.3 | async-start | bytes 8388608
  10.5 3.4 %collective-permute-start.3 = (bf16[144,128]{1,0:T(8,128)(2,1)S(1)}, bf16[144,128]{1,0:T(8,128)(2,1)S(1)}, u32[]{:S(2)}, u32[]{:S(2)}) collective-permute-start(bf16[144,128]{1,0:T(8,128)(2,1)S(1)} %get-tuple-element.28), channel_id=1, source_target_pairs={{0,16},{16,0},{1,17},{17,1},{2,18},{18,2},{3,19},{19,3},{4,20},{20... | collective-permute-start | bytes 110600 | tf_op jit(solution)/shard_map/ppermute | solution.py:383
  11.6 3.4 %collective-permute-start.4 = (bf16[144,128]{1,0:T(8,128)(2,1)S(1)}, bf16[144,128]{1,0:T(8,128)(2,1)S(1)}, u32[]{:S(2)}, u32[]{:S(2)}) collective-permute-start(bf16[144,128]{1,0:T(8,128)(2,1)S(1)} %get-tuple-element.29), channel_id=1, source_target_pairs={{0,28},{16,0},{4,16},{20,4},{8,20},{24,8},{12,24},{28,12},{1,29},{... | collective-permute-start | bytes 110600 | tf_op jit(solution)/shard_map/ppermute | solution.py:386
  13.3 2.0 %collective-permute-start.5 = (bf16[144,128]{1,0:T(8,128)(2,1)S(1)}, bf16[144,128]{1,0:T(8,128)(2,1)S(1)}, u32[]{:S(2)}, u32[]{:S(2)}) collective-permute-start(bf16[144,128]{1,0:T(8,128)(2,1)S(1)} %get-tuple-element.30), channel_id=1, source_target_pairs={{0,24},{16,0},{4,28},{20,4},{8,16},{24,8},{12,20},{28,12},{1,25},{... | collective-permute-start | bytes 110600 | tf_op jit(solution)/shard_map/ppermute | solution.py:386
  13.3 2.3 %collective-permute-start.6 = (bf16[144,128]{1,0:T(8,128)(2,1)S(1)}, bf16[144,128]{1,0:T(8,128)(2,1)S(1)}, u32[]{:S(2)}, u32[]{:S(2)}) collective-permute-start(bf16[144,128]{1,0:T(8,128)(2,1)S(1)} %get-tuple-element.31), channel_id=1, source_target_pairs={{0,20},{16,0},{4,24},{20,4},{8,28},{24,8},{12,16},{28,12},{1,21},{... | collective-permute-start | bytes 110600 | tf_op jit(solution)/shard_map/ppermute | solution.py:386
  16.0 4.3 %collective-permute-start.7 = (bf16[8,2048]{1,0:T(8,128)(2,1)S(1)}, bf16[8,2048]{1,0:T(8,128)(2,1)S(1)}, u32[]{:S(2)}, u32[]{:S(2)}) collective-permute-start(bf16[8,2048]{1,0:T(8,128)(2,1)S(1)} %merge.1.attended), channel_id=1, source_target_pairs={{0,16},{16,0},{1,17},{17,1},{2,18},{18,2},{3,19},{19,3},{4,20},{20... | collective-permute-start | bytes 98312 | tf_op jit(solution)/shard_map/ppermute | solution.py:395
  22.1 5.2 %collective-permute-start.10 = (f32[8,1024]{1,0:T(8,128)S(1)}, f32[8,1024]{1,0:T(8,128)S(1)}, u32[]{:S(2)}, u32[]{:S(2)}) collective-permute-start(f32[8,1024]{1,0:T(8,128)S(1)} %get-tuple-element.34), channel_id=1, source_target_pairs={{0,1},{1,2},{2,3},{3,0},{4,5},{5,6},{6,7},{7,4},{8,9},{9,10},{10,1... | collective-permute-start | bytes 98312 | tf_op jit(solution)/shard_map/ppermute | solution.py:413
  23.6 3.9 %collective-permute-start.9 = (f32[8,1024]{1,0:T(8,128)S(1)}, f32[8,1024]{1,0:T(8,128)S(1)}, u32[]{:S(2)}, u32[]{:S(2)}) collective-permute-start(f32[8,1024]{1,0:T(8,128)S(1)} %get-tuple-element.33), channel_id=1, source_target_pairs={{0,2},{1,3},{2,0},{3,1},{4,6},{5,7},{6,4},{7,5},{8,10},{9,11},{10,... | collective-permute-start | bytes 98312 | tf_op jit(solution)/shard_map/ppermute | solution.py:413
  25.2 3.9 %collective-permute-start.8 = (f32[8,1024]{1,0:T(8,128)S(1)}, f32[8,1024]{1,0:T(8,128)S(1)}, u32[]{:S(2)}, u32[]{:S(2)}) collective-permute-start(f32[8,1024]{1,0:T(8,128)S(1)} %get-tuple-element.32), channel_id=1, source_target_pairs={{0,3},{1,0},{2,1},{3,2},{4,7},{5,4},{6,5},{7,6},{8,11},{9,8},{10,9... | collective-permute-start | bytes 98312 | tf_op jit(solution)/shard_map/ppermute | solution.py:413

commit v10 on v8

--- a/solution.py
+++ b/solution.py
@@ -16,6 +16,7 @@
 LANES = 128
 PAGE = 128
 NEG = -1e30
+FLOOR = -1e29
 SCALE = 1.0 / math.sqrt(HD)
 PARTS = CAP + CAPP
 CHUNK = 8
@@ -95,24 +96,13 @@
     write_part(out, acc, top, total, held, per_held)
 
 
-def resident_part(
-    span, qa, fresh_at, lists_ready, send, tables, lengths, maxp, group, kv, pages, flags, listed, sems, out, held, per_held
-):
+def resident_part(qa, lists_ready, send, tables, lengths, maxp, group, kv, pages, flags, listed, sems, out, held, per_held):
     rows = qa.shape[0]
     slots = kv.shape[0]
     q = query_block(qa, held, per_held)
     count = q.shape[0]
     lane_row = lax.rem(lax.broadcasted_iota(jnp.int32, (1, count), 1), rows)
     token = lax.broadcasted_iota(jnp.int32, (PAGE, count), 0)
-    fresh = qa[:, fresh_at : fresh_at + 2 * held * HD].astype(jnp.float32)
-    fresh = jnp.concatenate([fresh, jnp.zeros_like(fresh)], 0).astype(jnp.bfloat16)
-    own_mask = lax.broadcasted_iota(jnp.int32, (2 * rows, count), 0) == lane_row
-    own = jnp.where(own_mask, dot(lanes_of(fresh, 0, held), q, 1, 1) * SCALE, NEG)
-    own_top = jnp.max(own, 0, keepdims=True)
-    here = jnp.logical_and(lane_row >= span[0], lane_row < span[1])
-    lift = jnp.where(here, jnp.exp(own - own_top), 0.0)
-    own_total = jnp.sum(lift, 0, keepdims=True)
-    own_acc = dot(lift.astype(jnp.bfloat16), lanes_of(fresh, 1, held), 0, 0)
     for i in range(slots):
         flags[i] = 0
 
@@ -125,7 +115,7 @@
         return pltpu.make_async_copy(kv.at[slot], pages.at[i], sems.at[i])
 
     listed_count = jnp.int32(0)
-    for r in range(*span):
+    for r in range(rows):
         length = lengths[0, r]
         for e in range(maxp):
             slot = tables[r, e]
@@ -168,7 +158,12 @@
         acc = acc * jnp.broadcast_to(fade, (8, count)).T[:, :1] + dot(p.astype(jnp.bfloat16), values, 0, 0)
         return new_top, total, acc
 
-    top, total, acc = lax.fori_loop(0, chunks, step, (own_top, own_total, own_acc))
+    start = (
+        jnp.full((1, count), FLOOR, jnp.float32),
+        jnp.zeros((1, count), jnp.float32),
+        jnp.zeros((count, held * HD), jnp.float32),
+    )
+    top, total, acc = lax.fori_loop(0, chunks, step, start)
     write_part(out, acc, top, total, held, per_held)
 
 
@@ -205,12 +200,11 @@
     return ready
 
 
-def first_kernel(span, held, per_held, groups, maxp, qa, send_hbm, wanted_hbm, tables_hbm, lengths_hbm, kv, *refs):
+def first_kernel(held, per_held, groups, maxp, qa, send_hbm, wanted_hbm, tables_hbm, lengths_hbm, kv, *refs):
     out, sent, chosen, entries, pages, send, wanted, tables, lengths = refs[:9]
     flags, listed, page_list, slot_list, list_sems, chosen_sems, sems = refs[9:]
     group = lax.axis_index("group")
     prefill = lax.axis_index("role") == 0
-    fresh_at = held * per_held * HD + LANES
     lists = ((send_hbm, send), (wanted_hbm, wanted), (tables_hbm, tables), (lengths_hbm, lengths))
     lists_ready = copy_lists(lists, list_sems)
 
@@ -237,21 +231,23 @@
     @pl.when(jnp.logical_not(prefill))
     def _():
         resident_part(
-            span, qa, fresh_at, lists_ready, send, tables, lengths, maxp, group, kv, pages, flags, listed, sems, out, held, per_held
+            qa, lists_ready, send, tables, lengths, maxp, group, kv, pages, flags, listed, sems, out, held, per_held
         )
 
 
-def third_kernel(span, held, per_held, maxp, qa, send_hbm, tables_hbm, lengths_hbm, kv, *refs):
-    out, pages, send, tables, lengths, flags, listed, list_sems, sems = refs
-    group = lax.axis_index("group")
-    fresh_at = held * per_held * HD + LANES
-
-    @pl.when(lax.axis_index("role") == 1)
-    def _():
-        lists_ready = copy_lists(((send_hbm, send), (tables_hbm, tables), (lengths_hbm, lengths)), list_sems)
-        resident_part(
-            span, qa, fresh_at, lists_ready, send, tables, lengths, maxp, group, kv, pages, flags, listed, sems, out, held, per_held
-        )
+def fresh_kernel(held, per_held, qa, new_kv, out):
+    rows = qa.shape[0]
+    q = query_block(qa, held, per_held)
+    count = q.shape[0]
+    lane_row = lax.rem(lax.broadcasted_iota(jnp.int32, (1, count), 1), rows)
+    fresh = new_kv[...].astype(jnp.float32)
+    fresh = jnp.concatenate([fresh, jnp.zeros_like(fresh)], 0).astype(jnp.bfloat16)
+    mask = lax.broadcasted_iota(jnp.int32, (2 * rows, count), 0) == lane_row
+    s = jnp.where(mask, dot(lanes_of(fresh, 0, held), q, 1, 1) * SCALE, NEG)
+    top = jnp.max(s, 0, keepdims=True)
+    p = jnp.exp(s - top)
+    acc = dot(p.astype(jnp.bfloat16), lanes_of(fresh, 1, held), 0, 0)
+    write_part(out, acc, top, jnp.sum(p, 0, keepdims=True), held, per_held)
 
 
 def second_kernel(held, per_held, maxp, count, chosen, entries, *refs):
@@ -281,15 +277,14 @@
     out[...] = jnp.concatenate([merged[h * rows : (h + 1) * rows] for h in range(heads)], 1).astype(out.dtype)
 
 
-def project_kernel(steps, attended, partner, weight, *outs):
+def project_kernel(share, first_step, attended, partner, weight, out):
     tps = lax.axis_size("tp")
-    share = outs[0].shape[1]
     here = jnp.where(lax.axis_index("role") == 0, partner[...].astype(jnp.float32), attended[...].astype(jnp.float32))
     here = here.astype(jnp.bfloat16)
-    for d, out in zip(steps, outs):
-        first = lax.rem(lax.axis_index("tp") + d, tps) * share
+    for i in range(out.shape[1] // share):
+        first = lax.bitwise_xor(lax.axis_index("tp"), tps - 1 - first_step - i) * share
         columns = pl.ds(pl.multiple_of(first, LANES), share)
-        out[...] = jnp.dot(here, weight[:, columns], preferred_element_type=jnp.float32)
+        out[:, i * share : (i + 1) * share] = jnp.dot(here, weight[:, columns], preferred_element_type=jnp.float32)
 
 
 def per_device(kv_pages, send_list, wanted, lengths, tables, queries, new_kv, out_weight):
@@ -302,16 +297,13 @@
     per_held = heads // held
     maxp = tables.shape[2]
     send = jnp.transpose(send_list, (2, 0, 1))
-    fresh_at = wide + LANES
-    width = fresh_at + new_kv.shape[2]
-
     def place(block, at):
-        return jnp.pad(block, ((0, rows - block.shape[0]), (at, width - at - block.shape[1])))
+        return jnp.pad(block, ((0, rows - block.shape[0]), (at, wide + LANES - at - block.shape[1])))
 
     high = lax.shift_right_logical(place(lengths, wide + maxp), 3)
     low = jnp.bitwise_and(place(lengths, wide + maxp + rows), 7)
     integers = place(tables[0], wide) + high + low
-    qa = place(queries[0], 0) + place(new_kv[0], fresh_at) + integers.astype(jnp.bfloat16)
+    qa = place(queries[0], 0) + integers.astype(jnp.bfloat16)
     asked = []
     for k in range(1, groups):
         pairs = [pair for i in range(groups) for pair in ((groups + i, (i + k) % groups), (i, groups + i))]
@@ -322,14 +314,13 @@
     hbm = pl.BlockSpec(memory_space=pltpu.HBM)
     page_shape = stored.shape[1:]
     chosen_count = groups * PARTS
-    half = (rows + 1) // 2
-    read_count = -(-half * maxp // CHUNK) * CHUNK
+    read_count = -(-rows * maxp // CHUNK) * CHUNK
     lists = [send, wanted, tables[0], lengths]
     pinned = [pltpu.with_memory_space_constraint(x, pltpu.HBM) for x in lists + [stored]]
     smem = [pltpu.SMEM(x.shape, jnp.int32) for x in lists]
     reading = [pltpu.SMEM((slots + 1,), jnp.int32), pltpu.SMEM((2, read_count), jnp.int32)]
     mine, mine_sent, chosen, entries = pl.pallas_call(
-        functools.partial(first_kernel, (0, half), held, per_held, groups, maxp),
+        functools.partial(first_kernel, held, per_held, groups, maxp),
         out_shape=[
             part_shape,
             sent_shape,
@@ -362,25 +353,16 @@
         name="owned",
     )(chosen, entries, *reversed(asked))
     qa, mine_sent, theirs = lax.optimization_barrier((qa, mine_sent, theirs))
-    rest = pl.pallas_call(
-        functools.partial(third_kernel, (half, rows), held, per_held, maxp),
+    fresh = pl.pallas_call(
+        functools.partial(fresh_kernel, held, per_held),
         out_shape=part_shape,
-        in_specs=[vmem] + [hbm] * 4,
+        in_specs=[vmem] * 2,
         out_specs=vmem,
-        scratch_shapes=[
-            pltpu.VMEM((read_count,) + page_shape, jnp.bfloat16),
-            smem[0],
-            smem[2],
-            smem[3],
-            *reading,
-            pltpu.SemaphoreType.DMA((3,)),
-            pltpu.SemaphoreType.DMA((read_count,)),
-        ],
-        compiler_params=pltpu.CompilerParams(vmem_limit_bytes=20 * MIB),
-        cost_estimate=pl.CostEstimate(flops=4 * 10**9, bytes_accessed=8 * MIB, transcendentals=10**6),
-        name="resident_rest",
-    )(qa, pinned[0], *pinned[2:])
-    parts = [mine, rest, lax.ppermute(mine_sent, "role", [(0, 1), (1, 0)])]
+        compiler_params=pltpu.CompilerParams(vmem_limit_bytes=8 * MIB),
+        cost_estimate=pl.CostEstimate(flops=10**9, bytes_accessed=MIB, transcendentals=10**4),
+        name="fresh",
+    )(qa, new_kv[0])
+    parts = [mine, fresh, lax.ppermute(mine_sent, "role", [(0, 1), (1, 0)])]
     for k in range(1, groups):
         pairs = [pair for i in range(groups) for pair in ((i, groups + (i - k) % groups), (groups + i, i))]
         parts.append(lax.ppermute(theirs[k - 1], ("role", "group"), pairs))
@@ -395,24 +377,29 @@
     partner = lax.ppermute(attended, "role", [(0, 1), (1, 0)])
     share = out_weight.shape[1] // tps
 
-    def project(steps, name):
+    def project(first_step, steps, name):
         return pl.pallas_call(
-            functools.partial(project_kernel, steps),
-            out_shape=[jax.ShapeDtypeStruct((rows, share), jnp.float32)] * len(steps),
+            functools.partial(project_kernel, share, first_step),
+            out_shape=jax.ShapeDtypeStruct((rows, steps * share), jnp.float32),
             in_specs=[vmem] * 3,
-            out_specs=[vmem] * len(steps),
+            out_specs=vmem,
             compiler_params=pltpu.CompilerParams(vmem_limit_bytes=24 * MIB),
             cost_estimate=pl.CostEstimate(
-                flops=len(steps) * 32 * wide * share, bytes_accessed=len(steps) * 2 * wide * share, transcendentals=0
+                flops=steps * 32 * wide * share, bytes_accessed=steps * 2 * wide * share, transcendentals=0
             ),
             name=name,
         )(attended, partner, out_weight)
 
-    steps = list(range(1, tps))
-    sent = project(steps, "project")
-    arrived = [lax.ppermute(part, "tp", [(i, (i + d) % tps) for i in range(tps)]) for d, part in zip(steps, sent)]
-    total = functools.reduce(jnp.add, arrived, project([0], "project_own")[0])
-    return total.astype(jnp.bfloat16)[None]
+    sent, kept = project(0, tps // 2, "project_sent"), project(tps // 2, tps // 2, "project_kept")
+    step = tps // 2
+    while True:
+        arrived = lax.ppermute(sent, "tp", [(i, i ^ step) for i in range(tps)])
+        if step == 1:
+            return (kept + arrived).astype(jnp.bfloat16)[None]
+        middle = step * share // 2
+        sent = kept[:, :middle] + arrived[:, :middle]
+        kept = kept[:, middle:] + arrived[:, middle:]
+        step //= 2
 
 
 def solution(mesh):

time: 31.2 us -> 31.2 us (level)
  waiting for transfers between devices: 7.51 us -> 6.88 us
  Pallas kernels: 8.16 us -> 8.48 us
    ppermute x3, waiting for transfers between devices: 1.77 us -> 0.01 us  [per_device(): asked.append(lax.ppermute(qa, ('role', 'group'), pairs))]
    ppermute x3, starting transfers between devices: 5.17 us -> 4.21 us  [per_device(): asked.append(lax.ppermute(qa, ('role', 'group'), pairs))]
    ppermute x3, waiting for transfers between devices: 1.3 us -> 1.94 us  [per_device(): parts.append(lax.ppermute(theirs[k - 1], ('role', 'group'), pairs))]
    ppermute x4 -> x3, starting transfers between devices: 3.63 us -> 4.19 us  [the longest x2 3.02 us: per_device(): arrived = lax.ppermute(sent, 'tp', [(i, i ^ step) for i in range(tps)])]
    ppermute x4 -> x3, waiting for transfers between devices: 3.58 us -> 4.08 us  [the longest x2 4.07 us: per_device(): arrived = lax.ppermute(sent, 'tp', [(i, i ^ step) for i in range(tps)])]
    ppermute x1, starting transfers between devices: 2.98 us -> 3.43 us  [per_device(): partner = lax.ppermute(attended, 'role', [(0, 1), (1, 0)])]
    pallas_call x4, Pallas kernels: 6.15 us -> 6.48 us  [the longest x1 3.74 us: per_device(): pl.pallas_call(functools.partial(first_kernel, held, per_held, groups, ma...]
    add x1 -> x2, other arithmetic: 0.9 us -> 0.89 us  [the longest x1 0.88 us: per_device(): qa = place(queries[0], 0) + integers.astype(jnp.bfloat16)]
  transfers between devices with their start and end apart: 11 -> 10, of which waited for: 7 -> 6; matrix products, arithmetic and copies ran while one was open for 0% -> 0% of each run, Pallas kernels for 14% -> 17%
where the time goes in v10:
time: 31.2 us; the launch traced here: 31.3 us
  starting transfers between devices  14.3 us (46%)
  Pallas kernels  8.48 us (27%)
  waiting for transfers between devices  6.88 us (22%)
  other arithmetic  1.5 us (5%)
    ppermute x3, starting transfers between devices, per_device(): asked.append(lax.ppermute(qa, ('role', 'group'), pairs))  4.21 us
    ppermute x2, waiting for transfers between devices, per_device(): arrived = lax.ppermute(sent, 'tp', [(i, i ^ step) for i in range(tps)])  4.07 us
    pallas_call x1, Pallas kernels, per_device(): pl.pallas_call(functools.partial(first_kernel, held, per_held, groups, ma...  3.74 us
    ppermute x1, starting transfers between devices, per_device(): partner = lax.ppermute(attended, 'role', [(0, 1), (1, 0)])  3.43 us
    ppermute x2, starting transfers between devices, per_device(): arrived = lax.ppermute(sent, 'tp', [(i, i ^ step) for i in range(tps)])  3.02 us
    ppermute x3, starting transfers between devices, per_device(): parts.append(lax.ppermute(theirs[k - 1], ('role', 'group'), pairs))  2.48 us
    pallas_call x2, Pallas kernels, project(): pl.pallas_call(functools.partial(project_kernel, share, first_step), out_...  2.38 us
    ppermute x3, waiting for transfers between devices, per_device(): parts.append(lax.ppermute(theirs[k - 1], ('role', 'group'), pairs))  1.94 us
  transfers between devices with their start and end apart: 10, of which 6 were waited for; matrix products, arithmetic and copies ran while one was open for 0% of the time, Pallas kernels for 17%

profile of v10, /device:TPU:0, one launch (start us, length us, event | category | flops | bytes accessed | tf_op | source)
XLA Modules:
  0.0 31.3 jit_solution(12438664780368289680)
XLA Ops:
  0.0 0.9 %fusion.qa = bf16[8,2176]{1,0:T(8,128)(2,1)S(1)} fusion(s32[1,8]{1,0:T(1,128)} %lengths_hbm.1, s32[8,8]{1,0:T(8,128)} %bitcast.12, bf16[8,2048]{1,0:T(8,128)(2,1)} %bitcast.11), kind=kLoop, calls=%fused_computation.1 | loop fusion | flops 156672 | bytes 67872 | tf_op jit(solution)/shard_map/add | solution.py:306
  0.9 0.5 %collective-permute-start.2 = (bf16[8,2176]{1,0:T(8,128)(2,1)S(1)}, bf16[8,2176]{1,0:T(8,128)(2,1)S(1)}, u32[]{:S(2)}, u32[]{:S(2)}) collective-permute-start(bf16[8,2176]{1,0:T(8,128)(2,1)S(1)} %fusion.qa), channel_id=1, source_target_pairs={{16,4},{0,16},{20,8},{4,20},{24,12},{8,24},{28,0},{12,28},{17,5},{... | collective-permute-start | bytes 104456 | tf_op jit(solution)/shard_map/ppermute | solution.py:310
  1.3 2.7 %collective-permute-start.1 = (bf16[8,2176]{1,0:T(8,128)(2,1)S(1)}, bf16[8,2176]{1,0:T(8,128)(2,1)S(1)}, u32[]{:S(2)}, u32[]{:S(2)}) collective-permute-start(bf16[8,2176]{1,0:T(8,128)(2,1)S(1)} %fusion.qa), channel_id=1, source_target_pairs={{16,8},{0,16},{20,12},{4,20},{24,0},{8,24},{28,4},{12,28},{17,9},{... | collective-permute-start | bytes 104456 | tf_op jit(solution)/shard_map/ppermute | solution.py:310
  4.0 1.1 %collective-permute-start = (bf16[8,2176]{1,0:T(8,128)(2,1)S(1)}, bf16[8,2176]{1,0:T(8,128)(2,1)S(1)}, u32[]{:S(2)}, u32[]{:S(2)}) collective-permute-start(bf16[8,2176]{1,0:T(8,128)(2,1)S(1)} %fusion.qa), channel_id=1, source_target_pairs={{16,12},{0,16},{20,0},{4,20},{24,4},{8,24},{28,8},{12,28},{17,13},... | collective-permute-start | bytes 104456 | tf_op jit(solution)/shard_map/ppermute | solution.py:310
  5.1 3.7 %resident.1 = (f32[144,128]{1,0:T(8,128)S(1)}, bf16[144,128]{1,0:T(8,128)(2,1)S(1)}, bf16[24,128,512]{2,1,0:T(8,128)(2,1)S(1)}, f32[24,128]{1,0:T(8,128)S(1)}) custom-call(bf16[8,2176]{1,0:T(8,128)(2,1)S(1)} %fusion.qa, s32[3,4,12]{2,1,0:T(4,128)} %bitcast.14, s32[4,6]{1,0:T(4,128)} %wanted_hbm.1, s32[8,8]{1,0:T(8,128)} %bitcast.13, s32[1,8]{1,0:T(1,128)} %lengths_hbm.1, ...), custom_call_target="tpu_custom_call" | custom-call | tf_op jit(solution)/shard_map/resident/pallas_call | solution.py:322
  8.9 0.0 slice-start
  8.9 0.0 copy-start
  8.9 1.7 %owned.1 = (bf16[144,128]{1,0:T(8,128)(2,1)S(1)}, bf16[144,128]{1,0:T(8,128)(2,1)S(1)}, bf16[144,128]{1,0:T(8,128)(2,1)S(1)}) custom-call(bf16[24,128,512]{2,1,0:T(8,128)(2,1)S(1)} %get-tuple-element.19.chosen, f32[24,128]{1,0:T(8,128)S(1)} %get-tuple-element.20.entries, bf16[8,2176]{1,0:T(8,128)(2,1)S(1)} %collective-permute-done.refs_0_, ...), custom_call_target="tpu_custom_call" | custom-call | flops 40000000000 | bytes 8388608 | tf_op jit(solution)/shard_map/owned/pallas_call | solution.py:346
  10.6 1.2 %collective-permute-start.3 = (bf16[144,128]{1,0:T(8,128)(2,1)S(1)}, bf16[144,128]{1,0:T(8,128)(2,1)S(1)}, u32[]{:S(2)}, u32[]{:S(2)}) collective-permute-start(bf16[144,128]{1,0:T(8,128)(2,1)S(1)} %get-tuple-element.25), channel_id=1, source_target_pairs={{0,16},{16,0},{1,17},{17,1},{2,18},{18,2},{3,19},{19,3},{4,20},{20... | collective-permute-start | bytes 110600 | tf_op jit(solution)/shard_map/ppermute | solution.py:365
  11.8 2.5 %collective-permute-start.4 = (bf16[144,128]{1,0:T(8,128)(2,1)S(1)}, bf16[144,128]{1,0:T(8,128)(2,1)S(1)}, u32[]{:S(2)}, u32[]{:S(2)}) collective-permute-start(bf16[144,128]{1,0:T(8,128)(2,1)S(1)} %get-tuple-element.26), channel_id=1, source_target_pairs={{0,28},{16,0},{4,16},{20,4},{8,20},{24,8},{12,24},{28,12},{1,29},{... | collective-permute-start | bytes 110600 | tf_op jit(solution)/shard_map/ppermute | solution.py:368
  14.3 0.4 %fresh.1.refs_1_ = f32[144,128]{1,0:T(8,128)S(1)} custom-call(bf16[8,2176]{1,0:T(8,128)(2,1)S(1)} %fusion.qa, bf16[8,512]{1,0:T(8,128)(2,1)S(1)} %bitcast.9), custom_call_target="tpu_custom_call" | custom-call | flops 1000000000 | bytes 1048576 | tf_op jit(solution)/shard_map/fresh/pallas_call | solution.py:356
  14.6 1.2 %collective-permute-done.4.refs_3_ = bf16[144,128]{1,0:T(8,128)(2,1)S(1)} collective-permute-done((bf16[144,128]{1,0:T(8,128)(2,1)S(1)}, bf16[144,128]{1,0:T(8,128)(2,1)S(1)}, u32[]{:S(2)}, u32[]{:S(2)}) %collective-permute-start.4) | collective-permute-done | bytes 36896 | tf_op jit(solution)/shard_map/ppermute | solution.py:368
  15.9 0.3 %collective-permute-done.5.refs_4_ = bf16[144,128]{1,0:T(8,128)(2,1)S(1)} collective-permute-done((bf16[144,128]{1,0:T(8,128)(2,1)S(1)}, bf16[144,128]{1,0:T(8,128)(2,1)S(1)}, u32[]{:S(2)}, u32[]{:S(2)}) %collective-permute-start.5) | collective-permute-done | bytes 36896 | tf_op jit(solution)/shard_map/ppermute | solution.py:368
  16.2 0.3 %collective-permute-done.6.refs_5_ = bf16[144,128]{1,0:T(8,128)(2,1)S(1)} collective-permute-done((bf16[144,128]{1,0:T(8,128)(2,1)S(1)}, bf16[144,128]{1,0:T(8,128)(2,1)S(1)}, u32[]{:S(2)}, u32[]{:S(2)}) %collective-permute-start.6) | collective-permute-done | bytes 36896 | tf_op jit(solution)/shard_map/ppermute | solution.py:368
  16.6 0.3 %merge.1.attended = bf16[8,2048]{1,0:T(8,128)(2,1)S(1)} custom-call(f32[144,128]{1,0:T(8,128)S(1)} %get-tuple-element.17.refs_0_, f32[144,128]{1,0:T(8,128)S(1)} %fresh.1.refs_1_, bf16[144,128]{1,0:T(8,128)(2,1)S(1)} %collective-permute-done.3.refs_2_, bf16[144,128]{1,0:T(8,128)(2,1)S(1)} %collective-permute-done.4.refs_3_, ...), custom_call_target="tpu_custom_call" | custom-call | tf_op jit(solution)/shard_map/merge/pallas_call | solution.py:369
  16.9 3.4 %collective-permute-start.7 = (bf16[8,2048]{1,0:T(8,128)(2,1)S(1)}, bf16[8,2048]{1,0:T(8,128)(2,1)S(1)}, u32[]{:S(2)}, u32[]{:S(2)}) collective-permute-start(bf16[8,2048]{1,0:T(8,128)(2,1)S(1)} %merge.1.attended), channel_id=1, source_target_pairs={{0,16},{16,0},{1,17},{17,1},{2,18},{18,2},{3,19},{19,3},{4,20},{20... | collective-permute-start | bytes 98312 | tf_op jit(solution)/shard_map/ppermute | solution.py:377
  20.4 0.9 %collective-permute-done.7.partner = bf16[8,2048]{1,0:T(8,128)(2,1)S(1)} collective-permute-done((bf16[8,2048]{1,0:T(8,128)(2,1)S(1)}, bf16[8,2048]{1,0:T(8,128)(2,1)S(1)}, u32[]{:S(2)}, u32[]{:S(2)}) %collective-permute-start.7) | collective-permute-done | bytes 32800 | tf_op jit(solution)/shard_map/ppermute | solution.py:377
  21.2 1.2 %project_sent.1 = f32[8,2048]{1,0:T(8,128)S(1)} custom-call(bf16[8,2048]{1,0:T(8,128)(2,1)S(1)} %merge.1.attended, bf16[8,2048]{1,0:T(8,128)(2,1)S(1)} %collective-permute-done.7.partner, bf16[2048,4096]{1,0:T(8,128)(2,1)S(1)} %bitcast.8), custom_call_target="tpu_custom_call" | custom-call | flops 134217728 | bytes 8388608 | tf_op jit(solution)/shard_map/project_sent/pallas_call | solution.py:381
  22.4 1.5 %collective-permute-start.8 = (f32[8,2048]{1,0:T(8,128)S(1)}, f32[8,2048]{1,0:T(8,128)S(1)}, u32[]{:S(2)}, u32[]{:S(2)}) collective-permute-start(f32[8,2048]{1,0:T(8,128)S(1)} %project_sent.1), channel_id=1, source_target_pairs={{0,2},{1,3},{2,0},{3,1},{4,6},{5,7},{6,4},{7,5},{8,10},{9,11},{10,... | collective-permute-start | bytes 196616 | tf_op jit(solution)/shard_map/ppermute | solution.py:396
  24.0 1.2 %project_kept.1 = f32[8,2048]{1,0:T(8,128)S(1)} custom-call(bf16[8,2048]{1,0:T(8,128)(2,1)S(1)} %merge.1.attended, bf16[8,2048]{1,0:T(8,128)(2,1)S(1)} %collective-permute-done.7.partner, bf16[2048,4096]{1,0:T(8,128)(2,1)S(1)} %bitcast.8), custom_call_target="tpu_custom_call" | custom-call | flops 134217728 | bytes 8388608 | tf_op jit(solution)/shard_map/project_kept/pallas_call | solution.py:381
  25.1 1.6 %collective-permute-done.8 = f32[8,2048]{1,0:T(8,128)S(1)} collective-permute-done((f32[8,2048]{1,0:T(8,128)S(1)}, f32[8,2048]{1,0:T(8,128)S(1)}, u32[]{:S(2)}, u32[]{:S(2)}) %collective-permute-start.8) | collective-permute-done | bytes 65568 | tf_op jit(solution)/shard_map/ppermute | solution.py:396
  26.8 1.5 %collective-permute-start.9 = (f32[8,1024]{1,0:T(8,128)S(1)}, f32[8,1024]{1,0:T(8,128)S(1)}, u32[]{:S(2)}, u32[]{:S(2)}) collective-permute-start(f32[8,1024]{1,0:T(8,128)S(1)} %slice_add_fusion), channel_id=1, source_target_pairs={{0,1},{1,0},{2,3},{3,2},{4,5},{5,4},{6,7},{7,6},{8,9},{9,8},{10,11... | collective-permute-start | bytes 98312 | tf_op jit(solution)/shard_map/ppermute | solution.py:396
  28.3 2.4 %collective-permute-done.9 = f32[8,1024]{1,0:T(8,128)S(1)} collective-permute-done((f32[8,1024]{1,0:T(8,128)S(1)}, f32[8,1024]{1,0:T(8,128)S(1)}, u32[]{:S(2)}, u32[]{:S(2)}) %collective-permute-start.9) | collective-permute-done | bytes 32800 | tf_op jit(solution)/shard_map/ppermute | solution.py:396
  30.7 0.6 %fusion.3 = bf16[1,8,1024]{2,1,0:T(8,128)(2,1)} fusion(f32[8,1024]{1,0:T(8,128)S(1)} %collective-permute-done.9, f32[8,2048]{1,0:T(8,128)S(1)} %collective-permute-done.8, f32[8,2048]{1,0:T(8,128)S(1)} %project_kept.1), kind=kLoop, calls=%fused_computation.6 | loop fusion | flops 24576 | bytes 114688 | tf_op jit(solution)/shard_map/broadcast_in_dim | solution.py:398
  (16 shorter events, 0.0 us)
Async XLA Ops:
  0.9 8.0 %collective-permute-start.2 = (bf16[8,2176]{1,0:T(8,128)(2,1)S(1)}, bf16[8,2176]{1,0:T(8,128)(2,1)S(1)}, u32[]{:S(2)}, u32[]{:S(2)}) collective-permute-start(bf16[8,2176]{1,0:T(8,128)(2,1)S(1)} %fusion.qa), channel_id=1, source_target_pairs={{16,4},{0,16},{20,8},{4,20},{24,12},{8,24},{28,0},{12,28},{17,5},{... | collective-permute-start | bytes 104456 | tf_op jit(solution)/shard_map/ppermute | solution.py:310
  1.3 7.5 %collective-permute-start.1 = (bf16[8,2176]{1,0:T(8,128)(2,1)S(1)}, bf16[8,2176]{1,0:T(8,128)(2,1)S(1)}, u32[]{:S(2)}, u32[]{:S(2)}) collective-permute-start(bf16[8,2176]{1,0:T(8,128)(2,1)S(1)} %fusion.qa), channel_id=1, source_target_pairs={{16,8},{0,16},{20,12},{4,20},{24,0},{8,24},{28,4},{12,28},{17,9},{... | collective-permute-start | bytes 104456 | tf_op jit(solution)/shard_map/ppermute | solution.py:310
  4.0 4.8 %collective-permute-start = (bf16[8,2176]{1,0:T(8,128)(2,1)S(1)}, bf16[8,2176]{1,0:T(8,128)(2,1)S(1)}, u32[]{:S(2)}, u32[]{:S(2)}) collective-permute-start(bf16[8,2176]{1,0:T(8,128)(2,1)S(1)} %fusion.qa), channel_id=1, source_target_pairs={{16,12},{0,16},{20,0},{4,20},{24,4},{8,24},{28,8},{12,28},{17,13},... | collective-permute-start | bytes 104456 | tf_op jit(solution)/shard_map/ppermute | solution.py:310
  8.9 12.3 %slice-start = ((s8[16777216]{0:T(1024)(128)(4,1)}), s8[4194304]{0:T(1024)(128)(4,1)S(1)}, s32[]{:S(2)}) async-start(s8[16777216]{0:T(1024)(128)(4,1)} %bitcast.7), calls=%async_computation | async-start | bytes 8388608
  8.9 5.4 %copy-start = (bf16[1,8,512]{2,1,0:T(8,128)(2,1)S(1)}, bf16[1,8,512]{2,1,0:T(8,128)(2,1)}, u32[]{:S(2)}) copy-start(bf16[1,8,512]{2,1,0:T(8,128)(2,1)} %param.14) | copy-start | bytes 24580
  8.9 12.3 %slice-start.1 = ((s8[16777216]{0:T(1024)(128)(4,1)}), s8[4194304]{0:T(1024)(128)(4,1)S(1)}, s32[]{:S(2)}) async-start(s8[16777216]{0:T(1024)(128)(4,1)} %bitcast.7), calls=%async_computation.1 | async-start | bytes 8388608
  8.9 12.3 %slice-start.2 = ((s8[16777216]{0:T(1024)(128)(4,1)}), s8[4194304]{0:T(1024)(128)(4,1)S(1)}, s32[]{:S(2)}) async-start(s8[16777216]{0:T(1024)(128)(4,1)} %bitcast.7), calls=%async_computation.2 | async-start | bytes 8388608
  8.9 12.3 %slice-start.3 = ((s8[16777216]{0:T(1024)(128)(4,1)}), s8[4194304]{0:T(1024)(128)(4,1)S(1)}, s32[]{:S(2)}) async-start(s8[16777216]{0:T(1024)(128)(4,1)} %bitcast.7), calls=%async_computation.3 | async-start | bytes 8388608
  10.6 4.0 %collective-permute-start.3 = (bf16[144,128]{1,0:T(8,128)(2,1)S(1)}, bf16[144,128]{1,0:T(8,128)(2,1)S(1)}, u32[]{:S(2)}, u32[]{:S(2)}) collective-permute-start(bf16[144,128]{1,0:T(8,128)(2,1)S(1)} %get-tuple-element.25), channel_id=1, source_target_pairs={{0,16},{16,0},{1,17},{17,1},{2,18},{18,2},{3,19},{19,3},{4,20},{20... | collective-permute-start | bytes 110600 | tf_op jit(solution)/shard_map/ppermute | solution.py:365
  11.8 4.1 %collective-permute-start.4 = (bf16[144,128]{1,0:T(8,128)(2,1)S(1)}, bf16[144,128]{1,0:T(8,128)(2,1)S(1)}, u32[]{:S(2)}, u32[]{:S(2)}) collective-permute-start(bf16[144,128]{1,0:T(8,128)(2,1)S(1)} %get-tuple-element.26), channel_id=1, source_target_pairs={{0,28},{16,0},{4,16},{20,4},{8,20},{24,8},{12,24},{28,12},{1,29},{... | collective-permute-start | bytes 110600 | tf_op jit(solution)/shard_map/ppermute | solution.py:368
  14.3 2.0 %collective-permute-start.5 = (bf16[144,128]{1,0:T(8,128)(2,1)S(1)}, bf16[144,128]{1,0:T(8,128)(2,1)S(1)}, u32[]{:S(2)}, u32[]{:S(2)}) collective-permute-start(bf16[144,128]{1,0:T(8,128)(2,1)S(1)} %get-tuple-element.27), channel_id=1, source_target_pairs={{0,24},{16,0},{4,28},{20,4},{8,16},{24,8},{12,20},{28,12},{1,25},{... | collective-permute-start | bytes 110600 | tf_op jit(solution)/shard_map/ppermute | solution.py:368
  14.3 2.3 %collective-permute-start.6 = (bf16[144,128]{1,0:T(8,128)(2,1)S(1)}, bf16[144,128]{1,0:T(8,128)(2,1)S(1)}, u32[]{:S(2)}, u32[]{:S(2)}) collective-permute-start(bf16[144,128]{1,0:T(8,128)(2,1)S(1)} %get-tuple-element.28), channel_id=1, source_target_pairs={{0,20},{16,0},{4,24},{20,4},{8,28},{24,8},{12,16},{28,12},{1,21},{... | collective-permute-start | bytes 110600 | tf_op jit(solution)/shard_map/ppermute | solution.py:368
  16.9 4.3 %collective-permute-start.7 = (bf16[8,2048]{1,0:T(8,128)(2,1)S(1)}, bf16[8,2048]{1,0:T(8,128)(2,1)S(1)}, u32[]{:S(2)}, u32[]{:S(2)}) collective-permute-start(bf16[8,2048]{1,0:T(8,128)(2,1)S(1)} %merge.1.attended), channel_id=1, source_target_pairs={{0,16},{16,0},{1,17},{17,1},{2,18},{18,2},{3,19},{19,3},{4,20},{20... | collective-permute-start | bytes 98312 | tf_op jit(solution)/shard_map/ppermute | solution.py:377
  22.4 4.4 %collective-permute-start.8 = (f32[8,2048]{1,0:T(8,128)S(1)}, f32[8,2048]{1,0:T(8,128)S(1)}, u32[]{:S(2)}, u32[]{:S(2)}) collective-permute-start(f32[8,2048]{1,0:T(8,128)S(1)} %project_sent.1), channel_id=1, source_target_pairs={{0,2},{1,3},{2,0},{3,1},{4,6},{5,7},{6,4},{7,5},{8,10},{9,11},{10,... | collective-permute-start | bytes 196616 | tf_op jit(solution)/shard_map/ppermute | solution.py:396
  26.8 3.9 %collective-permute-start.9 = (f32[8,1024]{1,0:T(8,128)S(1)}, f32[8,1024]{1,0:T(8,128)S(1)}, u32[]{:S(2)}, u32[]{:S(2)}) collective-permute-start(f32[8,1024]{1,0:T(8,128)S(1)} %slice_add_fusion), channel_id=1, source_target_pairs={{0,1},{1,0},{2,3},{3,2},{4,5},{5,4},{6,7},{7,6},{8,9},{9,8},{10,11... | collective-permute-start | bytes 98312 | tf_op jit(solution)/shard_map/ppermute | solution.py:396
